TPU v7x, 32 devices: a whole 2x2x4 slice. The times are simulated.
32 devices in a mesh: pairs: 8 (over z, y), pw: 4 (over x, core).
Axes of the slice: x: 2, y: 2, z: 4, core: 2. Of those that a mesh axis runs over, the one named last changes fastest.
Arguments:
- orbitals: bfloat16 [16, 32, 16384], P(None, 'pairs', 'pw'), may hold values from -6 to 6
- vectors: bfloat16 [16, 64, 256], P(None, 'pairs'), may hold values from -6 to 6
- screened: bfloat16 [16, 2048, 2048], P('pairs', 'pw'), may hold values from -0.00018310547 to 0.00018310547
- pair_list: int32 [16, 2], replicated, may hold values from 0 to 15
- band_order: int32 [32], replicated, may hold values from 0 to 31, each once
Outputs:
- applied: float32 [16, 64, 256], P('pairs', 'pw')
All inputs are finite; a program needn't handle non-finite values.
Results may differ from a plain program's by a relative error of at most 0.013.
Values may be sent and summed in bfloat16 or wider, within the bound.
No kernel may reach another device: no remote copies, remote signals or barrier semaphores. Data moves between devices by JAX's collectives and lax.ppermute only.
A program may use at most 128 MiB of HBM per device.

v0:
```python
import math

import jax
import jax.numpy as jnp
from jax import lax
from jax.sharding import PartitionSpec as P

NV = 16
NC = 16
NG = 16384


def vector_products(first_rho, screened_rho, first_vec, second_vec):
    left_proj = jnp.einsum(
        "jvt,jth->jvh", second_vec, screened_rho, preferred_element_type=jnp.float32
    ).astype(jnp.bfloat16)
    right_proj = jnp.einsum(
        "jvt,jth->jvh", first_vec, first_rho, preferred_element_type=jnp.float32
    ).astype(jnp.bfloat16)
    forward = jnp.einsum("jvh,jah->jva", left_proj, first_rho, preferred_element_type=jnp.float32)
    backward = jnp.einsum(
        "jvh,jah->jva", right_proj, screened_rho, preferred_element_type=jnp.float32
    )
    stacked = jnp.stack([forward, backward], axis=1)
    return stacked.reshape((-1,) + forward.shape[1:])


def local(orbitals, vectors, screened, pair_list, band_order):
    groups = lax.axis_size("pairs")
    my_group = lax.axis_index("pairs")
    requests = pair_list.reshape(groups, -1)
    orb_send = jnp.take(orbitals, requests, axis=0)
    vec_send = jnp.take(vectors, requests, axis=0)
    orb_got, vec_got = (
        lax.all_to_all(orb_send, "pairs", split_axis=0, concat_axis=2, tiled=True),
        lax.all_to_all(vec_send, "pairs", split_axis=0, concat_axis=2, tiled=True),
    )
    orb_got = orb_got[0]
    vec_got = vec_got[0]
    band_count = orb_got.shape[1]
    picker = (band_order[:, None] == jnp.arange(band_count, dtype=jnp.int32)[None, :]).astype(
        jnp.bfloat16
    )
    band_psi = jnp.einsum(
        "sb,jsr->jbr", picker, orb_got, preferred_element_type=jnp.float32
    ).astype(jnp.bfloat16)
    wave_local = screened.shape[1]
    g_offset = lax.axis_index("pw") * wave_local
    piece = lax.all_gather(band_psi, "pw", axis=2, tiled=True)
    point_count = piece.shape[2]
    grid_rows = jnp.arange(point_count, dtype=jnp.int32)
    wave_cols = g_offset + jnp.arange(wave_local, dtype=jnp.int32)
    phase_index = (2 * grid_rows + 1)[:, None] * wave_cols[None, :] % (4 * NG)
    cos_table = (
        jnp.cos(phase_index.astype(jnp.float32) * (math.pi / (2 * NG))) * math.sqrt(2.0 / NG)
    ).astype(jnp.bfloat16)
    pair_prod = (
        piece[:, :NV][:, :, None, :].astype(jnp.float32)
        * piece[:, NV:][:, None, :, :].astype(jnp.float32)
    ).astype(jnp.bfloat16)
    pair_prod = pair_prod.reshape(piece.shape[0] * NV * NC, point_count)
    result = jnp.dot(pair_prod, cos_table, preferred_element_type=jnp.float32)
    rho_local = result.reshape(piece.shape[0], NV * NC, wave_local).astype(jnp.bfloat16)
    first_rho = rho_local[0::2]
    second_rho = rho_local[1::2]
    screened_rho = jnp.einsum(
        "jtn,jhn->jth",
        lax.all_gather(second_rho, "pw", axis=2, tiled=True),
        screened,
        preferred_element_type=jnp.float32,
    ).astype(jnp.bfloat16)
    full_terms = vector_products(first_rho, screened_rho, vec_got[0::2], vec_got[1::2])
    vector_terms = lax.psum_scatter(
        full_terms.astype(jnp.bfloat16), "pw", scatter_dimension=1, tiled=True
    ).astype(jnp.float32)
    pairs_here = pair_list.shape[0] // groups
    my_requests = lax.dynamic_slice_in_dim(pair_list, my_group * pairs_here, pairs_here, 0).reshape(
        -1
    )
    k_count = orbitals.shape[0]
    one_hot = (my_requests[:, None] == jnp.arange(k_count, dtype=jnp.int32)[None, :]).astype(
        jnp.float32
    )
    placed = jnp.sum(one_hot[:, :, None, None] * vector_terms[:, None, :, :], axis=0)
    return lax.psum_scatter(
        placed.astype(jnp.bfloat16), "pairs", scatter_dimension=0, tiled=True
    ).astype(jnp.float32)


def solution(mesh):
    in_specs = (P(None, "pairs", "pw"), P(None, "pairs", None), P("pairs", "pw", None), P(), P())
    out_specs = P("pairs", "pw", None)
    return jax.shard_map(local, mesh=mesh, in_specs=in_specs, out_specs=out_specs, check_vma=False)
```

profile of v0, /device:TPU:0, one launch (start us, length us, event | category | flops | bytes accessed | tf_op | source)
XLA Modules:
  0.0 374.7 jit_solution(18368561734910457694)
XLA Ops:
  6.5 0.0 copy-start
  6.5 0.0 all-gather.3.cloned.1.call-start
  6.5 0.8 copy.32
  7.4 0.1 reshape.93
  7.4 0.1 reshape.92
  7.5 0.1 reshape.96
  7.6 0.0 copy-done
  7.6 1.4 gather_fusion.1
  9.1 0.6 broadcast_select_fusion
  9.6 32.8 %all_to_all.30 = bf16[8,4,4,4096]{3,2,1,0:T(4,128)(2,1)S(1)} all-to-all(bf16[8,4,4,4096]{3,2,1,0:T(4,128)(2,1)S(1)} %broadcast_select_fusion), channel_id=1, replica_groups=mesh['pairs'=8,'pw'=4] {'pairs'}, dimensions={0} | all-to-all | bytes 2097152 | tf_op jit(solution)/shard_map/all_to_all | solution.py:35
  42.5 0.4 copy.35
  42.9 0.3 squeeze.7
  43.2 2.1 fusion.16
  45.3 0.0 all-gather.3.cloned.1.call-update
  45.3 0.0 all-gather.5.cloned.1.call-start
  45.4 33.6 %all-gather.3.cloned.1.call-done = bf16[4,32,16384]{2,1,0:T(8,128)(2,1)} async-done(((bf16[4,32,4096]{2,1,0:T(8,128)(2,1)}), bf16[4,32,16384]{2,1,0:T(8,128)(2,1)}) %all-gather.3.cloned.1.call-update) | async-done | bytes 4194320 | tf_op jit(solution)/shard_map/all_gather | solution.py:49
  78.9 4.8 %slice_convert_fusion.1 = (f32[4,16,16384]{2,1,0:T(8,128)S(1)}, f32[4,16,16384]{2,1,0:T(8,128)}) fusion(bf16[4,32,16384]{2,1,0:T(8,128)(2,1)} %all-gather.3.cloned.1.call-done), kind=kLoop, calls=%fused_computation.26 | loop fusion | flops 2097152 | bytes 12582912 | tf_op jit(solution)/shard_map/convert_element_type | solution.py:58
  83.8 12.5 %multiply_convert_fusion = bf16[4,16,16,16384]{3,2,1,0:T(8,128)(2,1)} fusion(f32[4,16,16384]{2,1,0:T(8,128)} %get-tuple-element.6, f32[4,16,16384]{2,1,0:T(8,128)S(1)} %get-tuple-element.5), kind=kLoop, calls=%fused_computation.2 | loop fusion | flops 33554432 | bytes 41943040 | tf_op jit(solution)/shard_map/convert_element_type | solution.py:60
  96.2 0.0 copy-start.1
  96.2 0.0 copy-start.2
  96.3 157.2 %fusion.17 = bf16[4,256,512]{2,1,0:T(8,128)(2,1)S(1)} fusion(bf16[4,256,16384]{2,1,0:T(8,128)(2,1)} %bitcast.39, s32[512]{0:T(512)S(1)} %iota_add_fusion, s32[16384]{0:T(1024)S(1)} %multiply_add_fusion), kind=kOutput, calls=%fused_computation.27 | convolution fusion | flops 17314611200 | bytes 34670592 | tf_op jit(solution)/shard_map/dot_general | solution.py:62
  253.4 0.8 slice.21
  254.3 0.0 all-gather.5.cloned.1.call-update
  254.3 0.0 copy-done.1
  254.3 0.6 gather_fusion
  254.9 0.8 broadcast_select_fusion.1
  255.7 5.5 %all-to-all-start = ((bf16[8,4,8,256]{3,2,1,0:T(8,128)(2,1)}), bf16[8,4,8,256]{3,2,1,0:T(8,128)(2,1)S(1)}, u32[]{:S(2)}, u32[]{:S(2)}) async-start(bf16[8,4,8,256]{3,2,1,0:T(8,128)(2,1)} %broadcast_select_fusion.1), calls=%async_computation | async-start | bytes 262144 | tf_op jit(solution)/shard_map/all_to_all | solution.py:36
  261.2 0.0 reduce-scatter.3.cloned.1.call-start
  261.2 7.3 %all-to-all-done = bf16[8,4,8,256]{3,2,1,0:T(8,128)(2,1)S(1)} async-done(((bf16[8,4,8,256]{3,2,1,0:T(8,128)(2,1)}), bf16[8,4,8,256]{3,2,1,0:T(8,128)(2,1)S(1)}, u32[]{:S(2)}, u32[]{:S(2)}) %all-to-all-start) | async-done | bytes 131104 | tf_op jit(solution)/shard_map/all_to_all | solution.py:36
  268.6 8.5 %all-gather.5.cloned.1.call-done = bf16[2,256,2048]{2,1,0:T(8,128)(2,1)} async-done(((bf16[2,256,512]{2,1,0:T(8,128)(2,1)}), bf16[2,256,2048]{2,1,0:T(8,128)(2,1)}) %all-gather.5.cloned.1.call-update) | async-done | bytes 2097168 | tf_op jit(solution)/shard_map/all_gather | solution.py:68
  277.1 4.1 %convolution_convert_fusion.1 = bf16[2,256,512]{2,1,0:T(8,128)(2,1)S(1)} fusion(bf16[2,256,2048]{2,1,0:T(8,128)(2,1)} %all-gather.5.cloned.1.call-done, bf16[2,512,2048]{2,1,0:T(8,128)(2,1)} %param.7), kind=kOutput, calls=%fused_computation.28 | convolution fusion | flops 1074003968 | bytes 6815744 | tf_op jit(solution)/shard_map/jtn,jhn->jth/dot_general | solution.py:66
  281.2 0.4 fusion.24
  281.6 0.4 fusion.25
  282.0 0.7 copy.36
  282.6 0.0 reduce-scatter.3.cloned.1.call-update
  282.7 0.0 reduce-scatter.5.cloned.1.call-start
  282.7 0.0 copy-done.2
  282.7 0.1 constant_dynamic-slice_fusion
  282.8 0.1 copy.31
  282.9 0.1 eq.34
  283.0 0.1 fusion.36
  283.1 19.4 %reduce-scatter.3.cloned.1.call-done = bf16[4,16,256]{2,1,0:T(8,128)(2,1)} async-done(((bf16[4,64,256]{2,1,0:T(8,128)(2,1)}), bf16[4,16,256]{2,1,0:T(8,128)(2,1)}) %reduce-scatter.3.cloned.1.call-update) | async-done | bytes 32784 | tf_op jit(solution)/shard_map/reduce_scatter | solution.py:73
  302.4 0.8 convert_element_type.75
  303.2 0.8 multiply_reduce_fusion
  304.0 0.0 reduce-scatter.5.cloned.1.call-update
  304.0 62.8 %reduce-scatter.5.cloned.1.call-done = bf16[2,16,256]{2,1,0:T(8,128)(2,1)} async-done(((bf16[16,16,256]{2,1,0:T(8,128)(2,1)}), bf16[2,16,256]{2,1,0:T(8,128)(2,1)}) %reduce-scatter.5.cloned.1.call-update) | async-done | bytes 16400 | tf_op jit(solution)/shard_map/reduce_scatter | solution.py:85
  366.8 1.3 convert_element_type.77
  (7 shorter events, 0.1 us)
Async XLA Ops:
  6.5 1.1 copy-start
  6.5 72.4 %all-gather.3.cloned.1.call-start = ((), (), s32[]{:S(2)}) async-start(), calls=%async_computation.4 | async-start | bytes 5242880 | tf_op jit(solution)/shard_map/all_gather | solution.py:49
  45.3 231.8 %all-gather.5.cloned.1.call-start = ((), (), s32[]{:S(2)}) async-start(), calls=%async_computation.5 | async-start | bytes 2621440 | tf_op jit(solution)/shard_map/all_gather | solution.py:68
  96.2 158.1 %copy-start.1 = (bf16[16,8,256]{2,1,0:T(8,128)(2,1)S(1)}, bf16[16,8,256]{2,1,0:T(8,128)(2,1)}, u32[]{:S(2)}) copy-start(bf16[16,8,256]{2,1,0:T(8,128)(2,1)} %param.6) | copy-start | bytes 196612
  96.2 186.5 %copy-start.2 = (s32[16,2]{0,1:T(2,128)S(1)}, s32[16,2]{0,1:T(2,128)}, u32[]{:S(2)}) copy-start(s32[16,2]{0,1:T(2,128)} %param.8) | copy-start | bytes 388
  255.7 12.9 %all-to-all-start = ((bf16[8,4,8,256]{3,2,1,0:T(8,128)(2,1)}), bf16[8,4,8,256]{3,2,1,0:T(8,128)(2,1)S(1)}, u32[]{:S(2)}, u32[]{:S(2)}) async-start(bf16[8,4,8,256]{3,2,1,0:T(8,128)(2,1)} %broadcast_select_fusion.1), calls=%async_computation | async-start | bytes 262144 | tf_op jit(solution)/shard_map/all_to_all | solution.py:36
  261.2 41.2 %reduce-scatter.3.cloned.1.call-start = ((), (), s32[]{:S(2)}) async-start(), calls=%async_computation.6 | async-start | bytes 163840 | tf_op jit(solution)/shard_map/reduce_scatter | solution.py:73
  282.7 84.2 %reduce-scatter.5.cloned.1.call-start = ((), (), s32[]{:S(2)}) async-start(), calls=%async_computation.7 | async-start | bytes 147456 | tf_op jit(solution)/shard_map/reduce_scatter | solution.py:85
Sparse Core Ops, SparseCore 0:
  45.4 33.4 all-gather.2
  254.4 22.5 all-gather.4
  282.8 19.5 reduce-scatter.2
  305.9 60.8 reduce-scatter.4
where the time goes:
time: 375 us
  matrix products  164 us (44%)
  waiting for transfers between devices  132 us (35%)
  blocking collectives  32.8 us (9%)
  other arithmetic  21.7 us (6%)
  between operations  13.3 us (4%)
  starting transfers between devices  5.64 us (2%)
  local copies, waits for them, and re-layouts  5.53 us (1%)
    dot_general x1, matrix products, local(): result = jnp.dot(pair_prod, cos_table, preferred_element_type=jnp.float32)  157 us
    reduce_scatter x1, waiting for transfers between devices, local(): lax.psum_scatter(placed.astype(jnp.bfloat16), 'pairs', scatter_dimension=...  62.8 us
    all_gather x1, waiting for transfers between devices, local(): piece = lax.all_gather(band_psi, 'pw', axis=2, tiled=True)  33.6 us
    all_to_all x1, blocking collectives, local(): lax.all_to_all(orb_send, 'pairs', split_axis=0, concat_axis=2, tiled=True)  32.8 us
    reduce_scatter x1, waiting for transfers between devices, local(): lax.psum_scatter(full_terms.astype(jnp.bfloat16), 'pw', scatter_dimension...  19.4 us
    convert_element_type x1, other arithmetic, local(): pair_prod = (piece[:, :NV][:, :, None, :].astype(jnp.float32) * piece[:,...  12.5 us
    all_gather x1, waiting for transfers between devices, local(): lax.all_gather(second_rho, 'pw', axis=2, tiled=True)  8.47 us
  transfers between devices with their start and end apart: 5, of which 5 were waited for; matrix products, arithmetic and copies ran while one was open for 0% of the time, Pallas kernels for 0%

commit v1 on v0

v1 whole, which is shorter than its diff:
```python
import functools
import math

import jax
import jax.numpy as jnp
import numpy as np
from jax import lax
from jax.experimental import pallas as pl
from jax.experimental.pallas import tpu as pltpu
from jax.sharding import PartitionSpec as P

NV = 16
NC = 16
FINE = 64
BF16 = jnp.bfloat16
F32 = jnp.float32


def phase_tables(points, waves, halves, columns):
    width = waves // columns
    sets = []
    for j in range(halves):
        own = np.concatenate(
            [np.arange(c * width, (c + 1) * width) for c in range(j, columns, halves)]
        )
        sets.append(np.concatenate([own[0::2], own[1::2]]))
    sets = np.stack(sets)[:, None, :].astype(np.int64)
    period = 4 * points
    scale = math.sqrt(2.0 / points)
    coarse = (2 * FINE * np.arange(points // FINE)[None, :, None] * sets) % period
    fine = ((2 * np.arange(FINE) + 1)[None, :, None] * sets) % period
    turn = math.pi / (2 * points)
    return (
        (np.cos(coarse * turn) * scale).astype(np.float32),
        (np.sin(coarse * turn) * scale).astype(np.float32),
        np.cos(fine * turn).astype(np.float32),
        np.sin(fine * turn).astype(np.float32),
    )


def one_hot_matrix(size, target):
    rows = lax.broadcasted_iota(jnp.int32, (size, size), 0)
    cols = lax.broadcasted_iota(jnp.int32, (size, size), 1)
    return jnp.where(target(rows) == cols, 1.0, 0.0).astype(BF16)


def interleave(size):
    half = size // 2
    return one_hot_matrix(size, lambda r: jnp.where(r < half, 2 * r, 2 * (r - half) + 1))


def dot(a, b):
    return jnp.dot(a, b, preferred_element_type=F32)


def dot_nt(a, b):
    return lax.dot_general(a, b, (((1,), (1,)), ((), ())), preferred_element_type=F32)


def transform_kernel(
    place, base, mirror, ca, sa, cb, sb, vec, rho, p_first, p_msg, sums, diffs, table, acc
):
    step = pl.program_id(0)
    block = base.shape[-1]
    waves = table.shape[1]
    half = waves // 2
    flip = one_hot_matrix(256, lambda r: 255 - r)

    @pl.when(step == 0)
    def _():
        acc[...] = jnp.zeros_like(acc)

    for a in range(block // FINE):
        table[a * FINE : (a + 1) * FINE, :] = (
            ca[0, a : a + 1, :] * cb[0] - sa[0, a : a + 1, :] * sb[0]
        ).astype(BF16)
    bands = base.shape[3]
    for slot in range(2):
        far = mirror[0, 0, slot]
        back = jnp.concatenate(
            [
                dot(far[:, block - 256 * (i + 1) : block - 256 * i], flip)
                for i in range(block // 256)
            ],
            axis=1,
        )
        near = base[0, 0, slot].astype(F32)
        for v in range(NV):
            here = near[v : v + 1] * near[NV:bands]
            there = back[v : v + 1] * back[NV:bands]
            row = slot * NV * NC + v * NC
            sums[row : row + NC, :] = (here + there).astype(BF16)
            diffs[row : row + NC, :] = (here - there).astype(BF16)
    acc[:, :half] += dot(sums[...], table[:, :half])
    acc[:, half:] += dot(diffs[...], table[:, half:])

    @pl.when(step == pl.num_programs(0) - 1)
    def _():
        order = interleave(256)
        x = place[1]
        width = p_first.shape[1]
        products = NV * NC
        for slot in range(2):
            done = acc[slot * products : (slot + 1) * products, :].astype(BF16)
            rho[slot] = done
            proj = dot(vec[slot], done).astype(BF16)
            natural = jnp.concatenate(
                [
                    dot(
                        jnp.concatenate(
                            [proj[:, 128 * i : 128 * (i + 1)], proj[:, half + 128 * i : half + 128 * (i + 1)]],
                            axis=1,
                        ),
                        order,
                    ).astype(BF16)
                    for i in range(waves // 256)
                ],
                axis=1,
            )
            if slot == 1:
                p_msg[:, width:] = natural
            else:
                first, second = natural[:, :width], natural[:, width:]
                p_first[...] = jnp.where(x == 0, first, second)
                p_msg[:, :width] = jnp.where(x == 0, second, first)


def screen_kernel(place, *refs, shifts):
    j, x = place[0], place[1]
    p_first, p_msg, p_far = refs[:3]
    near = refs[3 : 3 + shifts - 1]
    far = refs[2 + shifts : 1 + 2 * shifts]
    screened = refs[1 + 2 * shifts]
    left_own, left_msg, q_own = refs[2 + 2 * shifts : 5 + 2 * shifts]
    q_msgs = refs[5 + 2 * shifts :]
    width = p_first.shape[1]
    for rel in range(2):
        pair = x if rel == 0 else 1 - x
        first = p_first[...] if rel == 0 else p_far[:, :width]
        total = None
        for s in range(shifts):
            if s == 0:
                source = p_msg if rel == 0 else p_far
                offset = width
            else:
                source = near[s - 1] if rel == 0 else far[s - 1]
                offset = 0
            for c in range(2):
                start = pl.multiple_of((c * shifts + (j ^ s)) * width, width)
                block = screened[pair, :, pl.ds(start, width)]
                piece = source[:, offset + c * width : offset + (c + 1) * width]
                term = dot_nt(piece, block)
                total = term if total is None else total + term
                back = dot(first, block)
                if s == 0:
                    q_own[rel, :, c * width : (c + 1) * width] = back
                else:
                    q_msgs[s - 1][rel, :, c * width : (c + 1) * width] = back.astype(BF16)
        if rel == 0:
            left_own[...] = total.astype(BF16)
        else:
            left_msg[...] = total.astype(BF16)


def apply_kernel(place, left_own, left_far, q_mine, q_far, rho, own, *refs):
    j, x = place[0], place[1]
    msgs, scratch = refs[:-1], refs[-1]
    shifts = len(msgs) + 1
    waves = rho.shape[2]
    half = waves // 2
    order = interleave(256)
    mine, other = left_own[...], left_far[...]
    first = jnp.concatenate([jnp.where(x == 0, mine, other), jnp.where(x == 0, other, mine)], axis=1)
    second = (q_mine[...] + q_far[...].astype(F32)).astype(BF16)
    for slot, weight in enumerate((first, second)):
        parts = [
            dot_nt(weight[:, 256 * i : 256 * (i + 1)], order).astype(BF16)
            for i in range(waves // 256)
        ]
        sorted_weight = jnp.concatenate([p[:, :128] for p in parts] + [p[:, 128:] for p in parts], axis=1)
        scratch[slot] = dot_nt(sorted_weight, rho[slot]).reshape(scratch.shape[1:])
    for s in range(shifts):
        for c in range(2):
            for slot in range(2):
                value = scratch[slot, c * shifts + (j ^ s)]
                if s == 0:
                    own[slot, c] = value
                else:
                    msgs[s - 1][slot, c] = value.astype(BF16)


def local(orbitals, vectors, screened, pair_list, band_order):
    groups = lax.axis_size("pairs")
    columns = lax.axis_size("pw")
    pairs_here = screened.shape[0]
    halves = columns // pairs_here
    both = ("pairs", "pw")
    g = lax.axis_index("pairs")
    w = lax.axis_index("pw")
    x, j = w // halves, w % halves
    place = jnp.stack([j, x]).astype(jnp.int32)
    k_count, band_here, chunk = orbitals.shape
    points = chunk * columns
    waves = screened.shape[2]
    width = waves // columns
    own_waves = width * pairs_here
    transitions = vectors.shape[2]
    vec_count = vectors.shape[1] * groups
    vec_part = vectors.shape[1] // pairs_here
    bands = band_here * groups
    members = [
        [gg * columns + xx * halves + jj for gg in range(groups) for xx in range(pairs_here)]
        for jj in range(halves)
    ]

    def exchange(value):
        return lax.all_to_all(value, both, 0, 0, tiled=True, axis_index_groups=members)

    def shift(value, s):
        return lax.ppermute(value, "pw", [(i, i ^ s) for i in range(columns)])

    vec_mine = lax.dynamic_slice_in_dim(vectors, x * vec_part, vec_part, 1)
    stored = jnp.concatenate([orbitals, vec_mine], axis=2)
    sent = jnp.take(stored, pair_list.reshape(-1), axis=0, mode="clip")
    sent = sent.reshape(groups * pairs_here, 2, band_here, chunk + transitions)
    got = exchange(sent).reshape(groups, pairs_here, 2, band_here, chunk + transitions)
    vec = got[..., chunk:].transpose(2, 0, 1, 3, 4).reshape(2, vec_count, transitions)
    picker = (band_order[:, None] == jnp.arange(bands, dtype=jnp.int32)[None, :]).astype(BF16)
    psi = jnp.einsum(
        "gbn,gxlbr->xlnr",
        picker.reshape(groups, band_here, bands),
        got[..., :chunk],
        preferred_element_type=F32,
    ).astype(BF16)
    parts = [psi] + [shift(psi, s) for s in range(1, halves)]
    count = halves // 2
    base = jnp.stack([parts[s] for s in range(count)])
    mirror = jnp.stack([parts[s ^ (halves - 1)] for s in range(count)])

    block = min(1024, chunk)
    per_chunk = chunk // block
    steps = count * pairs_here * per_chunk
    rows = block // FINE
    tables = [jnp.asarray(t) for t in phase_tables(points, waves, halves, columns)]

    def parse(t):
        return t // (pairs_here * per_chunk), t // per_chunk % pairs_here, t % per_chunk

    def base_map(t, place):
        s, c, b = parse(t)
        return s, c, 0, 0, b

    def mirror_map(t, place):
        s, c, b = parse(t)
        return s, pairs_here - 1 - c, 0, 0, per_chunk - 1 - b

    def coarse_map(t, place):
        s, c, b = parse(t)
        return place[0], (c * halves + (place[0] ^ s)) * per_chunk + b, 0

    def fixed(*shape):
        return pl.BlockSpec(shape, lambda t, place: (0,) * len(shape))

    products = NV * NC
    rho, p_first, p_msg = pl.pallas_call(
        transform_kernel,
        grid_spec=pltpu.PrefetchScalarGridSpec(
            num_scalar_prefetch=1,
            grid=(steps,),
            in_specs=[
                pl.BlockSpec((1, 1, 2, bands, block), base_map),
                pl.BlockSpec((1, 1, 2, bands, block), mirror_map),
                pl.BlockSpec((1, rows, own_waves), coarse_map),
                pl.BlockSpec((1, rows, own_waves), coarse_map),
                pl.BlockSpec((1, FINE, own_waves), lambda t, place: (place[0], 0, 0)),
                pl.BlockSpec((1, FINE, own_waves), lambda t, place: (place[0], 0, 0)),
                fixed(2, vec_count, transitions),
            ],
            out_specs=[
                fixed(2, products, own_waves),
                fixed(vec_count, width),
                fixed(vec_count, width + own_waves),
            ],
            scratch_shapes=[
                pltpu.VMEM((2 * products, block), BF16),
                pltpu.VMEM((2 * products, block), BF16),
                pltpu.VMEM((block, own_waves), BF16),
                pltpu.VMEM((2 * products, own_waves), F32),
            ],
        ),
        out_shape=[
            jax.ShapeDtypeStruct((2, products, own_waves), BF16),
            jax.ShapeDtypeStruct((vec_count, width), BF16),
            jax.ShapeDtypeStruct((vec_count, width + own_waves), BF16),
        ],
        compiler_params=pltpu.CompilerParams(vmem_limit_bytes=40 * 2**20),
        name="transform",
    )(place, base, mirror, *tables, vec)

    p_far = shift(p_msg, halves)
    near = [shift(p_msg[:, width:], s) for s in range(1, halves)]
    far = [shift(p_far[:, width:], s) for s in range(1, halves)]
    smem = pl.BlockSpec(memory_space=pltpu.SMEM)
    vmem = pl.BlockSpec(memory_space=pltpu.VMEM)
    left_own, left_msg, q_own, *q_msgs = pl.pallas_call(
        functools.partial(screen_kernel, shifts=halves),
        in_specs=[smem] + [vmem] * (3 + 2 * (halves - 1) + 1),
        out_specs=[vmem] * (3 + halves - 1),
        out_shape=[
            jax.ShapeDtypeStruct((vec_count, width), BF16),
            jax.ShapeDtypeStruct((vec_count, width), BF16),
            jax.ShapeDtypeStruct((2, vec_count, own_waves), F32),
        ]
        + [jax.ShapeDtypeStruct((2, vec_count, own_waves), BF16)] * (halves - 1),
        compiler_params=pltpu.CompilerParams(vmem_limit_bytes=24 * 2**20),
        name="screen",
    )(place, p_first, p_msg, p_far, *near, *far, screened)
    left_far = shift(left_msg, halves)
    for s in range(1, halves):
        q_own = q_own + shift(q_msgs[s - 1], s).astype(F32)
    q_far = shift(q_own[1].astype(BF16), halves)

    vec_rows = vec_count // columns
    out_own, *out_msgs = pl.pallas_call(
        apply_kernel,
        in_specs=[smem] + [vmem] * 5,
        out_specs=[vmem] * halves,
        out_shape=[jax.ShapeDtypeStruct((2, pairs_here, vec_rows, transitions), F32)]
        + [jax.ShapeDtypeStruct((2, pairs_here, vec_rows, transitions), BF16)] * (halves - 1),
        scratch_shapes=[pltpu.VMEM((2, columns, vec_rows, transitions), F32)],
        compiler_params=pltpu.CompilerParams(vmem_limit_bytes=24 * 2**20),
        name="apply",
    )(place, left_own, left_far, q_own[0], q_far, rho)
    for s in range(1, halves):
        out_own = out_own + shift(out_msgs[s - 1], s).astype(F32)
    mine = lax.dynamic_slice_in_dim(pair_list, g * pairs_here + x, 1, 0).reshape(-1)
    k_here = k_count // groups
    owners = jnp.arange(k_count, dtype=jnp.int32).reshape(groups, 1, k_here, 1, 1)
    placed = sum(
        jnp.where(mine[slot] == owners, out_own[slot][None, :, None], 0.0) for slot in range(2)
    ).astype(BF16)
    placed = placed.reshape(groups * pairs_here, k_here, vec_rows, transitions)
    return jnp.sum(exchange(placed).astype(F32), axis=0)


def solution(mesh):
    in_specs = (P(None, "pairs", "pw"), P(None, "pairs", None), P("pairs", "pw", None), P(), P())
    out_specs = P("pairs", "pw", None)
    return jax.shard_map(local, mesh=mesh, in_specs=in_specs, out_specs=out_specs, check_vma=False)
```

time: 375 us -> 107 us (0.29)
  matrix products: 164 us -> 0.82 us
  waiting for transfers between devices: 132 us -> 39.9 us
  Pallas kernels: 0 us -> 19.4 us
  other arithmetic: 21.7 us -> 3.54 us
  blocking collectives: 32.8 us -> 16.3 us
  between operations: 13.3 us -> 0.28 us
  local copies, waits for them, and re-layouts: 5.53 us -> 14.1 us
  starting transfers between devices: 5.64 us -> 11.7 us
    dot_general x5 -> x1, matrix products: 164 us -> 0.82 us  [local(): jnp.einsum('gbn,gxlbr->xlnr', picker.reshape(groups, band_here, bands), g...]
    reduce_scatter x2 -> x0, waiting for transfers between devices: 82.2 us -> none  [the longest x1 62.8 us: local(): lax.psum_scatter(placed.astype(jnp.bfloat16), 'pairs', scatter_dimension=...]
    all_gather x2 -> x0, waiting for transfers between devices: 42 us -> none  [the longest x1 33.6 us: local(): piece = lax.all_gather(band_psi, 'pw', axis=2, tiled=True)]
    pallas_call x0 -> x3, Pallas kernels: none -> 19.4 us  [the longest x1 15.3 us: local(): pl.pallas_call(transform_kernel, grid_spec=pltpu.PrefetchScalarGridSpec(n...]
    convert_element_type x5 -> x1, other arithmetic: 19.5 us -> 0.14 us  [local(): placed = sum((jnp.where(mine[slot] == owners, out_own[slot][None, :, None...]
    all_to_all x1, waiting for transfers between devices: 7.35 us -> 25.6 us  [exchange(): lax.all_to_all(value, both, 0, 0, tiled=True, axis_index_groups=members)]
    all_to_all x1, blocking collectives: 32.8 us -> 16.3 us  [exchange(): lax.all_to_all(value, both, 0, 0, tiled=True, axis_index_groups=members)]
    ppermute x0 -> x8, waiting for transfers between devices: none -> 14.3 us  [shift(): return lax.ppermute(value, 'pw', [(i, i ^ s) for i in range(columns)])]
  transfers between devices with their start and end apart: 5 -> 9, of which waited for: 5 -> 6; matrix products, arithmetic and copies ran while one was open for 0% -> 3% of each run, Pallas kernels for 0% -> 0%
where the time goes in v1:
time: 107 us; the launch traced here: 106 us
  waiting for transfers between devices  39.9 us (37%)
  Pallas kernels  19.4 us (18%)
  blocking collectives  16.3 us (15%)
  local copies, waits for them, and re-layouts  14.1 us (13%)
  starting transfers between devices  11.7 us (11%)
  other arithmetic  3.54 us (3%)
    all_to_all x1, waiting for transfers between devices, exchange(): lax.all_to_all(value, both, 0, 0, tiled=True, axis_index_groups=members)  25.6 us
    all_to_all x1, blocking collectives, exchange(): lax.all_to_all(value, both, 0, 0, tiled=True, axis_index_groups=members)  16.3 us
    pallas_call x1, Pallas kernels, local(): pl.pallas_call(transform_kernel, grid_spec=pltpu.PrefetchScalarGridSpec(n...  15.3 us
    ppermute x8, waiting for transfers between devices, shift(): return lax.ppermute(value, 'pw', [(i, i ^ s) for i in range(columns)])  14.3 us
    unnamed x23, local copies, waits for them, and re-layouts  8.69 us
    all_to_all x1, starting transfers between devices, exchange(): lax.all_to_all(value, both, 0, 0, tiled=True, axis_index_groups=members)  8.44 us
    ppermute x8, starting transfers between devices, shift(): return lax.ppermute(value, 'pw', [(i, i ^ s) for i in range(columns)])  3.22 us
    pallas_call x1, Pallas kernels, local(): pl.pallas_call(functools.partial(screen_kernel, shifts=halves), in_specs=...  2.67 us
  transfers between devices with their start and end apart: 9, of which 6 were waited for; matrix products, arithmetic and copies ran while one was open for 3% of the time, Pallas kernels for 0%

profile of v1, /device:TPU:0, one launch (start us, length us, event | category | flops | bytes accessed | tf_op | source)
XLA Modules:
  0.0 106.0 jit_solution(7604086766164558694)
XLA Ops:
  0.0 0.8 copy.22
  0.8 0.1 reshape.70
  0.9 1.3 %pad_maximum_fusion = bf16[16,4,4352]{2,1,0:T(4,128)(2,1)S(1)} fusion(bf16[16,4,256]{2,1,0:T(4,128)(2,1)S(1)} %constant_dynamic-slice_fusion, bf16[16,4,4096]{2,1,0:T(4,128)(2,1)} %param.9), kind=kLoop, calls=%fused_computation.4 | loop fusion | flops 1114112 | bytes 1114112 | tf_op jit(solution)/shard_map/concatenate | solution.py:223
  2.2 2.5 %gather_fusion = bf16[32,4,4352]{2,1,0:T(4,128)(2,1)} fusion(bf16[16,4,4352]{2,1,0:T(4,128)(2,1)S(1)} %pad_maximum_fusion, s32[1024]{0:T(1024)S(1)} %pad_clamp_fusion), kind=kCustom, calls=%fused_computation | custom fusion | bytes 2228352 | tf_op jit(solution)/shard_map/jit(_take)/gather | solution.py:224
  4.7 8.4 %all-to-all-start = ((bf16[16,2,4,4352]{3,2,1,0:T(4,128)(2,1)}), bf16[16,2,4,4352]{3,2,1,0:T(4,128)(2,1)S(1)}, u32[]{:S(2)}, u32[]{:S(2)}) async-start(bf16[16,2,4,4352]{3,2,1,0:T(4,128)(2,1)} %bitcast.3), calls=%async_computation | async-start | bytes 2228224 | tf_op jit(solution)/shard_map/all_to_all | solution.py:217
  13.2 0.1 eq.42
  13.2 0.1 copy.24
  13.3 25.6 %all-to-all-done = bf16[16,2,4,4352]{3,2,1,0:T(4,128)(2,1)S(1)} async-done(((bf16[16,2,4,4352]{3,2,1,0:T(4,128)(2,1)}), bf16[16,2,4,4352]{3,2,1,0:T(4,128)(2,1)S(1)}, u32[]{:S(2)}, u32[]{:S(2)}) %all-to-all-start) | async-done | bytes 1114144 | tf_op jit(solution)/shard_map/all_to_all | solution.py:217
  38.9 1.0 copy-done.8
  39.9 0.5 slice.45
  40.5 0.8 fusion
  41.3 0.1 collective-permute-start
  41.4 0.1 pad_add_fusion.place
  41.5 0.9 slice_bitcast_fusion.1
  42.4 1.8 %collective-permute-done = bf16[2,2,32,4096]{3,2,1,0:T(8,128)(2,1)} collective-permute-done((bf16[2,2,32,4096]{3,2,1,0:T(8,128)(2,1)S(1)}, bf16[2,2,32,4096]{3,2,1,0:T(8,128)(2,1)}, u32[]{:S(2)}, u32[]{:S(2)}) %collective-permute-start) | collective-permute-done | bytes 1048608 | tf_op jit(solution)/shard_map/ppermute | solution.py:220
  44.2 1.6 %copy-done.3 = f32[2,256,1024]{2,1,0:T(8,128)S(1)} copy-done((f32[2,256,1024]{2,1,0:T(8,128)S(1)}, f32[2,256,1024]{2,1,0:T(8,128)}, u32[]{:S(2)}) %copy-start.3) | copy-done | bytes 2097176
  45.8 1.0 copy-done.6
  46.8 1.0 copy-done.7
  47.8 15.3 %transform.1 = (bf16[2,256,1024]{2,1,0:T(8,128)(2,1)S(1)}, bf16[64,512]{1,0:T(8,128)(2,1)S(1)}, bf16[64,1536]{1,0:T(8,128)(2,1)S(1)}) custom-call(s32[2]{0:T(128)S(1)} %pad_add_fusion.place, bf16[1,2,2,32,4096]{4,3,2,1,0:T(8,128)(2,1)S(1)} %bitcast.37, bf16[1,2,2,32,4096]{4,3,2,1,0:T(8,128)(2,1)} %bitcast.11.mirror, f32[2,256,1024]{2,1,0:T(8,128)S(1)} %copy-done.2, ...), custom_call_target="tpu_custom_call" | custom-call | tf_op jit(solution)/shard_map/transform/pallas_call | solution.py:265
  63.1 1.0 copy-done.4
  64.1 0.5 collective-permute-start.1
  64.7 0.1 collective-permute-start.2
  64.7 6.3 %collective-permute-done.1.refs_2_ = bf16[64,1536]{1,0:T(8,128)(2,1)S(1)} collective-permute-done((bf16[64,1536]{1,0:T(8,128)(2,1)S(1)}, bf16[64,1536]{1,0:T(8,128)(2,1)S(1)}, u32[]{:S(2)}, u32[]{:S(2)}) %collective-permute-start.1) | collective-permute-done | bytes 196640 | tf_op jit(solution)/shard_map/ppermute | solution.py:220
  71.0 0.1 collective-permute-start.3
  71.1 1.3 %collective-permute-done.3.refs_4_ = bf16[64,1024]{1,0:T(8,128)(2,1)S(1)} collective-permute-done((bf16[64,1024]{1,0:T(8,128)(2,1)S(1)}, bf16[64,1024]{1,0:T(8,128)(2,1)S(1)}, u32[]{:S(2)}, u32[]{:S(2)}) %collective-permute-start.3) | collective-permute-done | bytes 131104 | tf_op jit(solution)/shard_map/ppermute | solution.py:220
  72.5 2.2 %copy-done.1 = bf16[2,512,2048]{2,1,0:T(8,128)(2,1)S(1)} copy-done((bf16[2,512,2048]{2,1,0:T(8,128)(2,1)S(1)}, bf16[2,512,2048]{2,1,0:T(8,128)(2,1)}, u32[]{:S(2)}) %copy-start.1) | copy-done | bytes 4194328
  74.7 2.7 %screen.1 = (bf16[64,512]{1,0:T(8,128)(2,1)S(1)}, bf16[64,512]{1,0:T(8,128)(2,1)S(1)}, f32[2,64,1024]{2,1,0:T(8,128)S(1)}, bf16[2,64,1024]{2,1,0:T(8,128)(2,1)S(1)}) custom-call(s32[2]{0:T(128)S(1)} %pad_add_fusion.place, bf16[64,512]{1,0:T(8,128)(2,1)S(1)} %get-tuple-element.14.refs_0_, bf16[64,1536]{1,0:T(8,128)(2,1)S(1)} %get-tuple-element.15.refs_1_, ...), custom_call_target="tpu_custom_call" | custom-call | tf_op jit(solution)/shard_map/screen/pallas_call | solution.py:305
  77.3 0.2 collective-permute-start.5
  77.6 0.1 constant_dynamic-slice_fusion.1
  77.6 0.5 fusion.8
  78.2 0.7 fusion.7
  78.8 0.6 collective-permute-start.4
  79.5 0.1 convert_add_fusion
  79.6 1.5 %collective-permute-start.6 = (bf16[64,1024]{1,0:T(8,128)(2,1)S(1)}, bf16[64,1024]{1,0:T(8,128)(2,1)S(1)}, u32[]{:S(2)}, u32[]{:S(2)}) collective-permute-start(bf16[64,1024]{1,0:T(8,128)(2,1)S(1)} %fusion.2), channel_id=1, source_target_pairs={{0,2},{1,3},{2,0},{3,1},{4,6},{5,7},{6,4},{7,5},{8,10},{9,11},{10,... | collective-permute-start | bytes 393224 | tf_op jit(solution)/shard_map/ppermute | solution.py:220
  81.1 2.7 %collective-permute-done.4.left_far = bf16[64,512]{1,0:T(8,128)(2,1)S(1)} collective-permute-done((bf16[64,512]{1,0:T(8,128)(2,1)S(1)}, bf16[64,512]{1,0:T(8,128)(2,1)S(1)}, u32[]{:S(2)}, u32[]{:S(2)}) %collective-permute-start.4) | collective-permute-done | bytes 65568 | tf_op jit(solution)/shard_map/ppermute | solution.py:220
  83.8 2.2 %collective-permute-done.6.q_far = bf16[64,1024]{1,0:T(8,128)(2,1)S(1)} collective-permute-done((bf16[64,1024]{1,0:T(8,128)(2,1)S(1)}, bf16[64,1024]{1,0:T(8,128)(2,1)S(1)}, u32[]{:S(2)}, u32[]{:S(2)}) %collective-permute-start.6) | collective-permute-done | bytes 131104 | tf_op jit(solution)/shard_map/ppermute | solution.py:220
  86.1 1.5 %apply.1 = (f32[2,2,16,256]{3,2,1,0:T(8,128)S(1)}, bf16[2,2,16,256]{3,2,1,0:T(8,128)(2,1)S(1)}) custom-call(s32[2]{0:T(128)S(1)} %pad_add_fusion.place, bf16[64,512]{1,0:T(8,128)(2,1)S(1)} %get-tuple-element.16.left_own, bf16[64,512]{1,0:T(8,128)(2,1)S(1)} %collective-permute-done.4.left_far, f32[64,1024]{1,0:T(8,128)S(1)} %slice_bitcast_fusion.q_mine, ...), custom_call_target="tpu_custom_call" | custom-call | tf_op jit(solution)/shard_map/apply/pallas_call | solution.py:324
  87.6 0.1 collective-permute-start.7
  87.6 0.6 fusion.6
  88.3 0.1 broadcast_in_dim.57
  88.4 0.1 broadcast_in_dim.58
  88.5 0.1 copy.21
  88.6 0.1 broadcast_in_dim.66
  88.6 0.1 broadcast_in_dim.67
  88.7 0.1 copy.26
  88.9 0.1 add_convert_fusion
  89.1 16.3 %all_to_all.10 = bf16[16,2,16,256]{3,2,1,0:T(8,128)(2,1)S(1)} all-to-all(bf16[16,2,16,256]{3,2,1,0:T(8,128)(2,1)S(1)} %add_convert_fusion), channel_id=1, replica_groups={{0,2,4,6,8,10,12,14,16,18,20,22,24,26,28,30},{1,3,5,7,9,11,13,15,17,19,..., dimensions={0} | all-to-all | bytes 524288 | tf_op jit(solution)/shard_map/all_to_all | solution.py:217
  105.3 0.7 convert_reduce_fusion
  (31 shorter events, 0.2 us)
Async XLA Ops:
  0.0 0.9 copy-start
  4.7 8.5 %copy-start.10 = (s32[32]{0:T(128)S(1)}, s32[32]{0:T(128)}, u32[]{:S(2)}) copy-start(s32[32]{0:T(128)} %param.13) | copy-start | bytes 388
  4.7 34.2 %all-to-all-start = ((bf16[16,2,4,4352]{3,2,1,0:T(4,128)(2,1)}), bf16[16,2,4,4352]{3,2,1,0:T(4,128)(2,1)S(1)}, u32[]{:S(2)}, u32[]{:S(2)}) async-start(bf16[16,2,4,4352]{3,2,1,0:T(4,128)(2,1)} %bitcast.3), calls=%async_computation | async-start | bytes 2228224 | tf_op jit(solution)/shard_map/all_to_all | solution.py:217
  38.9 1.0 copy-start.8
  40.5 3.7 %copy-start.2 = (f32[2,256,1024]{2,1,0:T(8,128)S(1)}, f32[2,256,1024]{2,1,0:T(8,128)}, u32[]{:S(2)}) copy-start(f32[2,256,1024]{2,1,0:T(8,128)} %constant.53.clone.ca) | copy-start | bytes 6291460
  41.3 2.9 %collective-permute-start = (bf16[2,2,32,4096]{3,2,1,0:T(8,128)(2,1)S(1)}, bf16[2,2,32,4096]{3,2,1,0:T(8,128)(2,1)}, u32[]{:S(2)}, u32[]{:S(2)}) collective-permute-start(bf16[2,2,32,4096]{3,2,1,0:T(8,128)(2,1)S(1)} %bitcast.36), channel_id=1, source_target_pairs={{0,1},{1,0},{2,3},{3,2},{4,5},{5,4},{6,7},{7,6},{8,9},{9,8},{10,11... | collective-permute-start | bytes 3145736 | tf_op jit(solution)/shard_map/ppermute | solution.py:220
  44.2 1.6 %copy-start.3 = (f32[2,256,1024]{2,1,0:T(8,128)S(1)}, f32[2,256,1024]{2,1,0:T(8,128)}, u32[]{:S(2)}) copy-start(f32[2,256,1024]{2,1,0:T(8,128)} %constant.54.clone.sa) | copy-start | bytes 6291460
  45.8 1.0 copy-start.6
  46.8 1.0 copy-start.7
  63.1 1.0 copy-start.4
  64.1 6.9 %collective-permute-start.1 = (bf16[64,1536]{1,0:T(8,128)(2,1)S(1)}, bf16[64,1536]{1,0:T(8,128)(2,1)S(1)}, u32[]{:S(2)}, u32[]{:S(2)}) collective-permute-start(bf16[64,1536]{1,0:T(8,128)(2,1)S(1)} %get-tuple-element.15.refs_1_), channel_id=1, source_target_pairs={{0,2},{1,3},{2,0},{3,1},{4,6},{5,7},{6,4},{7,5},{8,10},{9,11},{10,... | collective-permute-start | bytes 589832 | tf_op jit(solution)/shard_map/ppermute | solution.py:220
  64.7 6.5 %collective-permute-start.2 = (bf16[64,1024]{1,0:T(8,128)(2,1)S(1)}, bf16[64,1024]{1,0:T(8,128)(2,1)S(1)}, u32[]{:S(2)}, u32[]{:S(2)}) collective-permute-start(bf16[64,1024]{1,0:T(8,128)(2,1)S(1)} %slice.36), channel_id=1, source_target_pairs={{0,1},{1,0},{2,3},{3,2},{4,5},{5,4},{6,7},{7,6},{8,9},{9,8},{10,11... | collective-permute-start | bytes 393224 | tf_op jit(solution)/shard_map/ppermute | solution.py:220
  71.0 1.4 %collective-permute-start.3 = (bf16[64,1024]{1,0:T(8,128)(2,1)S(1)}, bf16[64,1024]{1,0:T(8,128)(2,1)S(1)}, u32[]{:S(2)}, u32[]{:S(2)}) collective-permute-start(bf16[64,1024]{1,0:T(8,128)(2,1)S(1)} %slice.47), channel_id=1, source_target_pairs={{0,1},{1,0},{2,3},{3,2},{4,5},{5,4},{6,7},{7,6},{8,9},{9,8},{10,11... | collective-permute-start | bytes 393224 | tf_op jit(solution)/shard_map/ppermute | solution.py:220
  72.5 2.2 %copy-start.1 = (bf16[2,512,2048]{2,1,0:T(8,128)(2,1)S(1)}, bf16[2,512,2048]{2,1,0:T(8,128)(2,1)}, u32[]{:S(2)}) copy-start(bf16[2,512,2048]{2,1,0:T(8,128)(2,1)} %refs_5_.1) | copy-start | bytes 12582916
  74.6 2.9 %copy-start.9 = (s32[16,2]{0,1:T(2,128)S(1)}, s32[16,2]{0,1:T(2,128)}, u32[]{:S(2)}) copy-start(s32[16,2]{0,1:T(2,128)} %param.12) | copy-start | bytes 388
  77.3 8.7 %copy-start.5 = (bf16[2,256,1024]{2,1,0:T(8,128)(2,1)S(1)}, bf16[2,256,1024]{2,1,0:T(8,128)(2,1)}, u32[]{:S(2)}) copy-start(bf16[2,256,1024]{2,1,0:T(8,128)(2,1)} %copy-done.4) | copy-start | bytes 3145732
  77.3 2.1 %collective-permute-start.5 = (bf16[2,64,1024]{2,1,0:T(8,128)(2,1)S(1)}, bf16[2,64,1024]{2,1,0:T(8,128)(2,1)S(1)}, u32[]{:S(2)}, u32[]{:S(2)}) collective-permute-start(bf16[2,64,1024]{2,1,0:T(8,128)(2,1)S(1)} %get-tuple-element.19), channel_id=1, source_target_pairs={{0,1},{1,0},{2,3},{3,2},{4,5},{5,4},{6,7},{7,6},{8,9},{9,8},{10,11... | collective-permute-start | bytes 786440 | tf_op jit(solution)/shard_map/ppermute | solution.py:220
  78.8 5.0 %collective-permute-start.4 = (bf16[64,512]{1,0:T(8,128)(2,1)S(1)}, bf16[64,512]{1,0:T(8,128)(2,1)S(1)}, u32[]{:S(2)}, u32[]{:S(2)}) collective-permute-start(bf16[64,512]{1,0:T(8,128)(2,1)S(1)} %get-tuple-element.17), channel_id=1, source_target_pairs={{0,2},{1,3},{2,0},{3,1},{4,6},{5,7},{6,4},{7,5},{8,10},{9,11},{10,... | collective-permute-start | bytes 196616 | tf_op jit(solution)/shard_map/ppermute | solution.py:220
  79.6 6.5 %collective-permute-start.6 = (bf16[64,1024]{1,0:T(8,128)(2,1)S(1)}, bf16[64,1024]{1,0:T(8,128)(2,1)S(1)}, u32[]{:S(2)}, u32[]{:S(2)}) collective-permute-start(bf16[64,1024]{1,0:T(8,128)(2,1)S(1)} %fusion.2), channel_id=1, source_target_pairs={{0,2},{1,3},{2,0},{3,1},{4,6},{5,7},{6,4},{7,5},{8,10},{9,11},{10,... | collective-permute-start | bytes 393224 | tf_op jit(solution)/shard_map/ppermute | solution.py:220
  87.6 1.3 %collective-permute-start.7 = (bf16[2,2,16,256]{3,2,1,0:T(8,128)(2,1)S(1)}, bf16[2,2,16,256]{3,2,1,0:T(8,128)(2,1)S(1)}, u32[]{:S(2)}, u32[]{:S(2)}) collective-permute-start(bf16[2,2,16,256]{3,2,1,0:T(8,128)(2,1)S(1)} %get-tuple-element.22), channel_id=1, source_target_pairs={{0,1},{1,0},{2,3},{3,2},{4,5},{5,4},{6,7},{7,6},{8,9},{9,8},{10,11... | collective-permute-start | bytes 98312 | tf_op jit(solution)/shard_map/ppermute | solution.py:220

commit v2 on v1

v2 whole, which is shorter than its diff:
```python
import functools
import math

import jax
import jax.numpy as jnp
import numpy as np
from jax import lax
from jax.experimental import pallas as pl
from jax.experimental.pallas import tpu as pltpu
from jax.sharding import PartitionSpec as P

NV = 16
NC = 16
FINE = 64
BF16 = jnp.bfloat16
F32 = jnp.float32


def phase_tables(points, waves, halves, columns):
    width = waves // columns
    sets = []
    for j in range(halves):
        own = np.concatenate(
            [np.arange(c * width, (c + 1) * width) for c in range(j, columns, halves)]
        )
        sets.append(np.concatenate([own[0::2], own[1::2]]))
    sets = np.stack(sets)[:, None, :].astype(np.int64)
    period = 4 * points
    scale = math.sqrt(2.0 / points)
    coarse = (2 * FINE * np.arange(points // FINE)[None, :, None] * sets) % period
    fine = ((2 * np.arange(FINE) + 1)[None, :, None] * sets) % period
    turn = math.pi / (2 * points)
    return (
        (np.cos(coarse * turn) * scale).astype(np.float32),
        (np.sin(coarse * turn) * scale).astype(np.float32),
        np.cos(fine * turn).astype(np.float32),
        np.sin(fine * turn).astype(np.float32),
    )


def one_hot_matrix(size, target):
    rows = lax.broadcasted_iota(jnp.int32, (size, size), 0)
    cols = lax.broadcasted_iota(jnp.int32, (size, size), 1)
    return jnp.where(target(rows) == cols, 1.0, 0.0).astype(BF16)


def interleave(size):
    half = size // 2
    return one_hot_matrix(size, lambda r: jnp.where(r < half, 2 * r, 2 * (r - half) + 1))


def dot(a, b):
    return jnp.dot(a, b, preferred_element_type=F32)


def dot_nt(a, b):
    return lax.dot_general(a, b, (((1,), (1,)), ((), ())), preferred_element_type=F32)


def gather_kernel(requests, place, orbitals, vectors, out, sem):
    count, slots, rows = out.shape[:3]
    chunk = orbitals.shape[2]
    copies = []
    for i in range(count * slots):
        copies.append(
            pltpu.make_async_copy(
                orbitals.at[requests[i]], out.at[i // slots, i % slots, :, pl.ds(0, chunk)], sem.at[i]
            )
        )
    for copy in copies:
        copy.start()
    for i in range(count * slots):
        block = vectors[requests[i]]
        part = jnp.where(place[1] == 0, block[:rows], block[rows:])
        out[i // slots, i % slots, :, chunk:] = part
    for copy in copies:
        copy.wait()


def table_kernel(place, ca, sa, cb, sb, table, *, chunk, halves):
    j = place[0]
    rows = chunk // FINE
    for i in range(table.shape[0] // chunk):
        first = ((i % 2) * halves + (j ^ (i // 2))) * rows

        def step(a, carry):
            start = pl.multiple_of(i * chunk + a * FINE, FINE)
            table[pl.ds(start, FINE), :] = (
                ca[j, pl.ds(first + a, 1), :] * cb[j] - sa[j, pl.ds(first + a, 1), :] * sb[j]
            ).astype(BF16)
            return carry

        lax.fori_loop(0, rows, step, 0, unroll=4)


def transform_kernel(place, *refs, halves, slot):
    parts = refs[:halves]
    table, vec, rho = refs[halves : halves + 3]
    outs = refs[halves + 3 : -3]
    sums, diffs, acc = refs[-3:]
    chunk = parts[0].shape[2]
    block = sums.shape[2]
    waves = table.shape[1]
    half = waves // 2
    flip = one_hot_matrix(256, lambda r: 255 - r)
    per_chunk = chunk // block
    bands = parts[0].shape[1]
    for t in range(table.shape[0] // block):
        s, c, b = t // (2 * per_chunk), t // per_chunk % 2, t % per_chunk
        mirror = parts[s ^ (halves - 1)]
        end = chunk - b * block
        back = jnp.concatenate(
            [
                dot(mirror[1 - c, :, end - 256 * (i + 1) : end - 256 * i], flip)
                for i in range(block // 256)
            ],
            axis=1,
        )
        near = parts[s][c, :, b * block : (b + 1) * block].astype(F32)
        for v in range(NV):
            here = near[v : v + 1] * near[NV:bands]
            there = back[v : v + 1] * back[NV:bands]
            sums[t % 2, v * NC : (v + 1) * NC, :] = (here + there).astype(BF16)
            diffs[t % 2, v * NC : (v + 1) * NC, :] = (here - there).astype(BF16)
        even = dot(sums[t % 2], table[t * block : (t + 1) * block, :half])
        odd = dot(diffs[t % 2], table[t * block : (t + 1) * block, half:])
        if t == 0:
            acc[:, :half] = even
            acc[:, half:] = odd
        else:
            acc[:, :half] += even
            acc[:, half:] += odd
    done = acc[...].astype(BF16)
    rho[...] = done
    order = interleave(256)
    proj = dot(vec[...], done).astype(BF16)
    natural = jnp.concatenate(
        [
            dot(
                jnp.concatenate(
                    [proj[:, 128 * i : 128 * (i + 1)], proj[:, half + 128 * i : half + 128 * (i + 1)]],
                    axis=1,
                ),
                order,
            ).astype(BF16)
            for i in range(waves // 256)
        ],
        axis=1,
    )
    if slot == 1:
        outs[0][...] = natural
    else:
        x = place[1]
        width = outs[0].shape[1]
        first, second = natural[:, :width], natural[:, width:]
        outs[0][...] = jnp.where(x == 0, first, second)
        outs[1][...] = jnp.where(x == 0, second, first)


def back_kernel(place, p_own, p_far, screened, q_own, *q_msgs):
    j, x = place[0], place[1]
    shifts = len(q_msgs) + 1
    width = p_own.shape[1]
    for rel in range(2):
        pair = x if rel == 0 else 1 - x
        first = p_own[...] if rel == 0 else p_far[...]
        for s in range(shifts):
            for c in range(2):
                start = pl.multiple_of((c * shifts + (j ^ s)) * width, width)
                back = dot(first, screened[pair, :, pl.ds(start, width)])
                if s == 0:
                    q_own[rel, :, c * width : (c + 1) * width] = back
                else:
                    q_msgs[s - 1][rel, :, c * width : (c + 1) * width] = back.astype(BF16)


def left_kernel(place, *refs):
    j, x = place[0], place[1]
    sources, (screened, left_own, left_msg) = refs[:-3], refs[-3:]
    shifts = len(sources) // 2
    width = left_own.shape[1]
    for rel in range(2):
        pair = x if rel == 0 else 1 - x
        total = None
        for s in range(shifts):
            source = sources[rel * shifts + s]
            for c in range(2):
                start = pl.multiple_of((c * shifts + (j ^ s)) * width, width)
                term = dot_nt(
                    source[:, c * width : (c + 1) * width], screened[pair, :, pl.ds(start, width)]
                )
                total = term if total is None else total + term
        (left_msg if rel else left_own)[...] = total.astype(BF16)


def apply_kernel(place, left_own, left_far, q_mine, q_far, rho_first, rho_second, own, *refs):
    j, x = place[0], place[1]
    msgs, scratch = refs[:-1], refs[-1]
    shifts = len(msgs) + 1
    waves = rho_first.shape[1]
    order = interleave(256)
    mine, other = left_own[...], left_far[...]
    first = jnp.concatenate([jnp.where(x == 0, mine, other), jnp.where(x == 0, other, mine)], axis=1)
    second = (q_mine[...] + q_far[...].astype(F32)).astype(BF16)
    for slot, weight in enumerate((first, second)):
        parts = [
            dot_nt(weight[:, 256 * i : 256 * (i + 1)], order).astype(BF16)
            for i in range(waves // 256)
        ]
        sorted_weight = jnp.concatenate([p[:, :128] for p in parts] + [p[:, 128:] for p in parts], axis=1)
        scratch[slot] = dot_nt(sorted_weight, (rho_first, rho_second)[slot][...]).reshape(scratch.shape[1:])
    for s in range(shifts):
        for c in range(2):
            for slot in range(2):
                value = scratch[slot, c * shifts + (j ^ s)]
                if s == 0:
                    own[slot, c] = value
                else:
                    msgs[s - 1][slot, c] = value.astype(BF16)


def local(orbitals, vectors, screened, pair_list, band_order):
    groups = lax.axis_size("pairs")
    columns = lax.axis_size("pw")
    pairs_here = screened.shape[0]
    halves = columns // pairs_here
    both = ("pairs", "pw")
    g = lax.axis_index("pairs")
    w = lax.axis_index("pw")
    x, j = w // halves, w % halves
    place = jnp.stack([j, x]).astype(jnp.int32)
    k_count, band_here, chunk = orbitals.shape
    points = chunk * columns
    waves = screened.shape[2]
    width = waves // columns
    own_waves = width * pairs_here
    transitions = vectors.shape[2]
    vec_count = vectors.shape[1] * groups
    vec_part = vectors.shape[1] // pairs_here
    bands = band_here * groups
    members = [
        [gg * columns + xx * halves + jj for gg in range(groups) for xx in range(pairs_here)]
        for jj in range(halves)
    ]

    def exchange(value):
        return lax.all_to_all(value, both, 0, 0, tiled=True, axis_index_groups=members)

    def shift(value, s):
        return lax.ppermute(value, "pw", [(i, i ^ s) for i in range(columns)])

    def call(kernel, outs, *args, flops=0, scratch=(), limit=4, scalars=1):
        moved = sum(math.prod(v.shape) * v.dtype.itemsize for v in (*args, *outs))
        return pl.pallas_call(
            kernel,
            in_specs=[smem] * scalars + [vmem] * (len(args) - scalars),
            out_specs=[vmem] * len(outs),
            out_shape=list(outs),
            scratch_shapes=list(scratch),
            compiler_params=pltpu.CompilerParams(vmem_limit_bytes=limit * 2**20),
            cost_estimate=pl.CostEstimate(flops=flops, bytes_accessed=moved, transcendentals=0),
        )(*args)

    smem = pl.BlockSpec(memory_space=pltpu.SMEM)
    vmem = pl.BlockSpec(memory_space=pltpu.VMEM)
    like = jax.ShapeDtypeStruct

    slots = 2 * groups * pairs_here
    sent = pl.pallas_call(
        gather_kernel,
        in_specs=[smem, smem, pl.BlockSpec(memory_space=pl.ANY), vmem],
        out_specs=vmem,
        out_shape=like((slots // 2, 2, band_here, chunk + transitions), BF16),
        scratch_shapes=[pltpu.SemaphoreType.DMA((slots,))],
        compiler_params=pltpu.CompilerParams(vmem_limit_bytes=8 * 2**20),
    )(pair_list.reshape(-1), place, orbitals, vectors)
    got = exchange(sent).reshape(groups, pairs_here, 2, band_here, chunk + transitions)
    tables = [jnp.asarray(t) for t in phase_tables(points, waves, halves, columns)]
    (table,) = call(
        functools.partial(table_kernel, chunk=chunk, halves=halves),
        [like((points // 2, own_waves), BF16)],
        place,
        *tables,
        flops=3 * points // 2 * own_waves,
        limit=2,
    )
    vec = got[..., chunk:].transpose(2, 0, 1, 3, 4).reshape(2, vec_count, transitions)
    picker = (band_order[:, None] == jnp.arange(bands, dtype=jnp.int32)[None, :]).astype(BF16)
    psi = jnp.einsum(
        "gbn,gxlbr->lxnr",
        picker.reshape(groups, band_here, bands),
        got[..., :chunk],
        preferred_element_type=F32,
    ).astype(BF16)
    products = NV * NC
    block = min(2048, chunk)

    def transform(slot, outs):
        parts = [psi[slot]] + [shift(psi[slot], s) for s in range(1, halves)]
        return call(
            functools.partial(transform_kernel, halves=halves, slot=slot),
            [like((products, own_waves), BF16)] + outs,
            place,
            *parts,
            table,
            vec[slot],
            flops=products * points * own_waves,
            scratch=[pltpu.VMEM((2, products, block), BF16)] * 2
            + [pltpu.VMEM((products, own_waves), F32)],
            limit=12,
        )

    shape = like((vec_count, width), BF16)
    full = like((vec_count, own_waves), BF16)
    rho_first, p_own, p_msg = transform(0, [shape, shape])
    rho_second, p_second = transform(1, [full])
    p_far = shift(p_msg, halves)
    far = shift(p_second, halves)
    near = [shift(p_second, s) for s in range(1, halves)]
    fars = [shift(far, s) for s in range(1, halves)]
    both_q = like((2, vec_count, own_waves), F32)
    flops = 4 * vec_count * width * waves
    q_own, *q_msgs = call(
        back_kernel,
        [both_q] + [like(both_q.shape, BF16)] * (halves - 1),
        place,
        p_own,
        p_far,
        screened,
        flops=flops,
    )
    for s in range(1, halves):
        q_own = q_own + shift(q_msgs[s - 1], s).astype(F32)
    q_far = shift(q_own[1].astype(BF16), halves)
    left_own, left_msg = call(
        left_kernel, [shape, shape], place, p_second, *near, far, *fars, screened, flops=flops
    )
    left_far = shift(left_msg, halves)

    vec_rows = vec_count // columns
    terms = like((2, pairs_here, vec_rows, transitions), F32)
    out_own, *out_msgs = call(
        apply_kernel,
        [terms] + [like(terms.shape, BF16)] * (halves - 1),
        place,
        left_own,
        left_far,
        q_own[0],
        q_far,
        rho_first,
        rho_second,
        flops=4 * vec_count * products * own_waves,
        scratch=[pltpu.VMEM((2, columns, vec_rows, transitions), F32)],
    )
    for s in range(1, halves):
        out_own = out_own + shift(out_msgs[s - 1], s).astype(F32)
    mine = lax.dynamic_slice_in_dim(pair_list, g * pairs_here + x, 1, 0).reshape(-1)
    k_here = k_count // groups
    owners = jnp.arange(k_count, dtype=jnp.int32).reshape(groups, 1, k_here, 1, 1)
    placed = sum(
        jnp.where(mine[slot] == owners, out_own[slot][None, :, None], 0.0) for slot in range(2)
    ).astype(BF16)
    placed = placed.reshape(groups * pairs_here, k_here, vec_rows, transitions)
    return jnp.sum(exchange(placed).astype(F32), axis=0)


def solution(mesh):
    in_specs = (P(None, "pairs", "pw"), P(None, "pairs", None), P("pairs", "pw", None), P(), P())
    out_specs = P("pairs", "pw", None)
    return jax.shard_map(local, mesh=mesh, in_specs=in_specs, out_specs=out_specs, check_vma=False)
```

time: 107 us -> 121 us (1.13)
  Pallas kernels: 19.4 us -> 31 us
  local copies, waits for them, and re-layouts: 14.1 us -> 22.4 us
  waiting for transfers between devices: 39.9 us -> 32.8 us
  starting transfers between devices: 11.7 us -> 13.4 us
  other arithmetic: 3.54 us -> 2.21 us
    pallas_call x3 -> x7, Pallas kernels: 19.4 us -> 31 us  [the longest x6 27.6 us: call(): pl.pallas_call(kernel, in_specs=[smem] * scalars + [vmem] * (len(args) -...]
    unnamed x23 -> x25, local copies, waits for them, and re-layouts: 8.69 us -> 19.4 us
    ppermute x8 -> x10, waiting for transfers between devices: 14.3 us -> 7.23 us  [shift(): return lax.ppermute(value, 'pw', [(i, i ^ s) for i in range(columns)])]
    gather x1 -> x0, local copies, waits for them, and re-layouts: 2.46 us -> none  [local(): sent = jnp.take(stored, pair_list.reshape(-1), axis=0, mode='clip')]
    ppermute x8 -> x10, starting transfers between devices: 3.22 us -> 5.03 us  [shift(): return lax.ppermute(value, 'pw', [(i, i ^ s) for i in range(columns)])]
    concatenate x1 -> x0, other arithmetic: 1.29 us -> none  [local(): stored = jnp.concatenate([orbitals, vec_mine], axis=2)]
  transfers between devices with their start and end apart: 9 -> 11, of which waited for: 6 -> 5; matrix products, arithmetic and copies ran while one was open for 3% -> 3% of each run, Pallas kernels for 0% -> 22%
where the time goes in v2:
time: 121 us; the launch traced here: 120 us
  waiting for transfers between devices  32.8 us (27%)
  Pallas kernels  31 us (26%)
  local copies, waits for them, and re-layouts  22.4 us (19%)
  blocking collectives  17.2 us (14%)
  starting transfers between devices  13.4 us (11%)
  other arithmetic  2.21 us (2%)
    pallas_call x6, Pallas kernels, call(): pl.pallas_call(kernel, in_specs=[smem] * scalars + [vmem] * (len(args) -...  27.6 us
    all_to_all x1, waiting for transfers between devices, exchange(): lax.all_to_all(value, both, 0, 0, tiled=True, axis_index_groups=members)  25.6 us
    unnamed x25, local copies, waits for them, and re-layouts  19.4 us
    all_to_all x1, blocking collectives, exchange(): lax.all_to_all(value, both, 0, 0, tiled=True, axis_index_groups=members)  17.2 us
    all_to_all x1, starting transfers between devices, exchange(): lax.all_to_all(value, both, 0, 0, tiled=True, axis_index_groups=members)  8.32 us
    ppermute x10, waiting for transfers between devices, shift(): return lax.ppermute(value, 'pw', [(i, i ^ s) for i in range(columns)])  7.23 us
    ppermute x10, starting transfers between devices, shift(): return lax.ppermute(value, 'pw', [(i, i ^ s) for i in range(columns)])  5.03 us
    pallas_call x1, Pallas kernels, local(): pl.pallas_call(gather_kernel, in_specs=[smem, smem, pl.BlockSpec(memory_s...  3.36 us
  transfers between devices with their start and end apart: 11, of which 5 were waited for; matrix products, arithmetic and copies ran while one was open for 3% of the time, Pallas kernels for 22%

profile of v2, /device:TPU:0, one launch (start us, length us, event | category | flops | bytes accessed | tf_op | source)
XLA Modules:
  0.0 120.1 jit_solution(14539192231820406888)
XLA Ops:
  0.0 0.8 copy.25
  0.8 0.1 reshape.65.requests
  0.9 0.1 pad_add_fusion.place
  1.0 1.0 copy-done.5
  2.0 0.8 copy-done.8
  2.8 3.4 %shard_map.91 = bf16[16,2,4,4352]{3,2,1,0:T(4,128)(2,1)} custom-call(s32[32]{0:T(128)S(1)} %reshape.65.requests, s32[2]{0:T(128)S(1)} %pad_add_fusion.place, bf16[16,4,4096]{2,1,0:T(4,128)(2,1)S(1)} %copy-done.5, bf16[16,8,256]{2,1,0:T(8,128)(2,1)S(1)} %copy-done.8), custom_call_target="tpu_custom_call" | custom-call | tf_op jit(solution)/shard_map/pallas_call | solution.py:269
  6.2 8.3 %all-to-all-start = ((bf16[16,2,4,4352]{3,2,1,0:T(4,128)(2,1)}), bf16[16,2,4,4352]{3,2,1,0:T(4,128)(2,1)S(1)}, u32[]{:S(2)}, u32[]{:S(2)}) async-start(bf16[16,2,4,4352]{3,2,1,0:T(4,128)(2,1)} %shard_map.91), calls=%async_computation | async-start | bytes 2228224 | tf_op jit(solution)/shard_map/all_to_all | solution.py:247
  14.6 0.1 eq.42
  14.6 0.1 copy.27
  14.7 25.6 %all-to-all-done = bf16[16,2,4,4352]{3,2,1,0:T(4,128)(2,1)S(1)} async-done(((bf16[16,2,4,4352]{3,2,1,0:T(4,128)(2,1)}), bf16[16,2,4,4352]{3,2,1,0:T(4,128)(2,1)S(1)}, u32[]{:S(2)}, u32[]{:S(2)}) %all-to-all-start) | async-done | bytes 1114144 | tf_op jit(solution)/shard_map/all_to_all | solution.py:247
  40.3 1.0 copy-done.9
  41.3 0.5 slice.55
  41.9 0.8 fusion.1
  42.7 0.1 slice_bitcast_fusion
  42.9 0.6 copy-done.3
  43.4 1.6 %copy-done.4 = f32[2,256,1024]{2,1,0:T(8,128)S(1)} copy-done((f32[2,256,1024]{2,1,0:T(8,128)S(1)}, f32[2,256,1024]{2,1,0:T(8,128)}, u32[]{:S(2)}) %copy-start.4) | copy-done | bytes 2097176
  45.0 1.0 copy-done.6
  46.1 1.0 copy-done.7
  47.1 9.5 %shard_map.92.refs_2_ = bf16[8192,1024]{1,0:T(8,128)(2,1)S(1)} custom-call(s32[2]{0:T(128)S(1)} %pad_add_fusion.place, f32[2,256,1024]{2,1,0:T(8,128)S(1)} %copy-done.3, f32[2,256,1024]{2,1,0:T(8,128)S(1)} %copy-done.4, f32[2,64,1024]{2,1,0:T(8,128)S(1)} %copy-done.6, f32[2,64,1024]{2,1,0:T(8,128)S(1)} %copy-done.7), custom_call_target="tpu_custom_call" | custom-call | flops 25165824 | bytes 22020104 | tf_op jit(solution)/shard_map/pallas_call | solution.py:254
  56.6 5.7 %copy-done = bf16[8192,1024]{1,0:T(8,128)(2,1)} copy-done((bf16[8192,1024]{1,0:T(8,128)(2,1)}, bf16[8192,1024]{1,0:T(8,128)(2,1)S(1)}, u32[]{:S(2)}) %copy-start) | copy-done | bytes 16777240
  62.3 0.9 copy_bitcast_fusion
  63.3 5.8 %copy-done.1 = bf16[8192,1024]{1,0:T(8,128)(2,1)S(1)} copy-done((bf16[8192,1024]{1,0:T(8,128)(2,1)S(1)}, bf16[8192,1024]{1,0:T(8,128)(2,1)}, u32[]{:S(2)}) %copy-start.1) | copy-done | bytes 16777240
  69.1 6.9 %shard_map.95 = (bf16[256,1024]{1,0:T(8,128)(2,1)S(1)}, bf16[64,512]{1,0:T(8,128)(2,1)S(1)}, bf16[64,512]{1,0:T(8,128)(2,1)S(1)}) custom-call(s32[2]{0:T(128)S(1)} %pad_add_fusion.place, bf16[2,32,4096]{2,1,0:T(8,128)(2,1)S(1)} %get-tuple-element.27.refs_0_, bf16[2,32,4096]{2,1,0:T(8,128)(2,1)} %collective-permute-done.5.refs_1_, ...), custom_call_target="tpu_custom_call" | custom-call | flops 4294967296 | bytes 18513928 | tf_op jit(solution)/shard_map/pallas_call | solution.py:254
  76.0 0.6 collective-permute-start.6
  76.6 6.4 %shard_map.93 = (bf16[256,1024]{1,0:T(8,128)(2,1)S(1)}, bf16[64,1024]{1,0:T(8,128)(2,1)S(1)}) custom-call(s32[2]{0:T(128)S(1)} %pad_add_fusion.place, bf16[2,32,4096]{2,1,0:T(8,128)(2,1)S(1)} %get-tuple-element.28.refs_0_, bf16[2,32,4096]{2,1,0:T(8,128)(2,1)S(1)} %collective-permute-done.refs_1_, bf16[8192,1024]{1,0:T(8,128)(2,1)S(1)} %copy-done.1, ...), custom_call_target="tpu_custom_call" | custom-call | flops 4294967296 | bytes 18513928 | tf_op jit(solution)/shard_map/pallas_call | solution.py:254
  83.1 1.5 %collective-permute-start.2 = (bf16[64,1024]{1,0:T(8,128)(2,1)S(1)}, bf16[64,1024]{1,0:T(8,128)(2,1)S(1)}, u32[]{:S(2)}, u32[]{:S(2)}) collective-permute-start(bf16[64,1024]{1,0:T(8,128)(2,1)S(1)} %get-tuple-element.16.refs_0_), channel_id=1, source_target_pairs={{0,2},{1,3},{2,0},{3,1},{4,6},{5,7},{6,4},{7,5},{8,10},{9,11},{10,... | collective-permute-start | bytes 393224 | tf_op jit(solution)/shard_map/ppermute | solution.py:250
  84.6 1.4 %shard_map.96 = (f32[2,64,1024]{2,1,0:T(8,128)S(1)}, bf16[2,64,1024]{2,1,0:T(8,128)(2,1)S(1)}) custom-call(s32[2]{0:T(128)S(1)} %pad_add_fusion.place, bf16[64,512]{1,0:T(8,128)(2,1)S(1)} %get-tuple-element.19.p_own, bf16[64,512]{1,0:T(8,128)(2,1)S(1)} %collective-permute-done.6.p_far, bf16[2,512,2048]{2,1,0:T(8,128)(2,1)S(1)} %copy-done.2), custom_call_target="tpu_custom_call" | custom-call | flops 268435456 | bytes 5111816 | tf_op jit(solution)/shard_map/pallas_call | solution.py:254
  86.1 0.1 constant_dynamic-slice_fusion
  86.1 0.5 collective-permute-start.1
  86.6 2.1 %collective-permute-done.2.refs_2_ = bf16[64,1024]{1,0:T(8,128)(2,1)S(1)} collective-permute-done((bf16[64,1024]{1,0:T(8,128)(2,1)S(1)}, bf16[64,1024]{1,0:T(8,128)(2,1)S(1)}, u32[]{:S(2)}, u32[]{:S(2)}) %collective-permute-start.2) | collective-permute-done | bytes 131104 | tf_op jit(solution)/shard_map/ppermute | solution.py:250
  88.7 0.6 fusion.10
  89.3 0.6 fusion.7
  89.9 0.2 collective-permute-done.3.refs_3_
  90.1 1.9 %shard_map.94 = (bf16[64,512]{1,0:T(8,128)(2,1)S(1)}, bf16[64,512]{1,0:T(8,128)(2,1)S(1)}) custom-call(s32[2]{0:T(128)S(1)} %pad_add_fusion.place, bf16[64,1024]{1,0:T(8,128)(2,1)S(1)} %get-tuple-element.16.refs_0_, bf16[64,1024]{1,0:T(8,128)(2,1)S(1)} %collective-permute-done.1.refs_1_, bf16[64,1024]{1,0:T(8,128)(2,1)S(1)} %collective-permute-done.2.refs_2_, ...), custom_call_target="tpu_custom_call" | custom-call | flops 268435456 | bytes 4849672 | tf_op jit(solution)/shard_map/pallas_call | solution.py:254
  92.0 1.6 %collective-permute-start.4 = (bf16[64,512]{1,0:T(8,128)(2,1)S(1)}, bf16[64,512]{1,0:T(8,128)(2,1)S(1)}, u32[]{:S(2)}, u32[]{:S(2)}) collective-permute-start(bf16[64,512]{1,0:T(8,128)(2,1)S(1)} %get-tuple-element.18), channel_id=1, source_target_pairs={{0,2},{1,3},{2,0},{3,1},{4,6},{5,7},{6,4},{7,5},{8,10},{9,11},{10,... | collective-permute-start | bytes 196616 | tf_op jit(solution)/shard_map/ppermute | solution.py:250
  93.7 0.6 collective-permute-start.8
  94.3 2.2 %collective-permute-done.4.left_far = bf16[64,512]{1,0:T(8,128)(2,1)S(1)} collective-permute-done((bf16[64,512]{1,0:T(8,128)(2,1)S(1)}, bf16[64,512]{1,0:T(8,128)(2,1)S(1)}, u32[]{:S(2)}, u32[]{:S(2)}) %collective-permute-start.4) | collective-permute-done | bytes 65568 | tf_op jit(solution)/shard_map/ppermute | solution.py:250
  96.5 2.7 %collective-permute-done.8.q_far = bf16[64,1024]{1,0:T(8,128)(2,1)S(1)} collective-permute-done((bf16[64,1024]{1,0:T(8,128)(2,1)S(1)}, bf16[64,1024]{1,0:T(8,128)(2,1)S(1)}, u32[]{:S(2)}, u32[]{:S(2)}) %collective-permute-start.8) | collective-permute-done | bytes 131104 | tf_op jit(solution)/shard_map/ppermute | solution.py:250
  99.2 1.5 %shard_map.97 = (f32[2,2,16,256]{3,2,1,0:T(8,128)S(1)}, bf16[2,2,16,256]{3,2,1,0:T(8,128)(2,1)S(1)}) custom-call(s32[2]{0:T(128)S(1)} %pad_add_fusion.place, bf16[64,512]{1,0:T(8,128)(2,1)S(1)} %get-tuple-element.17.left_own, bf16[64,512]{1,0:T(8,128)(2,1)S(1)} %collective-permute-done.4.left_far, f32[64,1024]{1,0:T(8,128)S(1)} %slice_bitcast_fusion.2.q_mine, ...), custom_call_target="tpu_custom_call" | custom-call | flops 67108864 | bytes 1671176 | tf_op jit(solution)/shard_map/pallas_call | solution.py:254
  100.8 0.7 fusion.8
  101.5 0.1 broadcast_in_dim.61
  101.6 0.1 broadcast_in_dim.62
  101.6 0.1 copy.30
  101.8 0.1 broadcast_in_dim.54
  101.9 0.1 copy.24
  102.1 0.1 add_convert_fusion
  102.3 17.2 %all_to_all.10 = bf16[16,2,16,256]{3,2,1,0:T(8,128)(2,1)S(1)} all-to-all(bf16[16,2,16,256]{3,2,1,0:T(8,128)(2,1)S(1)} %add_convert_fusion), channel_id=1, replica_groups={{0,2,4,6,8,10,12,14,16,18,20,22,24,26,28,30},{1,3,5,7,9,11,13,15,17,19,..., dimensions={0} | all-to-all | bytes 524288 | tf_op jit(solution)/shard_map/all_to_all | solution.py:247
  119.5 0.7 convert_reduce_fusion
  (37 shorter events, 0.5 us)
Async XLA Ops:
  0.0 14.5 %copy-start.11 = (s32[32]{0:T(128)S(1)}, s32[32]{0:T(128)}, u32[]{:S(2)}) copy-start(s32[32]{0:T(128)} %param.13) | copy-start | bytes 388
  1.0 1.0 copy-start.5
  2.0 0.8 copy-start.8
  6.2 34.1 %all-to-all-start = ((bf16[16,2,4,4352]{3,2,1,0:T(4,128)(2,1)}), bf16[16,2,4,4352]{3,2,1,0:T(4,128)(2,1)S(1)}, u32[]{:S(2)}, u32[]{:S(2)}) async-start(bf16[16,2,4,4352]{3,2,1,0:T(4,128)(2,1)} %shard_map.91), calls=%async_computation | async-start | bytes 2228224 | tf_op jit(solution)/shard_map/all_to_all | solution.py:247
  40.3 1.0 copy-start.9
  41.9 1.6 %copy-start.3 = (f32[2,256,1024]{2,1,0:T(8,128)S(1)}, f32[2,256,1024]{2,1,0:T(8,128)}, u32[]{:S(2)}) copy-start(f32[2,256,1024]{2,1,0:T(8,128)} %constant.49.clone.ca) | copy-start | bytes 6291460
  42.8 20.5 %collective-permute-start.5 = (bf16[2,32,4096]{2,1,0:T(8,128)(2,1)S(1)}, bf16[2,32,4096]{2,1,0:T(8,128)(2,1)}, u32[]{:S(2)}, u32[]{:S(2)}) collective-permute-start(bf16[2,32,4096]{2,1,0:T(8,128)(2,1)S(1)} %get-tuple-element.27.refs_0_), channel_id=1, source_target_pairs={{0,1},{1,0},{2,3},{3,2},{4,5},{5,4},{6,7},{7,6},{8,9},{9,8},{10,11... | collective-permute-start | bytes 1572872 | tf_op jit(solution)/shard_map/ppermute | solution.py:250
  43.4 1.6 %copy-start.4 = (f32[2,256,1024]{2,1,0:T(8,128)S(1)}, f32[2,256,1024]{2,1,0:T(8,128)}, u32[]{:S(2)}) copy-start(f32[2,256,1024]{2,1,0:T(8,128)} %constant.50.clone.sa) | copy-start | bytes 6291460
  45.0 1.0 copy-start.6
  46.1 1.0 copy-start.7
  56.6 5.7 %copy-start = (bf16[8192,1024]{1,0:T(8,128)(2,1)}, bf16[8192,1024]{1,0:T(8,128)(2,1)S(1)}, u32[]{:S(2)}) copy-start(bf16[8192,1024]{1,0:T(8,128)(2,1)S(1)} %shard_map.92.refs_2_) | copy-start | bytes 50331652
  62.3 14.3 %collective-permute-start = (bf16[2,32,4096]{2,1,0:T(8,128)(2,1)S(1)}, bf16[2,32,4096]{2,1,0:T(8,128)(2,1)S(1)}, u32[]{:S(2)}, u32[]{:S(2)}) collective-permute-start(bf16[2,32,4096]{2,1,0:T(8,128)(2,1)S(1)} %get-tuple-element.28.refs_0_), channel_id=1, source_target_pairs={{0,1},{1,0},{2,3},{3,2},{4,5},{5,4},{6,7},{7,6},{8,9},{9,8},{10,11... | collective-permute-start | bytes 1572872 | tf_op jit(solution)/shard_map/ppermute | solution.py:250
  63.3 5.8 %copy-start.1 = (bf16[8192,1024]{1,0:T(8,128)(2,1)S(1)}, bf16[8192,1024]{1,0:T(8,128)(2,1)}, u32[]{:S(2)}) copy-start(bf16[8192,1024]{1,0:T(8,128)(2,1)} %copy-done) | copy-start | bytes 50331652
  76.0 8.6 %collective-permute-start.6 = (bf16[64,512]{1,0:T(8,128)(2,1)S(1)}, bf16[64,512]{1,0:T(8,128)(2,1)S(1)}, u32[]{:S(2)}, u32[]{:S(2)}) collective-permute-start(bf16[64,512]{1,0:T(8,128)(2,1)S(1)} %get-tuple-element.20), channel_id=1, source_target_pairs={{0,2},{1,3},{2,0},{3,1},{4,6},{5,7},{6,4},{7,5},{8,10},{9,11},{10,... | collective-permute-start | bytes 196616 | tf_op jit(solution)/shard_map/ppermute | solution.py:250
  76.6 7.9 %copy-start.2 = (bf16[2,512,2048]{2,1,0:T(8,128)(2,1)S(1)}, bf16[2,512,2048]{2,1,0:T(8,128)(2,1)}, u32[]{:S(2)}) copy-start(bf16[2,512,2048]{2,1,0:T(8,128)(2,1)} %screened.1) | copy-start | bytes 12582916
  83.1 5.7 %collective-permute-start.2 = (bf16[64,1024]{1,0:T(8,128)(2,1)S(1)}, bf16[64,1024]{1,0:T(8,128)(2,1)S(1)}, u32[]{:S(2)}, u32[]{:S(2)}) collective-permute-start(bf16[64,1024]{1,0:T(8,128)(2,1)S(1)} %get-tuple-element.16.refs_0_), channel_id=1, source_target_pairs={{0,2},{1,3},{2,0},{3,1},{4,6},{5,7},{6,4},{7,5},{8,10},{9,11},{10,... | collective-permute-start | bytes 393224 | tf_op jit(solution)/shard_map/ppermute | solution.py:250
  84.6 1.5 %copy-start.10 = (s32[16,2]{0,1:T(2,128)S(1)}, s32[16,2]{0,1:T(2,128)}, u32[]{:S(2)}) copy-start(s32[16,2]{0,1:T(2,128)} %param.12) | copy-start | bytes 388
  86.0 7.6 %collective-permute-start.7 = (bf16[2,64,1024]{2,1,0:T(8,128)(2,1)S(1)}, bf16[2,64,1024]{2,1,0:T(8,128)(2,1)S(1)}, u32[]{:S(2)}, u32[]{:S(2)}) collective-permute-start(bf16[2,64,1024]{2,1,0:T(8,128)(2,1)S(1)} %get-tuple-element.22), channel_id=1, source_target_pairs={{0,1},{1,0},{2,3},{3,2},{4,5},{5,4},{6,7},{7,6},{8,9},{9,8},{10,11... | collective-permute-start | bytes 786440 | tf_op jit(solution)/shard_map/ppermute | solution.py:250
  86.1 3.8 %collective-permute-start.1 = (bf16[64,1024]{1,0:T(8,128)(2,1)S(1)}, bf16[64,1024]{1,0:T(8,128)(2,1)S(1)}, u32[]{:S(2)}, u32[]{:S(2)}) collective-permute-start(bf16[64,1024]{1,0:T(8,128)(2,1)S(1)} %get-tuple-element.16.refs_0_), channel_id=1, source_target_pairs={{0,1},{1,0},{2,3},{3,2},{4,5},{5,4},{6,7},{7,6},{8,9},{9,8},{10,11... | collective-permute-start | bytes 393224 | tf_op jit(solution)/shard_map/ppermute | solution.py:250
  88.7 1.3 %collective-permute-start.3 = (bf16[64,1024]{1,0:T(8,128)(2,1)S(1)}, bf16[64,1024]{1,0:T(8,128)(2,1)S(1)}, u32[]{:S(2)}, u32[]{:S(2)}) collective-permute-start(bf16[64,1024]{1,0:T(8,128)(2,1)S(1)} %collective-permute-done.2.refs_2_), channel_id=1, source_target_pairs={{0,1},{1,0},{2,3},{3,2},{4,5},{5,4},{6,7},{7,6},{8,9},{9,8},{10,11... | collective-permute-start | bytes 393224 | tf_op jit(solution)/shard_map/ppermute | solution.py:250
  92.0 4.5 %collective-permute-start.4 = (bf16[64,512]{1,0:T(8,128)(2,1)S(1)}, bf16[64,512]{1,0:T(8,128)(2,1)S(1)}, u32[]{:S(2)}, u32[]{:S(2)}) collective-permute-start(bf16[64,512]{1,0:T(8,128)(2,1)S(1)} %get-tuple-element.18), channel_id=1, source_target_pairs={{0,2},{1,3},{2,0},{3,1},{4,6},{5,7},{6,4},{7,5},{8,10},{9,11},{10,... | collective-permute-start | bytes 196616 | tf_op jit(solution)/shard_map/ppermute | solution.py:250
  93.7 5.6 %collective-permute-start.8 = (bf16[64,1024]{1,0:T(8,128)(2,1)S(1)}, bf16[64,1024]{1,0:T(8,128)(2,1)S(1)}, u32[]{:S(2)}, u32[]{:S(2)}) collective-permute-start(bf16[64,1024]{1,0:T(8,128)(2,1)S(1)} %fusion.3), channel_id=1, source_target_pairs={{0,2},{1,3},{2,0},{3,1},{4,6},{5,7},{6,4},{7,5},{8,10},{9,11},{10,... | collective-permute-start | bytes 393224 | tf_op jit(solution)/shard_map/ppermute | solution.py:250
  100.7 1.3 %collective-permute-start.9 = (bf16[2,2,16,256]{3,2,1,0:T(8,128)(2,1)S(1)}, bf16[2,2,16,256]{3,2,1,0:T(8,128)(2,1)S(1)}, u32[]{:S(2)}, u32[]{:S(2)}) collective-permute-start(bf16[2,2,16,256]{3,2,1,0:T(8,128)(2,1)S(1)} %get-tuple-element.26), channel_id=1, source_target_pairs={{0,1},{1,0},{2,3},{3,2},{4,5},{5,4},{6,7},{7,6},{8,9},{9,8},{10,11... | collective-permute-start | bytes 98312 | tf_op jit(solution)/shard_map/ppermute | solution.py:250

commit v3 on v2

v3 whole, which is shorter than its diff:
```python
import functools
import math

import jax
import jax.numpy as jnp
import numpy as np
from jax import lax
from jax.experimental import pallas as pl
from jax.experimental.pallas import tpu as pltpu
from jax.sharding import PartitionSpec as P

NV = 16
NC = 16
FINE = 64
BF16 = jnp.bfloat16
F32 = jnp.float32


def column_order(size):
    return np.concatenate([np.arange(0, size, 4), np.arange(2, size, 4), np.arange(1, size, 2)])


def phase_tables(points, waves, halves, columns):
    width, chunk = waves // columns, points // columns
    period, turn = 4 * points, math.pi / (2 * points)
    scale = math.sqrt(2.0 / points)
    seeds = []
    for j in range(halves):
        own = np.concatenate(
            [np.arange(c * width, (c + 1) * width) for c in range(j, columns, halves)]
        )
        own = own[column_order(own.size)].astype(np.int64)
        starts = np.concatenate(
            [
                np.arange((c * halves + (j ^ s)) * chunk, (c * halves + (j ^ s) + 1) * chunk, FINE)
                for s in range(halves // 2)
                for c in range(columns // halves)
            ]
        )
        coarse = (2 * starts[:, None] * own) % period * turn
        fine = ((2 * np.arange(FINE) + 1)[:, None] * own) % period * turn
        seeds.append(
            [
                np.concatenate([np.cos(coarse) * scale, np.cos(fine)]),
                np.concatenate([np.sin(coarse) * scale, np.sin(fine)]),
            ]
        )
    return np.array(seeds).astype(np.float32)


def one_hot_matrix(size, target):
    rows = lax.broadcasted_iota(jnp.int32, (size, size), 0)
    cols = lax.broadcasted_iota(jnp.int32, (size, size), 1)
    return jnp.where(target(rows) == cols, 1.0, 0.0).astype(BF16)


def interleave(size):
    part = size // 4
    return one_hot_matrix(
        size,
        lambda r: jnp.where(r < part, 4 * r, jnp.where(r < 2 * part, 4 * r - size + 2, 2 * r - size + 1)),
    )


def pieces(waves, i, size):
    part, quarter = size // 4, waves // 4
    yield i * part, part
    yield quarter + i * part, part
    yield 2 * quarter + 2 * i * part, 2 * part


def place(halves):
    w = lax.axis_index("pw")
    return lax.rem(w, halves), lax.div(w, halves)


def dot(a, b):
    return jnp.dot(a, b, preferred_element_type=F32)


def dot_nt(a, b):
    return lax.dot_general(a, b, (((1,), (1,)), ((), ())), preferred_element_type=F32)


def gather_kernel(requests, orbitals, vectors, out, held, load, store, *, halves):
    count, slots, rows = out.shape[:3]
    chunk = orbitals.shape[2]
    spots = [(i // slots, i % slots) for i in range(count * slots)]
    loads = [
        pltpu.make_async_copy(
            orbitals.at[requests[slot, i]], held.at[i, slot, :, pl.ds(0, chunk)], load.at[i, slot]
        )
        for i, slot in spots
    ]
    for copy in loads:
        copy.start()
    x = place(halves)[1]
    for i, slot in spots:
        block = vectors[requests[slot, i]]
        held[i, slot, :, chunk:] = jnp.where(x == 0, block[:rows], block[rows:])
    stores = []
    for copy, (i, slot) in zip(loads, spots):
        copy.wait()
        if slot == slots - 1:
            stores.append(pltpu.make_async_copy(held.at[i], out.at[i], store.at[i]))
            stores[-1].start()
    for copy in stores:
        copy.wait()


def transform_kernel(*refs, halves, slot):
    parts = refs[:halves]
    seeds, vec = refs[halves : halves + 2]
    refs = refs[halves + 2 :]
    if slot == 1:
        far_screened, rho, natural_out, screened = refs[:4]
        copy = pltpu.make_async_copy(far_screened, screened, refs[-1])
        copy.start()
        refs = refs[:-1]
    else:
        rho, p_own, p_msg = refs[:3]
    evens, odds, table, acc = refs[-4:]
    x = place(halves)[1]
    chunk = parts[0].shape[2]
    block = evens.shape[3]
    waves = acc.shape[1]
    half, quarter = waves // 2, waves // 4
    flip = one_hot_matrix(256, lambda r: 255 - r)
    per_chunk = chunk // block
    bands = parts[0].shape[1]
    coarse = seeds.shape[1] - FINE
    rows = chunk // FINE
    for t in range(halves // 2 * per_chunk):
        s, b = t // per_chunk, t % per_chunk
        now = t % 2
        end = chunk - b * block
        near, back = [], []
        for c in range(2):
            mirror = parts[s ^ (halves - 1)]
            back.append(
                jnp.concatenate(
                    [
                        dot(mirror[1 - c, :, end - 256 * (i + 1) : end - 256 * i], flip)
                        for i in range(block // 256)
                    ],
                    axis=1,
                )
            )
            near.append(parts[s][c, :, b * block : (b + 1) * block].astype(F32))
        for v in range(NV):
            to = slice(v * NC, (v + 1) * NC)
            even = []
            for c in range(2):
                here = near[c][v : v + 1] * near[c][NV:bands]
                there = back[c][v : v + 1] * back[c][NV:bands]
                even.append(here + there)
                odds[now, to, c * block : (c + 1) * block] = (here - there).astype(BF16)
            evens[now, 0, to, :] = (even[0] + even[1]).astype(BF16)
            evens[now, 1, to, :] = (even[0] - even[1]).astype(BF16)
        for c in range(2):
            cols = slice(0, waves) if c == 0 else slice(half, waves)
            cb, sb = seeds[0, coarse:, cols], seeds[1, coarse:, cols]
            for a in range(block // FINE):
                row = (s * 2 + c) * rows + b * (block // FINE) + a
                table[now, c * block + a * FINE : c * block + (a + 1) * FINE, cols] = (
                    seeds[0, row : row + 1, cols] * cb - seeds[1, row : row + 1, cols] * sb
                ).astype(BF16)
        terms = (
            dot(evens[now, 0], table[now, :block, :quarter]),
            dot(evens[now, 1], table[now, :block, quarter:half]),
            dot(odds[now], table[now, :, half:]),
        )
        for cols, term in zip((slice(0, quarter), slice(quarter, half), slice(half, waves)), terms):
            if t == 0:
                acc[:, cols] = term
            else:
                acc[:, cols] += term
    done = acc[...].astype(BF16)
    rho[...] = done
    size = min(512, waves)
    order = interleave(size)
    proj = dot(vec[...], done).astype(BF16)
    natural = jnp.concatenate(
        [
            dot(
                jnp.concatenate([proj[:, o : o + n] for o, n in pieces(waves, i, size)], axis=1),
                order,
            ).astype(BF16)
            for i in range(waves // size)
        ],
        axis=1,
    )
    if slot == 1:
        natural_out[...] = natural
        copy.wait()
    else:
        width = p_own.shape[1]
        first, second = natural[:, :width], natural[:, width:]
        p_own[...] = jnp.where(x == 0, first, second)
        p_msg[...] = jnp.where(x == 0, second, first)


def back_kernel(p_own, p_far, screened, q_keep, q_part, *q_msgs):
    shifts = len(q_msgs) + 1
    j, x = place(shifts)
    width = p_own.shape[1]
    for rel in range(2):
        pair = x if rel == 0 else 1 - x
        first = p_own[...] if rel == 0 else p_far[...]
        for s in range(shifts):
            for c in range(2):
                start = pl.multiple_of((c * shifts + (j ^ s)) * width, width)
                term = dot(first, screened[pair, :, pl.ds(start, width)])
                cols = slice(c * width, (c + 1) * width)
                if s == 0:
                    (q_part if rel else q_keep)[:, cols] = term
                else:
                    q_msgs[s - 1][rel, :, cols] = term.astype(BF16)


def left_kernel(*refs):
    sources, (screened, left_own, left_msg) = refs[:-3], refs[-3:]
    shifts = len(sources) // 2
    j, x = place(shifts)
    width = left_own.shape[1]
    for rel in range(2):
        pair = x if rel == 0 else 1 - x
        total = None
        for s in range(shifts):
            source = sources[rel * shifts + s]
            for c in range(2):
                start = pl.multiple_of((c * shifts + (j ^ s)) * width, width)
                term = dot_nt(
                    source[:, c * width : (c + 1) * width], screened[pair, :, pl.ds(start, width)]
                )
                total = term if total is None else total + term
        (left_msg if rel else left_own)[...] = total.astype(BF16)


def apply_weight(weight, rho, scratch, outs):
    shifts = len(outs)
    j = place(shifts)[0]
    waves = rho.shape[1]
    size = min(512, waves)
    order = interleave(size)
    parts = [
        dot_nt(weight[:, size * i : size * (i + 1)], order).astype(BF16)
        for i in range(waves // size)
    ]
    cuts = (0, size // 4, size // 2, size)
    sorted_weight = jnp.concatenate(
        [p[:, lo:hi] for lo, hi in zip(cuts, cuts[1:]) for p in parts], axis=1
    )
    scratch[...] = dot_nt(sorted_weight, rho[...]).reshape(scratch.shape)
    for s in range(shifts):
        for c in range(2):
            outs[s][c] = scratch[c * shifts + (j ^ s)].astype(outs[s].dtype)


def apply_second_kernel(q_keep, q_far, *refs):
    shifts = (len(refs) - 1) // 2
    received, rho = refs[: shifts - 1], refs[shifts - 1]
    outs, scratch = refs[shifts:-1], refs[-1]
    weight = q_keep[...] + q_far[...].astype(F32)
    for part in received:
        weight = weight + part[0].astype(F32)
    apply_weight(weight.astype(BF16), rho, scratch, outs)


def apply_first_kernel(left_own, left_far, rho, *refs):
    shifts = (len(refs) - 1) // 2
    others, outs, scratch = refs[:shifts], refs[shifts:-1], refs[-1]
    x = place(shifts)[1]
    mine, other = left_own[...], left_far[...]
    weight = jnp.concatenate(
        [jnp.where(x == 0, mine, other), jnp.where(x == 0, other, mine)], axis=1
    )
    apply_weight(weight, rho, scratch, [out.at[0] for out in outs])
    for out, second in zip(outs, others):
        out[1] = second[...]


def send_kernel(pairs, own, *refs, groups, halves):
    received, out = refs[:-1], refs[-1]
    slots, parts = own.shape[:2]
    x = place(halves)[1]
    index = lax.axis_index("pairs") * parts + x
    owned = out.shape[1]
    total = own[...]
    for part in received:
        total = total + part[...].astype(F32)
    for k in range(groups * owned):
        for part in range(parts):
            value = jnp.zeros(own.shape[2:], F32)
            for slot in range(slots):
                value = value + jnp.where(pairs[slot, index] == k, total[slot, part], 0.0)
            out[k // owned * parts + part, k % owned] = value.astype(BF16)


def local(orbitals, vectors, screened, pair_list, band_order):
    groups = lax.axis_size("pairs")
    columns = lax.axis_size("pw")
    pairs_here = screened.shape[0]
    halves = columns // pairs_here
    both = ("pairs", "pw")
    w = lax.axis_index("pw")
    k_count, band_here, chunk = orbitals.shape
    points = chunk * columns
    waves = screened.shape[2]
    width = waves // columns
    own_waves = width * pairs_here
    transitions = vectors.shape[2]
    vec_count = vectors.shape[1] * groups
    vec_part = vectors.shape[1] // pairs_here
    bands = band_here * groups
    members = [
        [gg * columns + xx * halves + jj for gg in range(groups) for xx in range(pairs_here)]
        for jj in range(halves)
    ]

    def exchange(value):
        return lax.all_to_all(value, both, 0, 0, tiled=True, axis_index_groups=members)

    def shift(value, s):
        return lax.ppermute(value, "pw", [(i, i ^ s) for i in range(columns)])

    def call(kernel, outs, *args, flops=0, scratch=(), limit=4, far=0):
        moved = sum(math.prod(v.shape) * v.dtype.itemsize for v in (*args, *outs))
        return pl.pallas_call(
            kernel,
            in_specs=[vmem] * (len(args) - far) + [hbm] * far,
            out_specs=[vmem] * len(outs),
            out_shape=list(outs),
            scratch_shapes=list(scratch),
            compiler_params=pltpu.CompilerParams(vmem_limit_bytes=limit * 2**20),
            cost_estimate=pl.CostEstimate(flops=flops, bytes_accessed=moved, transcendentals=0),
        )(*args)

    smem = pl.BlockSpec(memory_space=pltpu.SMEM)
    vmem = pl.BlockSpec(memory_space=pltpu.VMEM)
    hbm = pl.BlockSpec(memory_space=pltpu.HBM)
    like = jax.ShapeDtypeStruct

    slots = 2 * groups * pairs_here
    sent = pl.pallas_call(
        functools.partial(gather_kernel, halves=halves),
        in_specs=[smem, hbm, vmem],
        out_specs=hbm,
        out_shape=like((slots // 2, 2, band_here, chunk + transitions), BF16),
        scratch_shapes=[
            pltpu.VMEM((slots // 2, 2, band_here, chunk + transitions), BF16),
            pltpu.SemaphoreType.DMA((slots // 2, 2)),
            pltpu.SemaphoreType.DMA((slots // 2,)),
        ],
        compiler_params=pltpu.CompilerParams(vmem_limit_bytes=60 * 2**20),
    )(pair_list.T, orbitals, vectors)
    got = exchange(sent).reshape(groups, pairs_here, 2, band_here, chunk + transitions)
    seeds = lax.dynamic_index_in_dim(
        jnp.asarray(phase_tables(points, waves, halves, columns)), w % halves, keepdims=False
    )
    vec = got[..., chunk:].transpose(2, 0, 1, 3, 4).reshape(2, vec_count, transitions)
    picker = (band_order[:, None] == jnp.arange(bands, dtype=jnp.int32)[None, :]).astype(BF16)
    picker, seeds = lax.optimization_barrier((picker, seeds))
    psi = jnp.einsum(
        "gbn,gxlbr->lxnr",
        picker.reshape(groups, band_here, bands),
        got[..., :chunk],
        preferred_element_type=F32,
    ).astype(BF16)
    products = NV * NC
    block = min(1024, chunk)

    def transform(slot, outs, *far):
        parts = [psi[slot]] + [shift(psi[slot], s) for s in range(1, halves)]
        return call(
            functools.partial(transform_kernel, halves=halves, slot=slot),
            [like((products, own_waves), BF16)] + outs,
            *parts,
            seeds,
            vec[slot],
            *far,
            flops=products * points * own_waves,
            scratch=[
                pltpu.VMEM((2, 2, products, block), BF16),
                pltpu.VMEM((2, products, 2 * block), BF16),
                pltpu.VMEM((2, 2 * block, own_waves), BF16),
                pltpu.VMEM((products, own_waves), F32),
            ]
            + [pltpu.SemaphoreType.DMA] * len(far),
            limit=24,
            far=len(far),
        )

    shape = like((vec_count, width), BF16)
    full = like((vec_count, own_waves), BF16)
    rho_first, p_own, p_msg = transform(0, [shape, shape])
    rho_second, p_second, screened = transform(1, [full, like(screened.shape, BF16)], screened)
    p_far = shift(p_msg, halves)
    p_own, p_second = lax.optimization_barrier((p_own, p_second))
    far = shift(p_second, halves)
    near = [shift(p_second, s) for s in range(1, halves)]
    fars = [shift(far, s) for s in range(1, halves)]
    flops = 4 * vec_count * width * waves
    partial_q = like((vec_count, own_waves), F32)
    q_keep, q_part, *q_msgs = call(
        back_kernel,
        [partial_q] * 2 + [like((2, vec_count, own_waves), BF16)] * (halves - 1),
        p_own,
        p_far,
        screened,
        flops=flops,
    )
    received = [shift(q_msgs[s - 1], s) for s in range(1, halves)]
    q_send = (q_part + sum(v[1].astype(F32) for v in received)).astype(BF16)
    q_far = shift(q_send, halves)
    left_own, left_msg = call(
        left_kernel, [shape, shape], p_second, *near, far, *fars, screened, flops=flops
    )
    left_far = shift(left_msg, halves)

    vec_rows = vec_count // columns
    terms = like((pairs_here, vec_rows, transitions), F32)
    flops = 2 * vec_count * products * own_waves
    scratch = [pltpu.VMEM((columns, vec_rows, transitions), F32)]
    seconds = call(
        apply_second_kernel,
        [terms] + [like(terms.shape, BF16)] * (halves - 1),
        q_keep,
        q_far,
        *received,
        rho_second,
        flops=flops,
        scratch=scratch,
    )
    out_own, *out_msgs = call(
        apply_first_kernel,
        [like((2, *v.shape), v.dtype) for v in seconds],
        left_own,
        left_far,
        rho_first,
        *seconds,
        flops=flops,
        scratch=scratch,
    )
    received = [shift(out_msgs[s - 1], s) for s in range(1, halves)]
    placed = pl.pallas_call(
        functools.partial(send_kernel, groups=groups, halves=halves),
        in_specs=[smem] + [vmem] * halves,
        out_specs=vmem,
        out_shape=like(
            (groups * pairs_here, k_count // groups, vec_rows, transitions), BF16
        ),
        compiler_params=pltpu.CompilerParams(vmem_limit_bytes=4 * 2**20),
    )(pair_list.T, out_own, *received)
    return jnp.sum(exchange(placed).astype(F32), axis=0)


def solution(mesh):
    in_specs = (P(None, "pairs", "pw"), P(None, "pairs", None), P("pairs", "pw", None), P(), P())
    out_specs = P("pairs", "pw", None)
    return jax.shard_map(local, mesh=mesh, in_specs=in_specs, out_specs=out_specs, check_vma=False)
```

time: 121 us -> 92.6 us (0.77)
  local copies, waits for them, and re-layouts: 22.4 us -> 3.56 us
  Pallas kernels: 31 us -> 23.2 us
  other arithmetic: 2.21 us -> 0.75 us
    unnamed x25 -> x8, local copies, waits for them, and re-layouts: 19.4 us -> 0.5 us
    pallas_call x7 -> x8, Pallas kernels: 31 us -> 23.2 us  [the longest x6 19.1 us: call(): pl.pallas_call(kernel, in_specs=[vmem] * (len(args) - far) + [hbm] * far,...]
    squeeze x1, local copies, waits for them, and re-layouts: 0.02 us -> 1.52 us  [local(): lax.dynamic_index_in_dim(jnp.asarray(phase_tables(points, waves, halves,...]
    all_to_all x1, waiting for transfers between devices: 25.6 us -> 24.1 us  [exchange(): lax.all_to_all(value, both, 0, 0, tiled=True, axis_index_groups=members)]
    eq x2 -> x0, other arithmetic: 1.27 us -> none  [local(): mine[slot] == owners]
  transfers between devices with their start and end apart: 11 -> 11, of which waited for: 5 -> 6; matrix products, arithmetic and copies ran while one was open for 3% -> 3% of each run, Pallas kernels for 22% -> 19%
where the time goes in v3:
time: 92.6 us; the launch traced here: 92.1 us
  waiting for transfers between devices  32.5 us (35%)
  Pallas kernels  23.2 us (25%)
  blocking collectives  16.8 us (18%)
  starting transfers between devices  14.2 us (15%)
  local copies, waits for them, and re-layouts  3.56 us (4%)
    all_to_all x1, waiting for transfers between devices, exchange(): lax.all_to_all(value, both, 0, 0, tiled=True, axis_index_groups=members)  24.1 us
    pallas_call x6, Pallas kernels, call(): pl.pallas_call(kernel, in_specs=[vmem] * (len(args) - far) + [hbm] * far,...  19.1 us
    all_to_all x1, blocking collectives, exchange(): lax.all_to_all(value, both, 0, 0, tiled=True, axis_index_groups=members)  16.8 us
    ppermute x10, waiting for transfers between devices, shift(): return lax.ppermute(value, 'pw', [(i, i ^ s) for i in range(columns)])  8.42 us
    all_to_all x1, starting transfers between devices, exchange(): lax.all_to_all(value, both, 0, 0, tiled=True, axis_index_groups=members)  8.32 us
    ppermute x10, starting transfers between devices, shift(): return lax.ppermute(value, 'pw', [(i, i ^ s) for i in range(columns)])  5.87 us
    pallas_call x1, Pallas kernels, local(): pl.pallas_call(functools.partial(gather_kernel, halves=halves), in_specs=...  3.52 us
  transfers between devices with their start and end apart: 11, of which 6 were waited for; matrix products, arithmetic and copies ran while one was open for 3% of the time, Pallas kernels for 19%

profile of v3, /device:TPU:0, one launch (start us, length us, event | category | flops | bytes accessed | tf_op | source)
XLA Modules:
  0.0 92.1 jit_solution(16624179149007203033)
XLA Ops:
  0.0 3.5 %shard_map.64 = bf16[16,2,4,4352]{3,2,1,0:T(4,128)(2,1)} custom-call(s32[2,16]{1,0:T(2,128)} %bitcast.27, bf16[16,4,4096]{2,1,0:T(4,128)(2,1)} %orbitals.1, bf16[16,8,256]{2,1,0:T(8,128)(2,1)} %vectors.1), custom_call_target="tpu_custom_call" | custom-call | tf_op jit(solution)/shard_map/pallas_call | solution.py:345
  3.5 8.3 %all-to-all-start = ((bf16[16,2,4,4352]{3,2,1,0:T(4,128)(2,1)}), bf16[16,2,4,4352]{3,2,1,0:T(4,128)(2,1)S(1)}, u32[]{:S(2)}, u32[]{:S(2)}) async-start(bf16[16,2,4,4352]{3,2,1,0:T(4,128)(2,1)} %shard_map.64), calls=%async_computation | async-start | bytes 2228224 | tf_op jit(solution)/shard_map/all_to_all | solution.py:322
  11.9 0.0 copy-start.3
  11.9 1.5 %dynamic-slice_bitcast_fusion.refs_2_ = f32[2,192,1024]{2,1,0:T(8,128)S(1)} fusion(f32[2,2,192,1024]{3,2,1,0:T(8,128)} %constant.25.clone, s32[]{:T(128)S(6)} %select_n.12), kind=kLoop, calls=%fused_computation.3 | loop fusion | bytes 3145732 | tf_op jit(solution)/shard_map/jit(dynamic_index_in_dim)/squeeze | solution.py:358
  13.4 0.0 copy-done.3
  13.4 0.1 fusion.4
  13.5 24.1 %all-to-all-done = bf16[16,2,4,4352]{3,2,1,0:T(4,128)(2,1)S(1)} async-done(((bf16[16,2,4,4352]{3,2,1,0:T(4,128)(2,1)}), bf16[16,2,4,4352]{3,2,1,0:T(4,128)(2,1)S(1)}, u32[]{:S(2)}, u32[]{:S(2)}) %all-to-all-start) | async-done | bytes 1114144 | tf_op jit(solution)/shard_map/all_to_all | solution.py:322
  37.6 0.0 copy-start.2
  37.6 0.5 slice.32
  38.1 0.5 copy-done.2
  38.6 0.8 fusion.1
  39.4 0.1 slice_bitcast_fusion
  39.5 0.1 collective-permute-start
  39.6 0.5 collective-permute-start.1
  40.1 0.9 copy_bitcast_fusion
  41.0 0.0 copy-start.1
  41.0 0.6 collective-permute-done.refs_1_
  41.6 8.1 %shard_map.65 = (bf16[256,1024]{1,0:T(8,128)(2,1)S(1)}, bf16[64,512]{1,0:T(8,128)(2,1)S(1)}, bf16[64,512]{1,0:T(8,128)(2,1)S(1)}) custom-call(bf16[2,32,4096]{2,1,0:T(8,128)(2,1)S(1)} %get-tuple-element.44.refs_0_, bf16[2,32,4096]{2,1,0:T(8,128)(2,1)} %collective-permute-done.refs_1_, f32[2,192,1024]{2,1,0:T(8,128)S(1)} %dynamic-slice_bitcast_fusion.refs_2_, ...), custom_call_target="tpu_custom_call" | custom-call | flops 4294967296 | bytes 3309568 | tf_op jit(solution)/shard_map/pallas_call | solution.py:329
  49.7 0.6 collective-permute-start.6
  50.4 0.0 collective-permute-done.1.refs_1_
  50.4 0.0 copy-done.1
  50.4 7.3 %shard_map.66 = (bf16[256,1024]{1,0:T(8,128)(2,1)S(1)}, bf16[64,1024]{1,0:T(8,128)(2,1)S(1)}, bf16[2,512,2048]{2,1,0:T(8,128)(2,1)S(1)}) custom-call(bf16[2,32,4096]{2,1,0:T(8,128)(2,1)S(1)} %get-tuple-element.43.refs_0_, bf16[2,32,4096]{2,1,0:T(8,128)(2,1)S(1)} %collective-permute-done.1.refs_1_, f32[2,192,1024]{2,1,0:T(8,128)S(1)} %dynamic-slice_bitcast_fusion.refs_2_, ...), custom_call_target="tpu_custom_call" | custom-call | flops 4294967296 | bytes 11698176 | tf_op jit(solution)/shard_map/pallas_call | solution.py:329
  57.6 0.0 collective-permute-done.6.p_far
  57.7 0.9 shard_map.68
  58.5 0.1 collective-permute-start.7
  58.6 1.5 %collective-permute-start.3 = (bf16[64,1024]{1,0:T(8,128)(2,1)S(1)}, bf16[64,1024]{1,0:T(8,128)(2,1)S(1)}, u32[]{:S(2)}, u32[]{:S(2)}) collective-permute-start(bf16[64,1024]{1,0:T(8,128)(2,1)S(1)} %get-tuple-element.28.refs_0_), channel_id=1, source_target_pairs={{0,2},{1,3},{2,0},{3,1},{4,6},{5,7},{6,4},{7,5},{8,10},{9,11},{10,... | collective-permute-start | bytes 393224 | tf_op jit(solution)/shard_map/ppermute | solution.py:325
  60.1 0.2 collective-permute-start.2
  60.3 4.2 %collective-permute-done.3.refs_2_ = bf16[64,1024]{1,0:T(8,128)(2,1)S(1)} collective-permute-done((bf16[64,1024]{1,0:T(8,128)(2,1)S(1)}, bf16[64,1024]{1,0:T(8,128)(2,1)S(1)}, u32[]{:S(2)}, u32[]{:S(2)}) %collective-permute-start.3) | collective-permute-done | bytes 131104 | tf_op jit(solution)/shard_map/ppermute | solution.py:325
  64.5 0.0 collective-permute-start.4
  64.5 0.0 collective-permute-done.7.refs_0_
  64.5 1.5 %collective-permute-start.8 = (bf16[64,1024]{1,0:T(8,128)(2,1)S(1)}, bf16[64,1024]{1,0:T(8,128)(2,1)S(1)}, u32[]{:S(2)}, u32[]{:S(2)}) collective-permute-start(bf16[64,1024]{1,0:T(8,128)(2,1)S(1)} %fusion.3), channel_id=1, source_target_pairs={{0,2},{1,3},{2,0},{3,1},{4,6},{5,7},{6,4},{7,5},{8,10},{9,11},{10,... | collective-permute-start | bytes 393224 | tf_op jit(solution)/shard_map/ppermute | solution.py:325
  66.1 0.0 collective-permute-done.2.refs_1_
  66.1 0.0 collective-permute-done.4.refs_3_
  66.1 1.4 %shard_map.67 = (bf16[64,512]{1,0:T(8,128)(2,1)S(1)}, bf16[64,512]{1,0:T(8,128)(2,1)S(1)}) custom-call(bf16[64,1024]{1,0:T(8,128)(2,1)S(1)} %get-tuple-element.28.refs_0_, bf16[64,1024]{1,0:T(8,128)(2,1)S(1)} %collective-permute-done.2.refs_1_, bf16[64,1024]{1,0:T(8,128)(2,1)S(1)} %collective-permute-done.3.refs_2_, ...), custom_call_target="tpu_custom_call" | custom-call | flops 268435456 | bytes 4849664 | tf_op jit(solution)/shard_map/pallas_call | solution.py:329
  67.5 0.0 copy-start
  67.5 1.3 %collective-permute-start.5 = (bf16[64,512]{1,0:T(8,128)(2,1)S(1)}, bf16[64,512]{1,0:T(8,128)(2,1)S(1)}, u32[]{:S(2)}, u32[]{:S(2)}) collective-permute-start(bf16[64,512]{1,0:T(8,128)(2,1)S(1)} %get-tuple-element.31), channel_id=1, source_target_pairs={{0,2},{1,3},{2,0},{3,1},{4,6},{5,7},{6,4},{7,5},{8,10},{9,11},{10,... | collective-permute-start | bytes 196616 | tf_op jit(solution)/shard_map/ppermute | solution.py:325
  68.8 1.8 %collective-permute-done.8.q_far = bf16[64,1024]{1,0:T(8,128)(2,1)S(1)} collective-permute-done((bf16[64,1024]{1,0:T(8,128)(2,1)S(1)}, bf16[64,1024]{1,0:T(8,128)(2,1)S(1)}, u32[]{:S(2)}, u32[]{:S(2)}) %collective-permute-start.8) | collective-permute-done | bytes 131104 | tf_op jit(solution)/shard_map/ppermute | solution.py:325
  70.6 0.7 shard_map.69
  71.3 0.6 collective-permute-done.5.left_far
  71.9 0.7 shard_map.70
  72.6 0.1 collective-permute-start.9
  72.7 1.2 %collective-permute-done.9.refs_0_ = bf16[2,2,16,256]{3,2,1,0:T(8,128)(2,1)S(1)} collective-permute-done((bf16[2,2,16,256]{3,2,1,0:T(8,128)(2,1)S(1)}, bf16[2,2,16,256]{3,2,1,0:T(8,128)(2,1)S(1)}, u32[]{:S(2)}, u32[]{:S(2)}) %collective-permute-start.9) | collective-permute-done | bytes 32800 | tf_op jit(solution)/shard_map/ppermute | solution.py:325
  73.9 0.0 copy-done
  73.9 0.6 shard_map.71
  74.6 16.8 %all_to_all.10 = bf16[16,2,16,256]{3,2,1,0:T(8,128)(2,1)S(1)} all-to-all(bf16[16,2,16,256]{3,2,1,0:T(8,128)(2,1)S(1)} %shard_map.71), channel_id=1, replica_groups={{0,2,4,6,8,10,12,14,16,18,20,22,24,26,28,30},{1,3,5,7,9,11,13,15,17,19,..., dimensions={0} | all-to-all | bytes 524288 | tf_op jit(solution)/shard_map/all_to_all | solution.py:322
  91.4 0.7 convert_reduce_fusion
  (4 shorter events, 0.1 us)
Async XLA Ops:
  3.5 34.1 %all-to-all-start = ((bf16[16,2,4,4352]{3,2,1,0:T(4,128)(2,1)}), bf16[16,2,4,4352]{3,2,1,0:T(4,128)(2,1)S(1)}, u32[]{:S(2)}, u32[]{:S(2)}) async-start(bf16[16,2,4,4352]{3,2,1,0:T(4,128)(2,1)} %shard_map.64), calls=%async_computation | async-start | bytes 2228224 | tf_op jit(solution)/shard_map/all_to_all | solution.py:322
  11.9 1.5 %copy-start.3 = (s32[32]{0:T(128)S(1)}, s32[32]{0:T(128)}, u32[]{:S(2)}) copy-start(s32[32]{0:T(128)} %param.10) | copy-start | bytes 388
  37.6 1.0 %copy-start.2 = (bf16[16,2,4,4352]{3,2,1,0:T(4,128)(2,1)}, bf16[16,2,4,4352]{3,2,1,0:T(4,128)(2,1)S(1)}, u32[]{:S(2)}) copy-start(bf16[16,2,4,4352]{3,2,1,0:T(4,128)(2,1)S(1)} %all-to-all-done) | copy-start | bytes 3342340
  39.5 2.1 %collective-permute-start = (bf16[2,32,4096]{2,1,0:T(8,128)(2,1)S(1)}, bf16[2,32,4096]{2,1,0:T(8,128)(2,1)}, u32[]{:S(2)}, u32[]{:S(2)}) collective-permute-start(bf16[2,32,4096]{2,1,0:T(8,128)(2,1)S(1)} %get-tuple-element.44.refs_0_), channel_id=1, source_target_pairs={{0,1},{1,0},{2,3},{3,2},{4,5},{5,4},{6,7},{7,6},{8,9},{9,8},{10,11... | collective-permute-start | bytes 1572872 | tf_op jit(solution)/shard_map/ppermute | solution.py:325
  39.6 10.8 %collective-permute-start.1 = (bf16[2,32,4096]{2,1,0:T(8,128)(2,1)S(1)}, bf16[2,32,4096]{2,1,0:T(8,128)(2,1)S(1)}, u32[]{:S(2)}, u32[]{:S(2)}) collective-permute-start(bf16[2,32,4096]{2,1,0:T(8,128)(2,1)S(1)} %get-tuple-element.43.refs_0_), channel_id=1, source_target_pairs={{0,1},{1,0},{2,3},{3,2},{4,5},{5,4},{6,7},{7,6},{8,9},{9,8},{10,11... | collective-permute-start | bytes 1572872 | tf_op jit(solution)/shard_map/ppermute | solution.py:325
  41.0 9.4 %copy-start.1 = (bf16[2,512,2048]{2,1,0:T(8,128)(2,1)S(1)}, bf16[2,512,2048]{2,1,0:T(8,128)(2,1)}, u32[]{:S(2)}) copy-start(bf16[2,512,2048]{2,1,0:T(8,128)(2,1)} %refs_4_.1) | copy-start | bytes 12582916
  49.7 7.9 %collective-permute-start.6 = (bf16[64,512]{1,0:T(8,128)(2,1)S(1)}, bf16[64,512]{1,0:T(8,128)(2,1)S(1)}, u32[]{:S(2)}, u32[]{:S(2)}) collective-permute-start(bf16[64,512]{1,0:T(8,128)(2,1)S(1)} %get-tuple-element.34), channel_id=1, source_target_pairs={{0,2},{1,3},{2,0},{3,1},{4,6},{5,7},{6,4},{7,5},{8,10},{9,11},{10,... | collective-permute-start | bytes 196616 | tf_op jit(solution)/shard_map/ppermute | solution.py:325
  58.5 6.0 %collective-permute-start.7 = (bf16[2,64,1024]{2,1,0:T(8,128)(2,1)S(1)}, bf16[2,64,1024]{2,1,0:T(8,128)(2,1)S(1)}, u32[]{:S(2)}, u32[]{:S(2)}) collective-permute-start(bf16[2,64,1024]{2,1,0:T(8,128)(2,1)S(1)} %get-tuple-element.37), channel_id=1, source_target_pairs={{0,1},{1,0},{2,3},{3,2},{4,5},{5,4},{6,7},{7,6},{8,9},{9,8},{10,11... | collective-permute-start | bytes 786440 | tf_op jit(solution)/shard_map/ppermute | solution.py:325
  58.6 5.9 %collective-permute-start.3 = (bf16[64,1024]{1,0:T(8,128)(2,1)S(1)}, bf16[64,1024]{1,0:T(8,128)(2,1)S(1)}, u32[]{:S(2)}, u32[]{:S(2)}) collective-permute-start(bf16[64,1024]{1,0:T(8,128)(2,1)S(1)} %get-tuple-element.28.refs_0_), channel_id=1, source_target_pairs={{0,2},{1,3},{2,0},{3,1},{4,6},{5,7},{6,4},{7,5},{8,10},{9,11},{10,... | collective-permute-start | bytes 393224 | tf_op jit(solution)/shard_map/ppermute | solution.py:325
  60.1 6.0 %collective-permute-start.2 = (bf16[64,1024]{1,0:T(8,128)(2,1)S(1)}, bf16[64,1024]{1,0:T(8,128)(2,1)S(1)}, u32[]{:S(2)}, u32[]{:S(2)}) collective-permute-start(bf16[64,1024]{1,0:T(8,128)(2,1)S(1)} %get-tuple-element.28.refs_0_), channel_id=1, source_target_pairs={{0,1},{1,0},{2,3},{3,2},{4,5},{5,4},{6,7},{7,6},{8,9},{9,8},{10,11... | collective-permute-start | bytes 393224 | tf_op jit(solution)/shard_map/ppermute | solution.py:325
  64.5 1.6 %collective-permute-start.4 = (bf16[64,1024]{1,0:T(8,128)(2,1)S(1)}, bf16[64,1024]{1,0:T(8,128)(2,1)S(1)}, u32[]{:S(2)}, u32[]{:S(2)}) collective-permute-start(bf16[64,1024]{1,0:T(8,128)(2,1)S(1)} %collective-permute-done.3.refs_2_), channel_id=1, source_target_pairs={{0,1},{1,0},{2,3},{3,2},{4,5},{5,4},{6,7},{7,6},{8,9},{9,8},{10,11... | collective-permute-start | bytes 393224 | tf_op jit(solution)/shard_map/ppermute | solution.py:325
  64.5 6.0 %collective-permute-start.8 = (bf16[64,1024]{1,0:T(8,128)(2,1)S(1)}, bf16[64,1024]{1,0:T(8,128)(2,1)S(1)}, u32[]{:S(2)}, u32[]{:S(2)}) collective-permute-start(bf16[64,1024]{1,0:T(8,128)(2,1)S(1)} %fusion.3), channel_id=1, source_target_pairs={{0,2},{1,3},{2,0},{3,1},{4,6},{5,7},{6,4},{7,5},{8,10},{9,11},{10,... | collective-permute-start | bytes 393224 | tf_op jit(solution)/shard_map/ppermute | solution.py:325
  67.5 6.4 %copy-start = (s32[16,2]{0,1:T(2,128)S(1)}, s32[16,2]{0,1:T(2,128)}, u32[]{:S(2)}) copy-start(s32[16,2]{0,1:T(2,128)} %param.9) | copy-start | bytes 388
  67.5 4.4 %collective-permute-start.5 = (bf16[64,512]{1,0:T(8,128)(2,1)S(1)}, bf16[64,512]{1,0:T(8,128)(2,1)S(1)}, u32[]{:S(2)}, u32[]{:S(2)}) collective-permute-start(bf16[64,512]{1,0:T(8,128)(2,1)S(1)} %get-tuple-element.31), channel_id=1, source_target_pairs={{0,2},{1,3},{2,0},{3,1},{4,6},{5,7},{6,4},{7,5},{8,10},{9,11},{10,... | collective-permute-start | bytes 196616 | tf_op jit(solution)/shard_map/ppermute | solution.py:325
  72.6 1.3 %collective-permute-start.9 = (bf16[2,2,16,256]{3,2,1,0:T(8,128)(2,1)S(1)}, bf16[2,2,16,256]{3,2,1,0:T(8,128)(2,1)S(1)}, u32[]{:S(2)}, u32[]{:S(2)}) collective-permute-start(bf16[2,2,16,256]{3,2,1,0:T(8,128)(2,1)S(1)} %get-tuple-element.42), channel_id=1, source_target_pairs={{0,1},{1,0},{2,3},{3,2},{4,5},{5,4},{6,7},{7,6},{8,9},{9,8},{10,11... | collective-permute-start | bytes 98312 | tf_op jit(solution)/shard_map/ppermute | solution.py:325

commit v4 on v3

v4 whole, which is shorter than its diff:
```python
import functools
import math

import jax
import jax.numpy as jnp
import numpy as np
from jax import lax
from jax.experimental import pallas as pl
from jax.experimental.pallas import tpu as pltpu
from jax.sharding import PartitionSpec as P

NV = 16
NC = 16
FINE = 64
BF16 = jnp.bfloat16
F32 = jnp.float32


def column_order(size):
    return np.concatenate([np.arange(0, size, 4), np.arange(2, size, 4), np.arange(1, size, 2)])


def phase_tables(points, waves, halves, columns):
    width, chunk = waves // columns, points // columns
    period, turn = 4 * points, math.pi / (2 * points)
    scale = math.sqrt(2.0 / points)
    seeds = []
    for j in range(halves):
        own = np.concatenate(
            [np.arange(c * width, (c + 1) * width) for c in range(j, columns, halves)]
        )
        own = own[column_order(own.size)].astype(np.int64)
        starts = np.concatenate(
            [
                np.arange((c * halves + (j ^ s)) * chunk, (c * halves + (j ^ s) + 1) * chunk, FINE)
                for s in range(halves // 2)
                for c in range(columns // halves)
            ]
        )
        coarse = (2 * starts[:, None] * own) % period * turn
        fine = ((2 * np.arange(FINE) + 1)[:, None] * own) % period * turn
        seeds.append(
            [
                np.concatenate([np.cos(coarse) * scale, np.cos(fine)]),
                np.concatenate([np.sin(coarse) * scale, np.sin(fine)]),
            ]
        )
    return np.array(seeds).astype(np.float32)


def one_hot_matrix(size, target):
    rows = lax.broadcasted_iota(jnp.int32, (size, size), 0)
    cols = lax.broadcasted_iota(jnp.int32, (size, size), 1)
    return jnp.where(target(rows) == cols, 1.0, 0.0).astype(BF16)


def interleave(size):
    part = size // 4
    return one_hot_matrix(
        size,
        lambda r: jnp.where(r < part, 4 * r, jnp.where(r < 2 * part, 4 * r - size + 2, 2 * r - size + 1)),
    )


def pieces(waves, i, size):
    part, quarter = size // 4, waves // 4
    yield i * part, part
    yield quarter + i * part, part
    yield 2 * quarter + 2 * i * part, 2 * part


def place(halves):
    w = lax.axis_index("pw")
    return lax.rem(w, halves), lax.div(w, halves)


def dot(a, b):
    return jnp.dot(a, b, preferred_element_type=F32)


def dot_nt(a, b):
    return lax.dot_general(a, b, (((1,), (1,)), ((), ())), preferred_element_type=F32)


def gather_kernel(
    requests, orbitals, far_vectors, out, held, vectors, load, store, fetch, *, halves
):
    count, slots, rows = out.shape[:3]
    chunk = orbitals.shape[2]
    fetched = pltpu.make_async_copy(far_vectors, vectors, fetch)
    fetched.start()

    def load_of(i, slot):
        return pltpu.make_async_copy(
            orbitals.at[requests[slot, i]], held.at[i, slot, :, pl.ds(0, chunk)], load.at[i, slot]
        )

    def start(i, carry):
        for slot in range(slots):
            load_of(i, slot).start()
        return carry

    lax.fori_loop(0, count, start, 0)
    x = place(halves)[1]
    fetched.wait()

    def pick(i, carry):
        for slot in range(slots):
            block = vectors[requests[slot, i]]
            held[i, slot, :, chunk:] = jnp.where(x == 0, block[:rows], block[rows:])
        return carry

    lax.fori_loop(0, count, pick, 0)

    def send(i, carry):
        for slot in range(slots):
            load_of(i, slot).wait()
        pltpu.make_async_copy(held.at[i], out.at[i], store.at[i]).start()
        return carry

    lax.fori_loop(0, count, send, 0)

    def end(i, carry):
        pltpu.make_async_copy(held.at[i], out.at[i], store.at[i]).wait()
        return carry

    lax.fori_loop(0, count, end, 0)


def table_kernel(seeds, table, *, block, chunk):
    half = table.shape[1]
    coarse = seeds.shape[1] - FINE
    per_chunk, rows = chunk // block, block // FINE
    for c in range(2):
        cols = slice(0, 2 * half) if c == 0 else slice(half, 2 * half)
        cb, sb = seeds[0, coarse:, cols], seeds[1, coarse:, cols]
        for t in range(table.shape[0] // (3 * block)):
            s, b = t // per_chunk, t % per_chunk

            def step(a, carry):
                row = (s * 2 + c) * per_chunk * rows + b * rows + a
                ca, sa = seeds[0, pl.ds(row, 1), :], seeds[1, pl.ds(row, 1), :]
                fresh = (ca[:, cols] * cb - sa[:, cols] * sb).astype(BF16)
                to = pl.multiple_of(3 * t * block + a * FINE, FINE)
                if c == 0:
                    table[pl.ds(to, FINE), :] = fresh[:, :half]
                    fresh = fresh[:, half:]
                to = pl.multiple_of((3 * t + 1 + c) * block + a * FINE, FINE)
                table[pl.ds(to, FINE), :] = fresh
                return carry

            lax.fori_loop(0, rows, step, 0, unroll=2)


def transform_kernel(*refs, halves, slot):
    parts, vec = refs[:halves], refs[halves]
    refs = refs[halves + 1 :]
    table_copies = []
    if slot == 0:
        far_table, rho_own, rho_msg, p_own, p_msg, table, sem = *refs[:6], refs[-1]
        for t in range(sem.shape[0]):
            span = pl.ds(t * (table.shape[0] // sem.shape[0]), table.shape[0] // sem.shape[0])
            table_copies.append(pltpu.make_async_copy(far_table.at[span], table.at[span], sem.at[t]))
            table_copies[-1].start()
    else:
        table, far_screened, rho, natural_out, screened = refs[:5]
        copy = pltpu.make_async_copy(far_screened, screened, refs[-1])
        copy.start()
    refs = refs[:-1]
    evens, odds, acc = refs[-3:]
    x = place(halves)[1]
    chunk = parts[0].shape[2]
    block = evens.shape[3]
    waves = acc.shape[1]
    half, quarter = waves // 2, waves // 4
    flip = one_hot_matrix(256, lambda r: 255 - r)
    per_chunk = chunk // block
    bands = parts[0].shape[1]
    count = halves // 2 * per_chunk

    def produce(t):
        s, b = t // per_chunk, t % per_chunk
        now = t % 2
        end = chunk - b * block
        near, back = [], []
        for c in range(2):
            mirror = parts[s ^ (halves - 1)]
            back.append(
                jnp.concatenate(
                    [
                        dot(mirror[1 - c, :, end - 256 * (i + 1) : end - 256 * i], flip)
                        for i in range(block // 256)
                    ],
                    axis=1,
                )
            )
            near.append(parts[s][c, :, b * block : (b + 1) * block].astype(F32))
        for v in range(NV):
            to = slice(v * NC, (v + 1) * NC)
            even = []
            for c in range(2):
                here = near[c][v : v + 1] * near[c][NV:bands]
                there = back[c][v : v + 1] * back[c][NV:bands]
                even.append(here + there)
                odds[now, to, c * block : (c + 1) * block] = (here - there).astype(BF16)
            evens[now, 0, to, :] = (even[0] + even[1]).astype(BF16)
            evens[now, 1, to, :] = (even[0] - even[1]).astype(BF16)

    def consume(t):
        now = t % 2
        for table_copy in table_copies[t : t + 1]:
            table_copy.wait()
        first, second, third = 3 * t * block, (3 * t + 1) * block, (3 * t + 3) * block
        terms = (
            dot(evens[now, 0], table[first:second, :quarter]),
            dot(evens[now, 1], table[first:second, quarter:]),
            dot(odds[now], table[second:third, :]),
        )
        for cols, term in zip((slice(0, quarter), slice(quarter, half), slice(half, waves)), terms):
            if t == 0:
                acc[:, cols] = term
            else:
                acc[:, cols] += term

    produce(0)
    for t in range(count):
        if t + 1 < count:
            produce(t + 1)
        consume(t)
    done = acc[...].astype(BF16)
    width = waves // 2
    proj = dot(vec[...], done).astype(BF16)
    order = interleave(width)

    def chunk_of(array, i):
        return jnp.concatenate([array[:, o : o + n] for o, n in pieces(waves, i, width)], axis=1)

    natural = [dot(chunk_of(proj, i), order).astype(BF16) for i in range(2)]
    if slot == 1:
        rho[...] = done
        natural_out[...] = jnp.concatenate(natural, axis=1)
        copy.wait()
    else:
        both = [chunk_of(done, i) for i in range(2)]
        rho_own[...] = jnp.where(x == 0, both[0], both[1])
        rho_msg[...] = jnp.where(x == 0, both[1], both[0])
        p_own[...] = jnp.where(x == 0, natural[0], natural[1])
        p_msg[...] = jnp.where(x == 0, natural[1], natural[0])


def back_kernel(p_own, p_far, screened, q_keep, q_part, *q_msgs):
    shifts = len(q_msgs) // 2 + 1
    j, x = place(shifts)
    width = p_own.shape[1]
    for rel in range(2):
        pair = x if rel == 0 else 1 - x
        first = (p_far if rel else p_own)[...]
        for s in range(shifts):
            for c in range(2):
                start = pl.multiple_of((c * shifts + (j ^ s)) * width, width)
                term = dot(first, screened[pair, :, pl.ds(start, width)])
                cols = slice(c * width, (c + 1) * width)
                if s == 0:
                    (q_part if rel else q_keep)[:, cols] = term
                else:
                    q_msgs[2 * (s - 1) + rel][:, cols] = term.astype(BF16)


def cut(value, scratch, outs):
    shifts = len(outs)
    j = place(shifts)[0]
    scratch[...] = value.reshape(scratch.shape)
    for s in range(shifts):
        for c in range(2):
            outs[s][c] = scratch[c * shifts + (j ^ s)].astype(outs[s].dtype)


def forward_kernel(*refs, shifts):
    sources, refs = refs[: 2 * shifts], refs[2 * shifts :]
    rho_own, rho_far, screened = refs[:3]
    outs, scratch = refs[3:-1], refs[-1]
    j, x = place(shifts)
    width = rho_own.shape[1]
    order = interleave(width)
    for rel in range(2):
        pair = x if rel == 0 else 1 - x
        total = None
        for s in range(shifts):
            source = sources[rel * shifts + s]
            for c in range(2):
                start = pl.multiple_of((c * shifts + (j ^ s)) * width, width)
                term = dot_nt(
                    source[:, c * width : (c + 1) * width], screened[pair, :, pl.ds(start, width)]
                )
                total = term if total is None else total + term
        weight = dot_nt(total.astype(BF16), order).astype(BF16)
        products = (rho_far if rel else rho_own)[...]
        cut(dot_nt(weight, products), scratch.at[rel], [out.at[rel] for out in outs])


def second_kernel(q_keep, q_far, *refs, shifts):
    received, rho = refs[: shifts - 1], refs[shifts - 1]
    others, outs, scratch = refs[shifts : 2 * shifts], refs[2 * shifts : -1], refs[-1]
    weight = q_keep[...] + q_far[...].astype(F32)
    for part in received:
        weight = weight + part[...].astype(F32)
    weight = weight.astype(BF16)
    waves = rho.shape[1]
    width = waves // 2
    order = interleave(width)
    parts = [
        dot_nt(weight[:, width * i : width * (i + 1)], order).astype(BF16) for i in range(2)
    ]
    cuts = (0, width // 4, width // 2, width)
    sorted_weight = jnp.concatenate(
        [p[:, lo:hi] for lo, hi in zip(cuts, cuts[1:]) for p in parts], axis=1
    )
    cut(dot_nt(sorted_weight, rho[...]), scratch, [out.at[2] for out in outs])
    for out, other in zip(outs, others):
        out[:2] = other[...]


def send_kernel(pairs, own, *refs, groups, halves):
    received, out = refs[:-1], refs[-1]
    parts = own.shape[1]
    x = place(halves)[1]
    first = lax.axis_index("pairs") * parts
    spots = ((0, first + x), (0, first + 1 - x), (1, first + x))
    owned = out.shape[1]
    total = own[...]
    for part in received:
        total = total + part[...].astype(F32)
    for k in range(groups * owned):
        for part in range(parts):
            value = jnp.zeros(own.shape[2:], F32)
            for term, (slot, index) in enumerate(spots):
                value = value + jnp.where(pairs[slot, index] == k, total[term, part], 0.0)
            out[k // owned * parts + part, k % owned] = value.astype(BF16)


def local(orbitals, vectors, screened, pair_list, band_order):
    groups = lax.axis_size("pairs")
    columns = lax.axis_size("pw")
    pairs_here = screened.shape[0]
    halves = columns // pairs_here
    both = ("pairs", "pw")
    w = lax.axis_index("pw")
    k_count, band_here, chunk = orbitals.shape
    points = chunk * columns
    waves = screened.shape[2]
    width = waves // columns
    own_waves = width * pairs_here
    transitions = vectors.shape[2]
    vec_count = vectors.shape[1] * groups
    vec_part = vectors.shape[1] // pairs_here
    bands = band_here * groups
    members = [
        [gg * columns + xx * halves + jj for gg in range(groups) for xx in range(pairs_here)]
        for jj in range(halves)
    ]

    def exchange(value):
        return lax.all_to_all(value, both, 0, 0, tiled=True, axis_index_groups=members)

    def shift(value, s):
        return lax.ppermute(value, "pw", [(i, i ^ s) for i in range(columns)])

    def call(kernel, outs, *args, flops=0, scratch=(), limit=4, far=0, cost=None):
        moved = cost or sum(math.prod(v.shape) * v.dtype.itemsize for v in (*args, *outs))
        return pl.pallas_call(
            kernel,
            in_specs=[vmem] * (len(args) - far) + [hbm] * far,
            out_specs=[vmem] * len(outs),
            out_shape=list(outs),
            scratch_shapes=list(scratch),
            compiler_params=pltpu.CompilerParams(vmem_limit_bytes=limit * 2**20),
            cost_estimate=pl.CostEstimate(flops=flops, bytes_accessed=moved, transcendentals=0),
        )(*args)

    smem = pl.BlockSpec(memory_space=pltpu.SMEM)
    vmem = pl.BlockSpec(memory_space=pltpu.VMEM)
    hbm = pl.BlockSpec(memory_space=pltpu.HBM)
    like = jax.ShapeDtypeStruct

    slots = 2 * groups * pairs_here
    sent = pl.pallas_call(
        functools.partial(gather_kernel, halves=halves),
        in_specs=[smem, hbm, hbm],
        out_specs=hbm,
        out_shape=like((slots // 2, 2, band_here, chunk + transitions), BF16),
        scratch_shapes=[
            pltpu.VMEM((slots // 2, 2, band_here, chunk + transitions), BF16),
            pltpu.VMEM(vectors.shape, BF16),
            pltpu.SemaphoreType.DMA((slots // 2, 2)),
            pltpu.SemaphoreType.DMA((slots // 2,)),
            pltpu.SemaphoreType.DMA,
        ],
        compiler_params=pltpu.CompilerParams(vmem_limit_bytes=60 * 2**20),
    )(pair_list.T, orbitals, vectors)
    got = exchange(sent).reshape(groups, pairs_here, 2, band_here, chunk + transitions)
    seeds = lax.dynamic_index_in_dim(
        jnp.asarray(phase_tables(points, waves, halves, columns)), w % halves, keepdims=False
    )
    vec = got[..., chunk:].transpose(2, 0, 1, 3, 4).reshape(2, vec_count, transitions)
    picker = (band_order[:, None] == jnp.arange(bands, dtype=jnp.int32)[None, :]).astype(BF16)
    half_waves = own_waves // 2
    block = min(1024, chunk)
    (table,) = call(
        functools.partial(table_kernel, block=block, chunk=chunk),
        [like((3 * points // 4, half_waves), BF16)],
        seeds,
        flops=3 * points * half_waves,
    )
    picker, table = lax.optimization_barrier((picker, table))
    psi = jnp.einsum(
        "gbn,gxlbr->lxnr",
        picker.reshape(groups, band_here, bands),
        got[..., :chunk],
        preferred_element_type=F32,
    ).astype(BF16)
    products = NV * NC

    def transform(slot, outs, *args):
        parts = [psi[slot]] + [shift(psi[slot], s) for s in range(1, halves)]
        return call(
            functools.partial(transform_kernel, halves=halves, slot=slot),
            outs,
            *parts,
            vec[slot],
            *args,
            flops=products * points * own_waves,
            scratch=[
                pltpu.VMEM((2, 2, products, block), BF16),
                pltpu.VMEM((2, products, 2 * block), BF16),
                pltpu.VMEM((products, own_waves), F32),
            ]
            + [pltpu.SemaphoreType.DMA if slot else pltpu.SemaphoreType.DMA((points // 4 // block,))],
            limit=24 if slot else 36,
            far=1,
        )

    part = like((products, width), BF16)
    p_part = like((vec_count, width), BF16)
    rho_own, rho_msg, p_own, p_msg, table = transform(
        0, [part, part, p_part, p_part, like(table.shape, BF16)], table
    )
    p_far = shift(p_msg, halves)
    rho_far = shift(rho_msg, halves)
    full = like((vec_count, own_waves), BF16)
    rho, p_second, screened = transform(
        1,
        [like((products, own_waves), BF16), full, like(screened.shape, BF16)],
        table,
        screened,
    )

    p_own, p_second = lax.optimization_barrier((p_own, p_second))
    far = shift(p_second, halves)
    near = [shift(p_second, s) for s in range(1, halves)]
    fars = [shift(far, s) for s in range(1, halves)]
    flops = 4 * vec_count * width * waves
    partial_q = like((vec_count, own_waves), F32)
    q_keep, q_part, *q_msgs = call(
        back_kernel,
        [partial_q] * 2 + [like((vec_count, own_waves), BF16)] * (2 * (halves - 1)),
        p_own,
        p_far,
        screened,
        cost=1,
    )
    q_msgs, rho_far = lax.optimization_barrier((q_msgs, rho_far))
    received = [
        [shift(q_msgs[2 * (s - 1) + rel], s) for s in range(1, halves)] for rel in range(2)
    ]
    q_send = (q_part + sum(v.astype(F32) for v in received[1])).astype(BF16)
    q_far = shift(q_send, halves)
    vec_rows = vec_count // columns
    shape = (pairs_here, vec_rows, transitions)
    forward = call(
        functools.partial(forward_kernel, shifts=halves),
        [like((2, *shape), F32)] + [like((2, *shape), BF16)] * (halves - 1),
        p_second,
        *near,
        far,
        *fars,
        rho_own,
        rho_far,
        screened,
        cost=1,
        scratch=[pltpu.VMEM((2, columns, vec_rows, transitions), F32)],
    )
    out_own, *out_msgs = call(
        functools.partial(second_kernel, shifts=halves),
        [like((3, *shape), F32)] + [like((3, *shape), BF16)] * (halves - 1),
        q_keep,
        q_far,
        *received[0],
        rho,
        *forward,
        flops=2 * vec_count * products * own_waves,
        scratch=[pltpu.VMEM((columns, vec_rows, transitions), F32)],
    )

    received = [shift(out_msgs[s - 1], s) for s in range(1, halves)]
    placed = pl.pallas_call(
        functools.partial(send_kernel, groups=groups, halves=halves),
        in_specs=[smem] + [vmem] * halves,
        out_specs=vmem,
        out_shape=like(
            (groups * pairs_here, k_count // groups, vec_rows, transitions), BF16
        ),
        compiler_params=pltpu.CompilerParams(vmem_limit_bytes=4 * 2**20),
    )(pair_list.T, out_own, *received)
    return jnp.sum(exchange(placed).astype(F32), axis=0)


def solution(mesh):
    in_specs = (P(None, "pairs", "pw"), P(None, "pairs", None), P("pairs", "pw", None), P(), P())
    out_specs = P("pairs", "pw", None)
    return jax.shard_map(local, mesh=mesh, in_specs=in_specs, out_specs=out_specs, check_vma=False)
```

time: 92.6 us -> 86.5 us (0.934)
  waiting for transfers between devices: 32.5 us -> 23.1 us
  local copies, waits for them, and re-layouts: 3.56 us -> 6.77 us
  Pallas kernels: 23.2 us -> 25 us
    all_to_all x1, waiting for transfers between devices: 24.1 us -> 14.7 us  [exchange(): lax.all_to_all(value, both, 0, 0, tiled=True, axis_index_groups=members)]
    unnamed x8, local copies, waits for them, and re-layouts: 0.5 us -> 4.54 us
    pallas_call x6, Pallas kernels: 19.1 us -> 20.9 us  [call(): pl.pallas_call(kernel, in_specs=[vmem] * (len(args) - far) + [hbm] * far,...]
    ppermute x10 -> x11, starting transfers between devices: 5.87 us -> 5.12 us  [shift(): return lax.ppermute(value, 'pw', [(i, i ^ s) for i in range(columns)])]
    ppermute x10 -> x11, waiting for transfers between devices: 8.42 us -> 8.41 us  [shift(): return lax.ppermute(value, 'pw', [(i, i ^ s) for i in range(columns)])]
  transfers between devices with their start and end apart: 11 -> 12, of which waited for: 6 -> 6; matrix products, arithmetic and copies ran while one was open for 3% -> 2% of each run, Pallas kernels for 19% -> 24%
where the time goes in v4:
time: 86.5 us; the launch traced here: 86.1 us
  Pallas kernels  25 us (29%)
  waiting for transfers between devices  23.1 us (27%)
  blocking collectives  16.1 us (19%)
  starting transfers between devices  13.4 us (15%)
  local copies, waits for them, and re-layouts  6.77 us (8%)
    pallas_call x6, Pallas kernels, call(): pl.pallas_call(kernel, in_specs=[vmem] * (len(args) - far) + [hbm] * far,...  20.9 us
    all_to_all x1, blocking collectives, exchange(): lax.all_to_all(value, both, 0, 0, tiled=True, axis_index_groups=members)  16.1 us
    all_to_all x1, waiting for transfers between devices, exchange(): lax.all_to_all(value, both, 0, 0, tiled=True, axis_index_groups=members)  14.7 us
    ppermute x11, waiting for transfers between devices, shift(): return lax.ppermute(value, 'pw', [(i, i ^ s) for i in range(columns)])  8.41 us
    all_to_all x1, starting transfers between devices, exchange(): lax.all_to_all(value, both, 0, 0, tiled=True, axis_index_groups=members)  8.32 us
    ppermute x11, starting transfers between devices, shift(): return lax.ppermute(value, 'pw', [(i, i ^ s) for i in range(columns)])  5.12 us
    unnamed x8, local copies, waits for them, and re-layouts  4.54 us
    pallas_call x1, Pallas kernels, local(): pl.pallas_call(functools.partial(gather_kernel, halves=halves), in_specs=...  3.4 us
  transfers between devices with their start and end apart: 12, of which 6 were waited for; matrix products, arithmetic and copies ran while one was open for 2% of the time, Pallas kernels for 24%

profile of v4, /device:TPU:0, one launch (start us, length us, event | category | flops | bytes accessed | tf_op | source)
XLA Modules:
  0.0 86.1 jit_solution(11062970865580976777)
XLA Ops:
  0.0 3.4 %shard_map.64 = bf16[16,2,4,4352]{3,2,1,0:T(4,128)(2,1)} custom-call(s32[2,16]{1,0:T(2,128)} %bitcast.22, bf16[16,4,4096]{2,1,0:T(4,128)(2,1)} %orbitals.1, bf16[16,8,256]{2,1,0:T(8,128)(2,1)} %far_vectors.1), custom_call_target="tpu_custom_call" | custom-call | tf_op jit(solution)/shard_map/pallas_call | solution.py:386
  3.4 8.3 %all-to-all-start = ((bf16[16,2,4,4352]{3,2,1,0:T(4,128)(2,1)}), bf16[16,2,4,4352]{3,2,1,0:T(4,128)(2,1)S(1)}, u32[]{:S(2)}, u32[]{:S(2)}) async-start(bf16[16,2,4,4352]{3,2,1,0:T(4,128)(2,1)} %shard_map.64), calls=%async_computation | async-start | bytes 2228224 | tf_op jit(solution)/shard_map/all_to_all | solution.py:363
  11.8 1.5 %dynamic-slice_bitcast_fusion.seeds = f32[2,192,1024]{2,1,0:T(8,128)S(1)} fusion(f32[2,2,192,1024]{3,2,1,0:T(8,128)} %constant.25.clone, s32[]{:T(128)S(6)} %select_n.12), kind=kLoop, calls=%fused_computation.3 | loop fusion | bytes 3145732 | tf_op jit(solution)/shard_map/jit(dynamic_index_in_dim)/squeeze | solution.py:401
  13.3 0.0 copy-start.3
  13.3 4.9 %shard_map.65.refs_3_ = bf16[12288,512]{1,0:T(8,128)(2,1)S(1)} custom-call(f32[2,192,1024]{2,1,0:T(8,128)S(1)} %dynamic-slice_bitcast_fusion.seeds), custom_call_target="tpu_custom_call" | custom-call | flops 25165824 | bytes 14155776 | tf_op jit(solution)/shard_map/pallas_call | solution.py:370
  18.2 0.0 copy-start
  18.2 4.5 %copy-done = bf16[12288,512]{1,0:T(8,128)(2,1)} copy-done((bf16[12288,512]{1,0:T(8,128)(2,1)}, bf16[12288,512]{1,0:T(8,128)(2,1)S(1)}, u32[]{:S(2)}) %copy-start) | copy-done | bytes 12582936
  22.7 0.0 copy-done.3
  22.7 0.1 fusion.3
  22.8 14.7 %all-to-all-done = bf16[16,2,4,4352]{3,2,1,0:T(4,128)(2,1)S(1)} async-done(((bf16[16,2,4,4352]{3,2,1,0:T(4,128)(2,1)}), bf16[16,2,4,4352]{3,2,1,0:T(4,128)(2,1)S(1)}, u32[]{:S(2)}, u32[]{:S(2)}) %all-to-all-start) | async-done | bytes 1114144 | tf_op jit(solution)/shard_map/all_to_all | solution.py:363
  37.5 0.5 slice.28
  38.0 0.8 fusion.1
  38.8 0.1 slice_bitcast_fusion
  38.9 0.1 collective-permute-start
  39.0 0.5 collective-permute-start.1
  39.6 0.0 copy-start.1
  39.6 1.3 %collective-permute-done.refs_1_ = bf16[2,32,4096]{2,1,0:T(8,128)(2,1)S(1)} collective-permute-done((bf16[2,32,4096]{2,1,0:T(8,128)(2,1)S(1)}, bf16[2,32,4096]{2,1,0:T(8,128)(2,1)S(1)}, u32[]{:S(2)}, u32[]{:S(2)}) %collective-permute-start) | collective-permute-done | bytes 524320 | tf_op jit(solution)/shard_map/ppermute | solution.py:366
  40.9 7.2 %shard_map.66 = (bf16[256,512]{1,0:T(8,128)(2,1)S(1)}, bf16[256,512]{1,0:T(8,128)(2,1)S(1)}, bf16[64,512]{1,0:T(8,128)(2,1)S(1)}, bf16[64,512]{1,0:T(8,128)(2,1)S(1)}, bf16[12288,512]{1,0:T(8,128)(2,1)S(1)}) custom-call(bf16[2,32,4096]{2,1,0:T(8,128)(2,1)S(1)} %get-tuple-element.52.refs_0_, bf16[2,32,4096]{2,1,0:T(8,128)(2,1)S(1)} %collective-permute-done.refs_1_, ...), custom_call_target="tpu_custom_call" | custom-call | flops 4294967296 | bytes 26902528 | tf_op jit(solution)/shard_map/pallas_call | solution.py:370
  48.1 0.6 collective-permute-start.2
  48.7 1.5 %collective-permute-start.3 = (bf16[256,512]{1,0:T(8,128)(2,1)S(1)}, bf16[256,512]{1,0:T(8,128)(2,1)S(1)}, u32[]{:S(2)}, u32[]{:S(2)}) collective-permute-start(bf16[256,512]{1,0:T(8,128)(2,1)S(1)} %get-tuple-element.40), channel_id=1, source_target_pairs={{0,2},{1,3},{2,0},{3,1},{4,6},{5,7},{6,4},{7,5},{8,10},{9,11},{10,... | collective-permute-start | bytes 786440 | tf_op jit(solution)/shard_map/ppermute | solution.py:366
  50.2 0.0 collective-permute-done.1.refs_1_
  50.2 0.0 copy-done.1
  50.2 5.3 %shard_map.67 = (bf16[256,1024]{1,0:T(8,128)(2,1)S(1)}, bf16[64,1024]{1,0:T(8,128)(2,1)S(1)}, bf16[2,512,2048]{2,1,0:T(8,128)(2,1)S(1)}) custom-call(bf16[2,32,4096]{2,1,0:T(8,128)(2,1)S(1)} %get-tuple-element.51.refs_0_, bf16[2,32,4096]{2,1,0:T(8,128)(2,1)S(1)} %collective-permute-done.1.refs_1_, bf16[64,256]{1,0:T(8,128)(2,1)S(1)} %squeeze.22.refs_2_, ...), custom_call_target="tpu_custom_call" | custom-call | flops 4294967296 | bytes 22708224 | tf_op jit(solution)/shard_map/pallas_call | solution.py:370
  55.5 0.6 collective-permute-start.8
  56.1 0.0 collective-permute-done.2.p_far
  56.1 0.8 shard_map.68
  56.9 1.1 %collective-permute-done.3.refs_5_ = bf16[256,512]{1,0:T(8,128)(2,1)S(1)} collective-permute-done((bf16[256,512]{1,0:T(8,128)(2,1)S(1)}, bf16[256,512]{1,0:T(8,128)(2,1)S(1)}, u32[]{:S(2)}, u32[]{:S(2)}) %collective-permute-start.3) | collective-permute-done | bytes 262176 | tf_op jit(solution)/shard_map/ppermute | solution.py:366
  58.0 0.0 collective-permute-start.4
  58.0 0.5 collective-permute-start.7
  58.5 2.2 %collective-permute-done.8.refs_2_ = bf16[64,1024]{1,0:T(8,128)(2,1)S(1)} collective-permute-done((bf16[64,1024]{1,0:T(8,128)(2,1)S(1)}, bf16[64,1024]{1,0:T(8,128)(2,1)S(1)}, u32[]{:S(2)}, u32[]{:S(2)}) %collective-permute-start.8) | collective-permute-done | bytes 131104 | tf_op jit(solution)/shard_map/ppermute | solution.py:366
  60.7 0.0 collective-permute-start.9
  60.7 0.5 collective-permute-start.6
  61.2 0.0 collective-permute-done.4
  61.2 0.8 collective-permute-start.5
  62.0 0.0 collective-permute-done.7.refs_1_
  62.0 0.0 collective-permute-done.9.refs_3_
  62.0 0.0 copy-start.2
  62.0 2.0 %shard_map.69 = (f32[2,2,16,256]{3,2,1,0:T(8,128)S(1)}, bf16[2,2,16,256]{3,2,1,0:T(8,128)(2,1)S(1)}) custom-call(bf16[64,1024]{1,0:T(8,128)(2,1)S(1)} %get-tuple-element.44.refs_0_, bf16[64,1024]{1,0:T(8,128)(2,1)S(1)} %collective-permute-done.7.refs_1_, bf16[64,1024]{1,0:T(8,128)(2,1)S(1)} %collective-permute-done.8.refs_2_, ...), custom_call_target="tpu_custom_call" | custom-call | bytes 1 | tf_op jit(solution)/shard_map/pallas_call | solution.py:370
  64.1 0.0 collective-permute-done.6.refs_0_
  64.1 2.6 %collective-permute-done.5.q_far = bf16[64,1024]{1,0:T(8,128)(2,1)S(1)} collective-permute-done((bf16[64,1024]{1,0:T(8,128)(2,1)S(1)}, bf16[64,1024]{1,0:T(8,128)(2,1)S(1)}, u32[]{:S(2)}, u32[]{:S(2)}) %collective-permute-start.5) | collective-permute-done | bytes 131104 | tf_op jit(solution)/shard_map/ppermute | solution.py:366
  66.7 0.7 shard_map.70
  67.4 0.1 collective-permute-start.10
  67.5 1.2 %collective-permute-done.10.refs_0_ = bf16[3,2,16,256]{3,2,1,0:T(8,128)(2,1)S(1)} collective-permute-done((bf16[3,2,16,256]{3,2,1,0:T(8,128)(2,1)S(1)}, bf16[3,2,16,256]{3,2,1,0:T(8,128)(2,1)S(1)}, u32[]{:S(2)}, u32[]{:S(2)}) %collective-permute-start.10) | collective-permute-done | bytes 49184 | tf_op jit(solution)/shard_map/ppermute | solution.py:366
  68.7 0.0 copy-done.2
  68.7 0.7 shard_map.71
  69.4 16.1 %all_to_all.10 = bf16[16,2,16,256]{3,2,1,0:T(8,128)(2,1)S(1)} all-to-all(bf16[16,2,16,256]{3,2,1,0:T(8,128)(2,1)S(1)} %shard_map.71), channel_id=1, replica_groups={{0,2,4,6,8,10,12,14,16,18,20,22,24,26,28,30},{1,3,5,7,9,11,13,15,17,19,..., dimensions={0} | all-to-all | bytes 524288 | tf_op jit(solution)/shard_map/all_to_all | solution.py:363
  85.5 0.7 convert_reduce_fusion
  (5 shorter events, 0.1 us)
Async XLA Ops:
  3.4 34.1 %all-to-all-start = ((bf16[16,2,4,4352]{3,2,1,0:T(4,128)(2,1)}), bf16[16,2,4,4352]{3,2,1,0:T(4,128)(2,1)S(1)}, u32[]{:S(2)}, u32[]{:S(2)}) async-start(bf16[16,2,4,4352]{3,2,1,0:T(4,128)(2,1)} %shard_map.64), calls=%async_computation | async-start | bytes 2228224 | tf_op jit(solution)/shard_map/all_to_all | solution.py:363
  13.3 9.4 %copy-start.3 = (s32[32]{0:T(128)S(1)}, s32[32]{0:T(128)}, u32[]{:S(2)}) copy-start(s32[32]{0:T(128)} %param.10) | copy-start | bytes 388
  18.2 4.5 %copy-start = (bf16[12288,512]{1,0:T(8,128)(2,1)}, bf16[12288,512]{1,0:T(8,128)(2,1)S(1)}, u32[]{:S(2)}) copy-start(bf16[12288,512]{1,0:T(8,128)(2,1)S(1)} %shard_map.65.refs_3_) | copy-start | bytes 37748740
  38.9 2.0 %collective-permute-start = (bf16[2,32,4096]{2,1,0:T(8,128)(2,1)S(1)}, bf16[2,32,4096]{2,1,0:T(8,128)(2,1)S(1)}, u32[]{:S(2)}, u32[]{:S(2)}) collective-permute-start(bf16[2,32,4096]{2,1,0:T(8,128)(2,1)S(1)} %get-tuple-element.52.refs_0_), channel_id=1, source_target_pairs={{0,1},{1,0},{2,3},{3,2},{4,5},{5,4},{6,7},{7,6},{8,9},{9,8},{10,11... | collective-permute-start | bytes 1572872 | tf_op jit(solution)/shard_map/ppermute | solution.py:366
  39.0 11.2 %collective-permute-start.1 = (bf16[2,32,4096]{2,1,0:T(8,128)(2,1)S(1)}, bf16[2,32,4096]{2,1,0:T(8,128)(2,1)S(1)}, u32[]{:S(2)}, u32[]{:S(2)}) collective-permute-start(bf16[2,32,4096]{2,1,0:T(8,128)(2,1)S(1)} %get-tuple-element.51.refs_0_), channel_id=1, source_target_pairs={{0,1},{1,0},{2,3},{3,2},{4,5},{5,4},{6,7},{7,6},{8,9},{9,8},{10,11... | collective-permute-start | bytes 1572872 | tf_op jit(solution)/shard_map/ppermute | solution.py:366
  39.6 10.6 %copy-start.1 = (bf16[2,512,2048]{2,1,0:T(8,128)(2,1)S(1)}, bf16[2,512,2048]{2,1,0:T(8,128)(2,1)}, u32[]{:S(2)}) copy-start(bf16[2,512,2048]{2,1,0:T(8,128)(2,1)} %refs_4_.1) | copy-start | bytes 12582916
  48.1 8.0 %collective-permute-start.2 = (bf16[64,512]{1,0:T(8,128)(2,1)S(1)}, bf16[64,512]{1,0:T(8,128)(2,1)S(1)}, u32[]{:S(2)}, u32[]{:S(2)}) collective-permute-start(bf16[64,512]{1,0:T(8,128)(2,1)S(1)} %get-tuple-element.34), channel_id=1, source_target_pairs={{0,2},{1,3},{2,0},{3,1},{4,6},{5,7},{6,4},{7,5},{8,10},{9,11},{10,... | collective-permute-start | bytes 196616 | tf_op jit(solution)/shard_map/ppermute | solution.py:366
  48.7 9.3 %collective-permute-start.3 = (bf16[256,512]{1,0:T(8,128)(2,1)S(1)}, bf16[256,512]{1,0:T(8,128)(2,1)S(1)}, u32[]{:S(2)}, u32[]{:S(2)}) collective-permute-start(bf16[256,512]{1,0:T(8,128)(2,1)S(1)} %get-tuple-element.40), channel_id=1, source_target_pairs={{0,2},{1,3},{2,0},{3,1},{4,6},{5,7},{6,4},{7,5},{8,10},{9,11},{10,... | collective-permute-start | bytes 786440 | tf_op jit(solution)/shard_map/ppermute | solution.py:366
  55.5 5.2 %collective-permute-start.8 = (bf16[64,1024]{1,0:T(8,128)(2,1)S(1)}, bf16[64,1024]{1,0:T(8,128)(2,1)S(1)}, u32[]{:S(2)}, u32[]{:S(2)}) collective-permute-start(bf16[64,1024]{1,0:T(8,128)(2,1)S(1)} %get-tuple-element.44.refs_0_), channel_id=1, source_target_pairs={{0,2},{1,3},{2,0},{3,1},{4,6},{5,7},{6,4},{7,5},{8,10},{9,11},{10,... | collective-permute-start | bytes 393224 | tf_op jit(solution)/shard_map/ppermute | solution.py:366
  58.0 3.2 %collective-permute-start.4 = (bf16[64,1024]{1,0:T(8,128)(2,1)S(1)}, bf16[64,1024]{1,0:T(8,128)(2,1)S(1)}, u32[]{:S(2)}, u32[]{:S(2)}) collective-permute-start(bf16[64,1024]{1,0:T(8,128)(2,1)S(1)} %get-tuple-element.41), channel_id=1, source_target_pairs={{0,1},{1,0},{2,3},{3,2},{4,5},{5,4},{6,7},{7,6},{8,9},{9,8},{10,11... | collective-permute-start | bytes 393224 | tf_op jit(solution)/shard_map/ppermute | solution.py:366
  58.0 4.0 %collective-permute-start.7 = (bf16[64,1024]{1,0:T(8,128)(2,1)S(1)}, bf16[64,1024]{1,0:T(8,128)(2,1)S(1)}, u32[]{:S(2)}, u32[]{:S(2)}) collective-permute-start(bf16[64,1024]{1,0:T(8,128)(2,1)S(1)} %get-tuple-element.44.refs_0_), channel_id=1, source_target_pairs={{0,1},{1,0},{2,3},{3,2},{4,5},{5,4},{6,7},{7,6},{8,9},{9,8},{10,11... | collective-permute-start | bytes 393224 | tf_op jit(solution)/shard_map/ppermute | solution.py:366
  60.7 1.3 %collective-permute-start.9 = (bf16[64,1024]{1,0:T(8,128)(2,1)S(1)}, bf16[64,1024]{1,0:T(8,128)(2,1)S(1)}, u32[]{:S(2)}, u32[]{:S(2)}) collective-permute-start(bf16[64,1024]{1,0:T(8,128)(2,1)S(1)} %collective-permute-done.8.refs_2_), channel_id=1, source_target_pairs={{0,1},{1,0},{2,3},{3,2},{4,5},{5,4},{6,7},{7,6},{8,9},{9,8},{10,11... | collective-permute-start | bytes 393224 | tf_op jit(solution)/shard_map/ppermute | solution.py:366
  60.7 3.4 %collective-permute-start.6 = (bf16[64,1024]{1,0:T(8,128)(2,1)S(1)}, bf16[64,1024]{1,0:T(8,128)(2,1)S(1)}, u32[]{:S(2)}, u32[]{:S(2)}) collective-permute-start(bf16[64,1024]{1,0:T(8,128)(2,1)S(1)} %get-tuple-element.42), channel_id=1, source_target_pairs={{0,1},{1,0},{2,3},{3,2},{4,5},{5,4},{6,7},{7,6},{8,9},{9,8},{10,11... | collective-permute-start | bytes 393224 | tf_op jit(solution)/shard_map/ppermute | solution.py:366
  61.2 5.5 %collective-permute-start.5 = (bf16[64,1024]{1,0:T(8,128)(2,1)S(1)}, bf16[64,1024]{1,0:T(8,128)(2,1)S(1)}, u32[]{:S(2)}, u32[]{:S(2)}) collective-permute-start(bf16[64,1024]{1,0:T(8,128)(2,1)S(1)} %add_convert_fusion), channel_id=1, source_target_pairs={{0,2},{1,3},{2,0},{3,1},{4,6},{5,7},{6,4},{7,5},{8,10},{9,11},{10,... | collective-permute-start | bytes 393224 | tf_op jit(solution)/shard_map/ppermute | solution.py:366
  62.0 6.7 %copy-start.2 = (s32[16,2]{0,1:T(2,128)S(1)}, s32[16,2]{0,1:T(2,128)}, u32[]{:S(2)}) copy-start(s32[16,2]{0,1:T(2,128)} %param.9) | copy-start | bytes 388
  67.4 1.3 %collective-permute-start.10 = (bf16[3,2,16,256]{3,2,1,0:T(8,128)(2,1)S(1)}, bf16[3,2,16,256]{3,2,1,0:T(8,128)(2,1)S(1)}, u32[]{:S(2)}, u32[]{:S(2)}) collective-permute-start(bf16[3,2,16,256]{3,2,1,0:T(8,128)(2,1)S(1)} %get-tuple-element.50), channel_id=1, source_target_pairs={{0,1},{1,0},{2,3},{3,2},{4,5},{5,4},{6,7},{7,6},{8,9},{9,8},{10,11... | collective-permute-start | bytes 147464 | tf_op jit(solution)/shard_map/ppermute | solution.py:366

commit v5 on v4

--- a/solution.py
+++ b/solution.py
@@ -153,17 +153,16 @@
 
 
 def transform_kernel(*refs, halves, slot):
-    parts, vec = refs[:halves], refs[halves]
-    refs = refs[halves + 1 :]
+    parts, refs = refs[:halves], refs[halves:]
     table_copies = []
     if slot == 0:
-        far_table, rho_own, rho_msg, p_own, p_msg, table, sem = *refs[:6], refs[-1]
+        vec, far_table, rho_own, rho_msg, table, sem = *refs[:5], refs[-1]
         for t in range(sem.shape[0]):
             span = pl.ds(t * (table.shape[0] // sem.shape[0]), table.shape[0] // sem.shape[0])
             table_copies.append(pltpu.make_async_copy(far_table.at[span], table.at[span], sem.at[t]))
             table_copies[-1].start()
     else:
-        table, far_screened, rho, natural_out, screened = refs[:5]
+        vec, table, far_screened, rho, natural_out, screened = refs[:6]
         copy = pltpu.make_async_copy(far_screened, screened, refs[-1])
         copy.start()
     refs = refs[:-1]
@@ -228,33 +227,45 @@
             produce(t + 1)
         consume(t)
     done = acc[...].astype(BF16)
-    width = waves // 2
-    proj = dot(vec[...], done).astype(BF16)
-    order = interleave(width)
-
-    def chunk_of(array, i):
-        return jnp.concatenate([array[:, o : o + n] for o, n in pieces(waves, i, width)], axis=1)
-
-    natural = [dot(chunk_of(proj, i), order).astype(BF16) for i in range(2)]
+    both = [
+        jnp.concatenate([done[:, o : o + n] for o, n in pieces(waves, i, waves // 2)], axis=1)
+        for i in range(2)
+    ]
     if slot == 1:
         rho[...] = done
-        natural_out[...] = jnp.concatenate(natural, axis=1)
+        order = interleave(waves // 2)
+        natural_out[...] = jnp.concatenate([project(vec, part, order) for part in both], axis=1)
         copy.wait()
     else:
-        both = [chunk_of(done, i) for i in range(2)]
         rho_own[...] = jnp.where(x == 0, both[0], both[1])
-        rho_msg[...] = jnp.where(x == 0, both[1], both[0])
-        p_own[...] = jnp.where(x == 0, natural[0], natural[1])
-        p_msg[...] = jnp.where(x == 0, natural[1], natural[0])
-
-
-def back_kernel(p_own, p_far, screened, q_keep, q_part, *q_msgs):
+        rho_msg[: NV * NC] = jnp.where(x == 0, both[1], both[0])
+        rho_msg[NV * NC :] = pack(vec[...], rho_msg.shape[1])
+
+
+def pack(array, width):
+    rows, cols = array.shape
+    if cols < width:
+        step = rows * cols // width
+        return jnp.concatenate([array[i : i + step] for i in range(0, rows, step)], axis=1)
+    return jnp.concatenate([array[:, i : i + width] for i in range(0, cols, width)], axis=0)
+
+
+def project(vec, rho, order):
+    return dot(dot(vec[...], rho).astype(BF16), order).astype(BF16)
+
+
+def back_kernel(vec_own, rho_own, rho_far, screened, q_keep, q_part, *q_msgs):
     shifts = len(q_msgs) // 2 + 1
     j, x = place(shifts)
-    width = p_own.shape[1]
+    width = rho_own.shape[1]
+    order = interleave(width)
     for rel in range(2):
         pair = x if rel == 0 else 1 - x
-        first = (p_far if rel else p_own)[...]
+        if rel:
+            vec = pack(rho_far[NV * NC :, :], vec_own.shape[1])
+            first = project(vec, rho_far[: NV * NC, :], order)
+        else:
+            first = project(vec_own, rho_own[...], order)
         for s in range(shifts):
             for c in range(2):
                 start = pl.multiple_of((c * shifts + (j ^ s)) * width, width)
@@ -294,7 +305,7 @@
                 )
                 total = term if total is None else total + term
         weight = dot_nt(total.astype(BF16), order).astype(BF16)
-        products = (rho_far if rel else rho_own)[...]
+        products = (rho_far if rel else rho_own)[: NV * NC, :]
         cut(dot_nt(weight, products), scratch.at[rel], [out.at[rel] for out in outs])
 
 
@@ -426,7 +437,6 @@
             functools.partial(transform_kernel, halves=halves, slot=slot),
             outs,
             *parts,
-            vec[slot],
             *args,
             flops=products * points * own_waves,
             scratch=[
@@ -440,21 +450,19 @@
         )
 
     part = like((products, width), BF16)
-    p_part = like((vec_count, width), BF16)
-    rho_own, rho_msg, p_own, p_msg, table = transform(
-        0, [part, part, p_part, p_part, like(table.shape, BF16)], table
-    )
-    p_far = shift(p_msg, halves)
+    packed = like((products + vec_count * transitions // width, width), BF16)
+    rho_own, rho_msg, table = transform(0, [part, packed, like(table.shape, BF16)], vec[0], table)
     rho_far = shift(rho_msg, halves)
     full = like((vec_count, own_waves), BF16)
     rho, p_second, screened = transform(
         1,
         [like((products, own_waves), BF16), full, like(screened.shape, BF16)],
+        vec[1],
         table,
         screened,
     )
 
-    p_own, p_second = lax.optimization_barrier((p_own, p_second))
+    rho_own, p_second = lax.optimization_barrier((rho_own, p_second))
     far = shift(p_second, halves)
     near = [shift(p_second, s) for s in range(1, halves)]
     fars = [shift(far, s) for s in range(1, halves)]
@@ -463,12 +471,12 @@
     q_keep, q_part, *q_msgs = call(
         back_kernel,
         [partial_q] * 2 + [like((vec_count, own_waves), BF16)] * (2 * (halves - 1)),
-        p_own,
-        p_far,
+        vec[0],
+        rho_own,
+        rho_far,
         screened,
         cost=1,
     )
-    q_msgs, rho_far = lax.optimization_barrier((q_msgs, rho_far))
     received = [
         [shift(q_msgs[2 * (s - 1) + rel], s) for s in range(1, halves)] for rel in range(2)
     ]

time: 86.5 us -> 85.6 us (0.990)
    ppermute x11 -> x10, waiting for transfers between devices: 8.41 us -> 7.77 us  [shift(): return lax.ppermute(value, 'pw', [(i, i ^ s) for i in range(columns)])]
    ppermute x11 -> x10, starting transfers between devices: 5.12 us -> 4.67 us  [shift(): return lax.ppermute(value, 'pw', [(i, i ^ s) for i in range(columns)])]
  transfers between devices with their start and end apart: 12 -> 11, of which waited for: 6 -> 7; matrix products, arithmetic and copies ran while one was open for 2% -> 2% of each run, Pallas kernels for 24% -> 24%
where the time goes in v5:
time: 85.6 us; the launch traced here: 85.4 us
  Pallas kernels  25.5 us (30%)
  waiting for transfers between devices  22.5 us (26%)
  blocking collectives  15.9 us (19%)
  starting transfers between devices  13 us (15%)
  local copies, waits for them, and re-layouts  6.78 us (8%)
    pallas_call x6, Pallas kernels, call(): pl.pallas_call(kernel, in_specs=[vmem] * (len(args) - far) + [hbm] * far,...  21.2 us
    all_to_all x1, blocking collectives, exchange(): lax.all_to_all(value, both, 0, 0, tiled=True, axis_index_groups=members)  15.9 us
    all_to_all x1, waiting for transfers between devices, exchange(): lax.all_to_all(value, both, 0, 0, tiled=True, axis_index_groups=members)  14.7 us
    all_to_all x1, starting transfers between devices, exchange(): lax.all_to_all(value, both, 0, 0, tiled=True, axis_index_groups=members)  8.32 us
    ppermute x10, waiting for transfers between devices, shift(): return lax.ppermute(value, 'pw', [(i, i ^ s) for i in range(columns)])  7.77 us
    ppermute x10, starting transfers between devices, shift(): return lax.ppermute(value, 'pw', [(i, i ^ s) for i in range(columns)])  4.67 us
    unnamed x8, local copies, waits for them, and re-layouts  4.55 us
    pallas_call x1, Pallas kernels, local(): pl.pallas_call(functools.partial(gather_kernel, halves=halves), in_specs=...  3.63 us
  transfers between devices with their start and end apart: 11, of which 7 were waited for; matrix products, arithmetic and copies ran while one was open for 2% of the time, Pallas kernels for 24%

profile of v5, /device:TPU:0, one launch (start us, length us, event | category | flops | bytes accessed | tf_op | source)
XLA Modules:
  0.0 85.4 jit_solution(11842411511386143552)
XLA Ops:
  0.0 3.6 %shard_map.64 = bf16[16,2,4,4352]{3,2,1,0:T(4,128)(2,1)} custom-call(s32[2,16]{1,0:T(2,128)} %bitcast.22, bf16[16,4,4096]{2,1,0:T(4,128)(2,1)} %orbitals.1, bf16[16,8,256]{2,1,0:T(8,128)(2,1)} %far_vectors.1), custom_call_target="tpu_custom_call" | custom-call | tf_op jit(solution)/shard_map/pallas_call | solution.py:397
  3.6 8.3 %all-to-all-start = ((bf16[16,2,4,4352]{3,2,1,0:T(4,128)(2,1)}), bf16[16,2,4,4352]{3,2,1,0:T(4,128)(2,1)S(1)}, u32[]{:S(2)}, u32[]{:S(2)}) async-start(bf16[16,2,4,4352]{3,2,1,0:T(4,128)(2,1)} %shard_map.64), calls=%async_computation | async-start | bytes 2228224 | tf_op jit(solution)/shard_map/all_to_all | solution.py:374
  12.0 1.5 %dynamic-slice_bitcast_fusion.seeds = f32[2,192,1024]{2,1,0:T(8,128)S(1)} fusion(f32[2,2,192,1024]{3,2,1,0:T(8,128)} %constant.25.clone, s32[]{:T(128)S(6)} %select_n.12), kind=kLoop, calls=%fused_computation.3 | loop fusion | bytes 3145732 | tf_op jit(solution)/shard_map/jit(dynamic_index_in_dim)/squeeze | solution.py:412
  13.5 0.0 copy-start.3
  13.5 4.9 %shard_map.65.refs_3_ = bf16[12288,512]{1,0:T(8,128)(2,1)S(1)} custom-call(f32[2,192,1024]{2,1,0:T(8,128)S(1)} %dynamic-slice_bitcast_fusion.seeds), custom_call_target="tpu_custom_call" | custom-call | flops 25165824 | bytes 14155776 | tf_op jit(solution)/shard_map/pallas_call | solution.py:381
  18.4 0.0 copy-start
  18.4 4.5 %copy-done = bf16[12288,512]{1,0:T(8,128)(2,1)} copy-done((bf16[12288,512]{1,0:T(8,128)(2,1)}, bf16[12288,512]{1,0:T(8,128)(2,1)S(1)}, u32[]{:S(2)}) %copy-start) | copy-done | bytes 12582936
  22.9 0.0 copy-done.3
  22.9 0.1 fusion.3
  23.0 14.7 %all-to-all-done = bf16[16,2,4,4352]{3,2,1,0:T(4,128)(2,1)S(1)} async-done(((bf16[16,2,4,4352]{3,2,1,0:T(4,128)(2,1)}), bf16[16,2,4,4352]{3,2,1,0:T(4,128)(2,1)S(1)}, u32[]{:S(2)}, u32[]{:S(2)}) %all-to-all-start) | async-done | bytes 1114144 | tf_op jit(solution)/shard_map/all_to_all | solution.py:374
  37.7 0.5 slice.31
  38.3 0.8 fusion.1
  39.0 0.1 slice_bitcast_fusion
  39.1 0.1 collective-permute-start
  39.2 0.5 collective-permute-start.1
  39.8 0.0 copy-start.1
  39.8 1.3 %collective-permute-done.refs_1_ = bf16[2,32,4096]{2,1,0:T(8,128)(2,1)S(1)} collective-permute-done((bf16[2,32,4096]{2,1,0:T(8,128)(2,1)S(1)}, bf16[2,32,4096]{2,1,0:T(8,128)(2,1)S(1)}, u32[]{:S(2)}, u32[]{:S(2)}) %collective-permute-start) | collective-permute-done | bytes 524320 | tf_op jit(solution)/shard_map/ppermute | solution.py:377
  41.1 6.8 %shard_map.66 = (bf16[256,512]{1,0:T(8,128)(2,1)S(1)}, bf16[288,512]{1,0:T(8,128)(2,1)S(1)}, bf16[12288,512]{1,0:T(8,128)(2,1)S(1)}) custom-call(bf16[2,32,4096]{2,1,0:T(8,128)(2,1)S(1)} %get-tuple-element.42.refs_0_, bf16[2,32,4096]{2,1,0:T(8,128)(2,1)S(1)} %collective-permute-done.refs_1_, bf16[64,256]{1,0:T(8,128)(2,1)S(1)} %squeeze.19.refs_2_.vec_own, ...), custom_call_target="tpu_custom_call" | custom-call | flops 4294967296 | bytes 26804224 | tf_op jit(solution)/shard_map/pallas_call | solution.py:381
  47.9 0.6 collective-permute-start.2
  48.5 0.0 collective-permute-done.1.refs_1_
  48.5 0.0 copy-done.1
  48.5 5.3 %shard_map.67 = (bf16[256,1024]{1,0:T(8,128)(2,1)S(1)}, bf16[64,1024]{1,0:T(8,128)(2,1)S(1)}, bf16[2,512,2048]{2,1,0:T(8,128)(2,1)S(1)}) custom-call(bf16[2,32,4096]{2,1,0:T(8,128)(2,1)S(1)} %get-tuple-element.41.refs_0_, bf16[2,32,4096]{2,1,0:T(8,128)(2,1)S(1)} %collective-permute-done.1.refs_1_, bf16[64,256]{1,0:T(8,128)(2,1)S(1)} %squeeze.23.refs_2_, ...), custom_call_target="tpu_custom_call" | custom-call | flops 4294967296 | bytes 22708224 | tf_op jit(solution)/shard_map/pallas_call | solution.py:381
  53.9 1.5 %collective-permute-start.7 = (bf16[64,1024]{1,0:T(8,128)(2,1)S(1)}, bf16[64,1024]{1,0:T(8,128)(2,1)S(1)}, u32[]{:S(2)}, u32[]{:S(2)}) collective-permute-start(bf16[64,1024]{1,0:T(8,128)(2,1)S(1)} %get-tuple-element.36.refs_0_), channel_id=1, source_target_pairs={{0,2},{1,3},{2,0},{3,1},{4,6},{5,7},{6,4},{7,5},{8,10},{9,11},{10,... | collective-permute-start | bytes 393224 | tf_op jit(solution)/shard_map/ppermute | solution.py:377
  55.4 2.2 %collective-permute-done.2.rho_far.refs_5_ = bf16[288,512]{1,0:T(8,128)(2,1)S(1)} collective-permute-done((bf16[288,512]{1,0:T(8,128)(2,1)S(1)}, bf16[288,512]{1,0:T(8,128)(2,1)S(1)}, u32[]{:S(2)}, u32[]{:S(2)}) %collective-permute-start.2) | collective-permute-done | bytes 294944 | tf_op jit(solution)/shard_map/ppermute | solution.py:377
  57.6 1.4 %shard_map.68 = (f32[64,1024]{1,0:T(8,128)S(1)}, f32[64,1024]{1,0:T(8,128)S(1)}, bf16[64,1024]{1,0:T(8,128)(2,1)S(1)}, bf16[64,1024]{1,0:T(8,128)(2,1)S(1)}) custom-call(bf16[64,256]{1,0:T(8,128)(2,1)S(1)} %squeeze.19.refs_2_.vec_own, bf16[256,512]{1,0:T(8,128)(2,1)S(1)} %get-tuple-element.28.rho_own.refs_4_, ...), custom_call_target="tpu_custom_call" | custom-call | bytes 1 | tf_op jit(solution)/shard_map/pallas_call | solution.py:381
  59.0 0.1 collective-permute-start.3
  59.1 0.5 collective-permute-start.6
  59.6 0.2 collective-permute-done.7.refs_2_
  59.8 0.0 collective-permute-start.8
  59.8 0.5 collective-permute-start.5
  60.3 0.1 collective-permute-done.3
  60.5 0.0 copy-start.2
  60.5 0.8 collective-permute-start.4
  61.3 0.0 collective-permute-done.6.refs_1_
  61.3 0.0 collective-permute-done.8.refs_3_
  61.3 2.0 %shard_map.69 = (f32[2,2,16,256]{3,2,1,0:T(8,128)S(1)}, bf16[2,2,16,256]{3,2,1,0:T(8,128)(2,1)S(1)}) custom-call(bf16[64,1024]{1,0:T(8,128)(2,1)S(1)} %get-tuple-element.36.refs_0_, bf16[64,1024]{1,0:T(8,128)(2,1)S(1)} %collective-permute-done.6.refs_1_, bf16[64,1024]{1,0:T(8,128)(2,1)S(1)} %collective-permute-done.7.refs_2_, ...), custom_call_target="tpu_custom_call" | custom-call | bytes 1 | tf_op jit(solution)/shard_map/pallas_call | solution.py:381
  63.3 0.0 collective-permute-done.5.refs_0_
  63.3 2.8 %collective-permute-done.4.q_far = bf16[64,1024]{1,0:T(8,128)(2,1)S(1)} collective-permute-done((bf16[64,1024]{1,0:T(8,128)(2,1)S(1)}, bf16[64,1024]{1,0:T(8,128)(2,1)S(1)}, u32[]{:S(2)}, u32[]{:S(2)}) %collective-permute-start.4) | collective-permute-done | bytes 131104 | tf_op jit(solution)/shard_map/ppermute | solution.py:377
  66.1 0.7 shard_map.70
  66.8 0.1 collective-permute-start.9
  66.9 1.2 %collective-permute-done.9.refs_0_ = bf16[3,2,16,256]{3,2,1,0:T(8,128)(2,1)S(1)} collective-permute-done((bf16[3,2,16,256]{3,2,1,0:T(8,128)(2,1)S(1)}, bf16[3,2,16,256]{3,2,1,0:T(8,128)(2,1)S(1)}, u32[]{:S(2)}, u32[]{:S(2)}) %collective-permute-start.9) | collective-permute-done | bytes 49184 | tf_op jit(solution)/shard_map/ppermute | solution.py:377
  68.1 0.0 copy-done.2
  68.1 0.7 shard_map.71
  68.8 15.9 %all_to_all.10 = bf16[16,2,16,256]{3,2,1,0:T(8,128)(2,1)S(1)} all-to-all(bf16[16,2,16,256]{3,2,1,0:T(8,128)(2,1)S(1)} %shard_map.71), channel_id=1, replica_groups={{0,2,4,6,8,10,12,14,16,18,20,22,24,26,28,30},{1,3,5,7,9,11,13,15,17,19,..., dimensions={0} | all-to-all | bytes 524288 | tf_op jit(solution)/shard_map/all_to_all | solution.py:374
  84.7 0.7 convert_reduce_fusion
  (5 shorter events, 0.1 us)
Async XLA Ops:
  3.6 34.1 %all-to-all-start = ((bf16[16,2,4,4352]{3,2,1,0:T(4,128)(2,1)}), bf16[16,2,4,4352]{3,2,1,0:T(4,128)(2,1)S(1)}, u32[]{:S(2)}, u32[]{:S(2)}) async-start(bf16[16,2,4,4352]{3,2,1,0:T(4,128)(2,1)} %shard_map.64), calls=%async_computation | async-start | bytes 2228224 | tf_op jit(solution)/shard_map/all_to_all | solution.py:374
  13.5 9.4 %copy-start.3 = (s32[32]{0:T(128)S(1)}, s32[32]{0:T(128)}, u32[]{:S(2)}) copy-start(s32[32]{0:T(128)} %param.10) | copy-start | bytes 388
  18.4 4.5 %copy-start = (bf16[12288,512]{1,0:T(8,128)(2,1)}, bf16[12288,512]{1,0:T(8,128)(2,1)S(1)}, u32[]{:S(2)}) copy-start(bf16[12288,512]{1,0:T(8,128)(2,1)S(1)} %shard_map.65.refs_3_) | copy-start | bytes 37748740
  39.1 2.0 %collective-permute-start = (bf16[2,32,4096]{2,1,0:T(8,128)(2,1)S(1)}, bf16[2,32,4096]{2,1,0:T(8,128)(2,1)S(1)}, u32[]{:S(2)}, u32[]{:S(2)}) collective-permute-start(bf16[2,32,4096]{2,1,0:T(8,128)(2,1)S(1)} %get-tuple-element.42.refs_0_), channel_id=1, source_target_pairs={{0,1},{1,0},{2,3},{3,2},{4,5},{5,4},{6,7},{7,6},{8,9},{9,8},{10,11... | collective-permute-start | bytes 1572872 | tf_op jit(solution)/shard_map/ppermute | solution.py:377
  39.2 9.3 %collective-permute-start.1 = (bf16[2,32,4096]{2,1,0:T(8,128)(2,1)S(1)}, bf16[2,32,4096]{2,1,0:T(8,128)(2,1)S(1)}, u32[]{:S(2)}, u32[]{:S(2)}) collective-permute-start(bf16[2,32,4096]{2,1,0:T(8,128)(2,1)S(1)} %get-tuple-element.41.refs_0_), channel_id=1, source_target_pairs={{0,1},{1,0},{2,3},{3,2},{4,5},{5,4},{6,7},{7,6},{8,9},{9,8},{10,11... | collective-permute-start | bytes 1572872 | tf_op jit(solution)/shard_map/ppermute | solution.py:377
  39.8 8.7 %copy-start.1 = (bf16[2,512,2048]{2,1,0:T(8,128)(2,1)S(1)}, bf16[2,512,2048]{2,1,0:T(8,128)(2,1)}, u32[]{:S(2)}) copy-start(bf16[2,512,2048]{2,1,0:T(8,128)(2,1)} %refs_4_.1) | copy-start | bytes 12582916
  47.9 9.7 %collective-permute-start.2 = (bf16[288,512]{1,0:T(8,128)(2,1)S(1)}, bf16[288,512]{1,0:T(8,128)(2,1)S(1)}, u32[]{:S(2)}, u32[]{:S(2)}) collective-permute-start(bf16[288,512]{1,0:T(8,128)(2,1)S(1)} %get-tuple-element.29), channel_id=1, source_target_pairs={{0,2},{1,3},{2,0},{3,1},{4,6},{5,7},{6,4},{7,5},{8,10},{9,11},{10,... | collective-permute-start | bytes 884744 | tf_op jit(solution)/shard_map/ppermute | solution.py:377
  53.9 5.9 %collective-permute-start.7 = (bf16[64,1024]{1,0:T(8,128)(2,1)S(1)}, bf16[64,1024]{1,0:T(8,128)(2,1)S(1)}, u32[]{:S(2)}, u32[]{:S(2)}) collective-permute-start(bf16[64,1024]{1,0:T(8,128)(2,1)S(1)} %get-tuple-element.36.refs_0_), channel_id=1, source_target_pairs={{0,2},{1,3},{2,0},{3,1},{4,6},{5,7},{6,4},{7,5},{8,10},{9,11},{10,... | collective-permute-start | bytes 393224 | tf_op jit(solution)/shard_map/ppermute | solution.py:377
  59.0 1.4 %collective-permute-start.3 = (bf16[64,1024]{1,0:T(8,128)(2,1)S(1)}, bf16[64,1024]{1,0:T(8,128)(2,1)S(1)}, u32[]{:S(2)}, u32[]{:S(2)}) collective-permute-start(bf16[64,1024]{1,0:T(8,128)(2,1)S(1)} %get-tuple-element.33), channel_id=1, source_target_pairs={{0,1},{1,0},{2,3},{3,2},{4,5},{5,4},{6,7},{7,6},{8,9},{9,8},{10,11... | collective-permute-start | bytes 393224 | tf_op jit(solution)/shard_map/ppermute | solution.py:377
  59.1 2.2 %collective-permute-start.6 = (bf16[64,1024]{1,0:T(8,128)(2,1)S(1)}, bf16[64,1024]{1,0:T(8,128)(2,1)S(1)}, u32[]{:S(2)}, u32[]{:S(2)}) collective-permute-start(bf16[64,1024]{1,0:T(8,128)(2,1)S(1)} %get-tuple-element.36.refs_0_), channel_id=1, source_target_pairs={{0,1},{1,0},{2,3},{3,2},{4,5},{5,4},{6,7},{7,6},{8,9},{9,8},{10,11... | collective-permute-start | bytes 393224 | tf_op jit(solution)/shard_map/ppermute | solution.py:377
  59.8 1.5 %collective-permute-start.8 = (bf16[64,1024]{1,0:T(8,128)(2,1)S(1)}, bf16[64,1024]{1,0:T(8,128)(2,1)S(1)}, u32[]{:S(2)}, u32[]{:S(2)}) collective-permute-start(bf16[64,1024]{1,0:T(8,128)(2,1)S(1)} %collective-permute-done.7.refs_2_), channel_id=1, source_target_pairs={{0,1},{1,0},{2,3},{3,2},{4,5},{5,4},{6,7},{7,6},{8,9},{9,8},{10,11... | collective-permute-start | bytes 393224 | tf_op jit(solution)/shard_map/ppermute | solution.py:377
  59.8 3.5 %collective-permute-start.5 = (bf16[64,1024]{1,0:T(8,128)(2,1)S(1)}, bf16[64,1024]{1,0:T(8,128)(2,1)S(1)}, u32[]{:S(2)}, u32[]{:S(2)}) collective-permute-start(bf16[64,1024]{1,0:T(8,128)(2,1)S(1)} %get-tuple-element.34), channel_id=1, source_target_pairs={{0,1},{1,0},{2,3},{3,2},{4,5},{5,4},{6,7},{7,6},{8,9},{9,8},{10,11... | collective-permute-start | bytes 393224 | tf_op jit(solution)/shard_map/ppermute | solution.py:377
  60.5 7.6 %copy-start.2 = (s32[16,2]{0,1:T(2,128)S(1)}, s32[16,2]{0,1:T(2,128)}, u32[]{:S(2)}) copy-start(s32[16,2]{0,1:T(2,128)} %param.9) | copy-start | bytes 388
  60.5 5.6 %collective-permute-start.4 = (bf16[64,1024]{1,0:T(8,128)(2,1)S(1)}, bf16[64,1024]{1,0:T(8,128)(2,1)S(1)}, u32[]{:S(2)}, u32[]{:S(2)}) collective-permute-start(bf16[64,1024]{1,0:T(8,128)(2,1)S(1)} %add_convert_fusion), channel_id=1, source_target_pairs={{0,2},{1,3},{2,0},{3,1},{4,6},{5,7},{6,4},{7,5},{8,10},{9,11},{10,... | collective-permute-start | bytes 393224 | tf_op jit(solution)/shard_map/ppermute | solution.py:377
  66.8 1.3 %collective-permute-start.9 = (bf16[3,2,16,256]{3,2,1,0:T(8,128)(2,1)S(1)}, bf16[3,2,16,256]{3,2,1,0:T(8,128)(2,1)S(1)}, u32[]{:S(2)}, u32[]{:S(2)}) collective-permute-start(bf16[3,2,16,256]{3,2,1,0:T(8,128)(2,1)S(1)} %get-tuple-element.40), channel_id=1, source_target_pairs={{0,1},{1,0},{2,3},{3,2},{4,5},{5,4},{6,7},{7,6},{8,9},{9,8},{10,11... | collective-permute-start | bytes 147464 | tf_op jit(solution)/shard_map/ppermute | solution.py:377

commit v6 on v5

--- a/solution.py
+++ b/solution.py
@@ -254,27 +254,23 @@
     return dot(dot(vec[...], rho).astype(BF16), order).astype(BF16)
 
 
-def back_kernel(vec_own, rho_own, rho_far, screened, q_keep, q_part, *q_msgs):
-    shifts = len(q_msgs) // 2 + 1
+def back_kernel(*refs, shifts, rel):
+    *vec, rho, screened = refs[: 3 - rel]
+    outs = refs[3 - rel :]
     j, x = place(shifts)
-    width = rho_own.shape[1]
-    order = interleave(width)
-    for rel in range(2):
-        pair = x if rel == 0 else 1 - x
-        if rel:
-            vec = pack(rho_far[NV * NC :, :], vec_own.shape[1])
-            first = project(vec, rho_far[: NV * NC, :], order)
-        else:
-            first = project(vec_own, rho_own[...], order)
-        for s in range(shifts):
-            for c in range(2):
-                start = pl.multiple_of((c * shifts + (j ^ s)) * width, width)
-                term = dot(first, screened[pair, :, pl.ds(start, width)])
-                cols = slice(c * width, (c + 1) * width)
-                if s == 0:
-                    (q_part if rel else q_keep)[:, cols] = term
-                else:
-                    q_msgs[2 * (s - 1) + rel][:, cols] = term.astype(BF16)
+    width = rho.shape[1]
+    pair = 1 - x if rel else x
+    products = rho[: NV * NC, :]
+    if rel:
+        vectors = pack(rho[NV * NC :, :], rho.shape[1] * (rho.shape[0] - NV * NC) // outs[0].shape[0])
+    else:
+        vectors = vec[0][...]
+    first = dot(dot(vectors, products).astype(BF16), interleave(width)).astype(BF16)
+    for s in range(shifts):
+        for c in range(2):
+            start = pl.multiple_of((c * shifts + (j ^ s)) * width, width)
+            term = dot(first, screened[pair, :, pl.ds(start, width)])
+            outs[s][:, c * width : (c + 1) * width] = term.astype(outs[s].dtype)
 
 
 def cut(value, scratch, outs):
@@ -415,7 +411,7 @@
     vec = got[..., chunk:].transpose(2, 0, 1, 3, 4).reshape(2, vec_count, transitions)
     picker = (band_order[:, None] == jnp.arange(bands, dtype=jnp.int32)[None, :]).astype(BF16)
     half_waves = own_waves // 2
-    block = min(1024, chunk)
+    block = min(2048, chunk)
     (table,) = call(
         functools.partial(table_kernel, block=block, chunk=chunk),
         [like((3 * points // 4, half_waves), BF16)],
@@ -423,12 +419,15 @@
         flops=3 * points * half_waves,
     )
     picker, table = lax.optimization_barrier((picker, table))
-    psi = jnp.einsum(
-        "gbn,gxlbr->lxnr",
-        picker.reshape(groups, band_here, bands),
-        got[..., :chunk],
-        preferred_element_type=F32,
-    ).astype(BF16)
+    psi = [
+        jnp.einsum(
+            "gbn,gxbr->xnr",
+            picker.reshape(groups, band_here, bands),
+            got[:, :, slot, :, :chunk],
+            preferred_element_type=F32,
+        ).astype(BF16)
+        for slot in range(2)
+    ]
     products = NV * NC
 
     def transform(slot, outs, *args):
@@ -468,18 +467,24 @@
     fars = [shift(far, s) for s in range(1, halves)]
     flops = 4 * vec_count * width * waves
     partial_q = like((vec_count, own_waves), F32)
-    q_keep, q_part, *q_msgs = call(
-        back_kernel,
-        [partial_q] * 2 + [like((vec_count, own_waves), BF16)] * (2 * (halves - 1)),
+    q_outs = [partial_q] + [like((vec_count, own_waves), BF16)] * (halves - 1)
+    q_keep, *q_near = call(
+        functools.partial(back_kernel, shifts=halves, rel=0),
+        q_outs,
         vec[0],
         rho_own,
+        screened,
+        cost=1,
+    )
+    rho_far, q_keep = lax.optimization_barrier((rho_far, q_keep))
+    q_part, *q_msgs = call(
+        functools.partial(back_kernel, shifts=halves, rel=1),
+        q_outs,
         rho_far,
         screened,
         cost=1,
     )
-    received = [
-        [shift(q_msgs[2 * (s - 1) + rel], s) for s in range(1, halves)] for rel in range(2)
-    ]
+    received = [[shift(v, s + 1) for s, v in enumerate(part)] for part in (q_near, q_msgs)]
     q_send = (q_part + sum(v.astype(F32) for v in received[1])).astype(BF16)
     q_far = shift(q_send, halves)
     vec_rows = vec_count // columns

time: 85.6 us -> 84.8 us (level)
    pallas_call x6 -> x7, Pallas kernels: 21.2 us -> 21 us  [call(): pl.pallas_call(kernel, in_specs=[vmem] * (len(args) - far) + [hbm] * far,...]
  transfers between devices with their start and end apart: 11 -> 11, of which waited for: 7 -> 7; matrix products, arithmetic and copies ran while one was open for 2% -> 3% of each run, Pallas kernels for 24% -> 24%
where the time goes in v6:
time: 84.8 us; the launch traced here: 84.4 us
  Pallas kernels  25 us (29%)
  waiting for transfers between devices  22 us (26%)
  blocking collectives  16.2 us (19%)
  starting transfers between devices  12.7 us (15%)
  local copies, waits for them, and re-layouts  6.68 us (8%)
  matrix products  0.85 us (1%)
    pallas_call x7, Pallas kernels, call(): pl.pallas_call(kernel, in_specs=[vmem] * (len(args) - far) + [hbm] * far,...  21 us
    all_to_all x1, blocking collectives, exchange(): lax.all_to_all(value, both, 0, 0, tiled=True, axis_index_groups=members)  16.2 us
    all_to_all x1, waiting for transfers between devices, exchange(): lax.all_to_all(value, both, 0, 0, tiled=True, axis_index_groups=members)  14.7 us
    all_to_all x1, starting transfers between devices, exchange(): lax.all_to_all(value, both, 0, 0, tiled=True, axis_index_groups=members)  8.32 us
    ppermute x10, waiting for transfers between devices, shift(): return lax.ppermute(value, 'pw', [(i, i ^ s) for i in range(columns)])  7.26 us
    unnamed x8, local copies, waits for them, and re-layouts  4.54 us
    ppermute x10, starting transfers between devices, shift(): return lax.ppermute(value, 'pw', [(i, i ^ s) for i in range(columns)])  4.4 us
    pallas_call x1, Pallas kernels, local(): pl.pallas_call(functools.partial(gather_kernel, halves=halves), in_specs=...  3.29 us
  transfers between devices with their start and end apart: 11, of which 7 were waited for; matrix products, arithmetic and copies ran while one was open for 3% of the time, Pallas kernels for 24%

profile of v6, /device:TPU:0, one launch (start us, length us, event | category | flops | bytes accessed | tf_op | source)
XLA Modules:
  0.0 84.4 jit_solution(12654154548162971756)
XLA Ops:
  0.0 3.3 %shard_map.64 = bf16[16,2,4,4352]{3,2,1,0:T(4,128)(2,1)} custom-call(s32[2,16]{1,0:T(2,128)} %bitcast.37, bf16[16,4,4096]{2,1,0:T(4,128)(2,1)} %orbitals.1, bf16[16,8,256]{2,1,0:T(8,128)(2,1)} %far_vectors.1), custom_call_target="tpu_custom_call" | custom-call | tf_op jit(solution)/shard_map/pallas_call | solution.py:393
  3.3 8.3 %all-to-all-start = ((bf16[16,2,4,4352]{3,2,1,0:T(4,128)(2,1)}), bf16[16,2,4,4352]{3,2,1,0:T(4,128)(2,1)S(1)}, u32[]{:S(2)}, u32[]{:S(2)}) async-start(bf16[16,2,4,4352]{3,2,1,0:T(4,128)(2,1)} %shard_map.64), calls=%async_computation | async-start | bytes 2228224 | tf_op jit(solution)/shard_map/all_to_all | solution.py:370
  11.6 1.5 %dynamic-slice_bitcast_fusion.seeds = f32[2,192,1024]{2,1,0:T(8,128)S(1)} fusion(f32[2,2,192,1024]{3,2,1,0:T(8,128)} %constant.25.clone, s32[]{:T(128)S(6)} %select_n.12), kind=kLoop, calls=%fused_computation.6 | loop fusion | bytes 3145732 | tf_op jit(solution)/shard_map/jit(dynamic_index_in_dim)/squeeze | solution.py:408
  13.2 0.0 copy-start.3
  13.2 4.9 %shard_map.65.refs_3_ = bf16[12288,512]{1,0:T(8,128)(2,1)S(1)} custom-call(f32[2,192,1024]{2,1,0:T(8,128)S(1)} %dynamic-slice_bitcast_fusion.seeds), custom_call_target="tpu_custom_call" | custom-call | flops 25165824 | bytes 14155776 | tf_op jit(solution)/shard_map/pallas_call | solution.py:377
  18.0 0.0 copy-start
  18.1 4.5 %copy-done = bf16[12288,512]{1,0:T(8,128)(2,1)} copy-done((bf16[12288,512]{1,0:T(8,128)(2,1)}, bf16[12288,512]{1,0:T(8,128)(2,1)S(1)}, u32[]{:S(2)}) %copy-start) | copy-done | bytes 12582936
  22.6 0.0 copy-done.3
  22.6 0.1 fusion.4
  22.7 14.7 %all-to-all-done = bf16[16,2,4,4352]{3,2,1,0:T(4,128)(2,1)S(1)} async-done(((bf16[16,2,4,4352]{3,2,1,0:T(4,128)(2,1)}), bf16[16,2,4,4352]{3,2,1,0:T(4,128)(2,1)S(1)}, u32[]{:S(2)}, u32[]{:S(2)}) %all-to-all-start) | async-done | bytes 1114144 | tf_op jit(solution)/shard_map/all_to_all | solution.py:370
  37.4 0.5 fusion.9
  37.9 0.4 fusion.3.refs_0_
  38.3 0.1 collective-permute-start
  38.4 0.4 fusion.2.refs_0_
  38.9 0.6 collective-permute-start.2
  39.5 0.8 collective-permute-done.refs_1_
  40.3 0.0 copy-start.1
  40.3 6.6 %shard_map.66 = (bf16[256,512]{1,0:T(8,128)(2,1)S(1)}, bf16[288,512]{1,0:T(8,128)(2,1)S(1)}, bf16[12288,512]{1,0:T(8,128)(2,1)S(1)}) custom-call(bf16[2,32,4096]{2,1,0:T(8,128)(2,1)S(1)} %fusion.3.refs_0_, bf16[2,32,4096]{2,1,0:T(8,128)(2,1)S(1)} %collective-permute-done.refs_1_, bf16[64,256]{1,0:T(8,128)(2,1)S(1)} %squeeze.19.refs_2_.refs_0_, ...), custom_call_target="tpu_custom_call" | custom-call | flops 4294967296 | bytes 26804224 | tf_op jit(solution)/shard_map/pallas_call | solution.py:377
  46.9 0.6 collective-permute-start.1
  47.5 0.0 collective-permute-done.2.refs_1_
  47.5 0.0 copy-done.1
  47.5 5.3 %shard_map.67 = (bf16[256,1024]{1,0:T(8,128)(2,1)S(1)}, bf16[64,1024]{1,0:T(8,128)(2,1)S(1)}, bf16[2,512,2048]{2,1,0:T(8,128)(2,1)S(1)}) custom-call(bf16[2,32,4096]{2,1,0:T(8,128)(2,1)S(1)} %fusion.2.refs_0_, bf16[2,32,4096]{2,1,0:T(8,128)(2,1)S(1)} %collective-permute-done.2.refs_1_, bf16[64,256]{1,0:T(8,128)(2,1)S(1)} %squeeze.21.refs_2_, ...), custom_call_target="tpu_custom_call" | custom-call | flops 4294967296 | bytes 22708224 | tf_op jit(solution)/shard_map/pallas_call | solution.py:377
  52.9 1.5 %collective-permute-start.7 = (bf16[64,1024]{1,0:T(8,128)(2,1)S(1)}, bf16[64,1024]{1,0:T(8,128)(2,1)S(1)}, u32[]{:S(2)}, u32[]{:S(2)}) collective-permute-start(bf16[64,1024]{1,0:T(8,128)(2,1)S(1)} %get-tuple-element.40.refs_0_), channel_id=1, source_target_pairs={{0,2},{1,3},{2,0},{3,1},{4,6},{5,7},{6,4},{7,5},{8,10},{9,11},{10,... | collective-permute-start | bytes 393224 | tf_op jit(solution)/shard_map/ppermute | solution.py:373
  54.4 0.8 shard_map.68
  55.2 1.4 %collective-permute-done.1.refs_0_.refs_5_ = bf16[288,512]{1,0:T(8,128)(2,1)S(1)} collective-permute-done((bf16[288,512]{1,0:T(8,128)(2,1)S(1)}, bf16[288,512]{1,0:T(8,128)(2,1)S(1)}, u32[]{:S(2)}, u32[]{:S(2)}) %collective-permute-start.1) | collective-permute-done | bytes 294944 | tf_op jit(solution)/shard_map/ppermute | solution.py:373
  56.6 0.8 shard_map.69
  57.4 0.1 collective-permute-start.3
  57.4 0.5 collective-permute-start.6
  57.9 0.1 collective-permute-start.5
  58.0 0.8 collective-permute-done.7.refs_2_
  58.8 0.0 collective-permute-start.8
  58.8 0.0 collective-permute-done.3
  58.9 0.0 copy-start.2
  58.9 0.9 %collective-permute-start.4 = (bf16[64,1024]{1,0:T(8,128)(2,1)S(1)}, bf16[64,1024]{1,0:T(8,128)(2,1)S(1)}, u32[]{:S(2)}, u32[]{:S(2)}) collective-permute-start(bf16[64,1024]{1,0:T(8,128)(2,1)S(1)} %add_convert_fusion), channel_id=1, source_target_pairs={{0,2},{1,3},{2,0},{3,1},{4,6},{5,7},{6,4},{7,5},{8,10},{9,11},{10,... | collective-permute-start | bytes 393224 | tf_op jit(solution)/shard_map/ppermute | solution.py:373
  59.8 0.0 collective-permute-done.6.refs_1_
  59.8 0.4 collective-permute-done.8.refs_3_
  60.2 2.0 %shard_map.70 = (f32[2,2,16,256]{3,2,1,0:T(8,128)S(1)}, bf16[2,2,16,256]{3,2,1,0:T(8,128)(2,1)S(1)}) custom-call(bf16[64,1024]{1,0:T(8,128)(2,1)S(1)} %get-tuple-element.40.refs_0_, bf16[64,1024]{1,0:T(8,128)(2,1)S(1)} %collective-permute-done.6.refs_1_, bf16[64,1024]{1,0:T(8,128)(2,1)S(1)} %collective-permute-done.7.refs_2_, ...), custom_call_target="tpu_custom_call" | custom-call | bytes 1 | tf_op jit(solution)/shard_map/pallas_call | solution.py:377
  62.2 0.0 collective-permute-done.5.refs_0_
  62.2 2.6 %collective-permute-done.4.q_far = bf16[64,1024]{1,0:T(8,128)(2,1)S(1)} collective-permute-done((bf16[64,1024]{1,0:T(8,128)(2,1)S(1)}, bf16[64,1024]{1,0:T(8,128)(2,1)S(1)}, u32[]{:S(2)}, u32[]{:S(2)}) %collective-permute-start.4) | collective-permute-done | bytes 131104 | tf_op jit(solution)/shard_map/ppermute | solution.py:373
  64.9 0.7 shard_map.71
  65.6 0.1 collective-permute-start.9
  65.6 1.2 %collective-permute-done.9.refs_0_ = bf16[3,2,16,256]{3,2,1,0:T(8,128)(2,1)S(1)} collective-permute-done((bf16[3,2,16,256]{3,2,1,0:T(8,128)(2,1)S(1)}, bf16[3,2,16,256]{3,2,1,0:T(8,128)(2,1)S(1)}, u32[]{:S(2)}, u32[]{:S(2)}) %collective-permute-start.9) | collective-permute-done | bytes 49184 | tf_op jit(solution)/shard_map/ppermute | solution.py:373
  66.9 0.0 copy-done.2
  66.9 0.7 shard_map.72
  67.6 16.2 %all_to_all.10 = bf16[16,2,16,256]{3,2,1,0:T(8,128)(2,1)S(1)} all-to-all(bf16[16,2,16,256]{3,2,1,0:T(8,128)(2,1)S(1)} %shard_map.72), channel_id=1, replica_groups={{0,2,4,6,8,10,12,14,16,18,20,22,24,26,28,30},{1,3,5,7,9,11,13,15,17,19,..., dimensions={0} | all-to-all | bytes 524288 | tf_op jit(solution)/shard_map/all_to_all | solution.py:370
  83.8 0.7 convert_reduce_fusion
  (5 shorter events, 0.1 us)
Async XLA Ops:
  3.3 34.1 %all-to-all-start = ((bf16[16,2,4,4352]{3,2,1,0:T(4,128)(2,1)}), bf16[16,2,4,4352]{3,2,1,0:T(4,128)(2,1)S(1)}, u32[]{:S(2)}, u32[]{:S(2)}) async-start(bf16[16,2,4,4352]{3,2,1,0:T(4,128)(2,1)} %shard_map.64), calls=%async_computation | async-start | bytes 2228224 | tf_op jit(solution)/shard_map/all_to_all | solution.py:370
  13.2 9.4 %copy-start.3 = (s32[32]{0:T(128)S(1)}, s32[32]{0:T(128)}, u32[]{:S(2)}) copy-start(s32[32]{0:T(128)} %param.10) | copy-start | bytes 388
  18.0 4.5 %copy-start = (bf16[12288,512]{1,0:T(8,128)(2,1)}, bf16[12288,512]{1,0:T(8,128)(2,1)S(1)}, u32[]{:S(2)}) copy-start(bf16[12288,512]{1,0:T(8,128)(2,1)S(1)} %shard_map.65.refs_3_) | copy-start | bytes 37748740
  38.3 2.0 %collective-permute-start = (bf16[2,32,4096]{2,1,0:T(8,128)(2,1)S(1)}, bf16[2,32,4096]{2,1,0:T(8,128)(2,1)S(1)}, u32[]{:S(2)}, u32[]{:S(2)}) collective-permute-start(bf16[2,32,4096]{2,1,0:T(8,128)(2,1)S(1)} %fusion.3.refs_0_), channel_id=1, source_target_pairs={{0,1},{1,0},{2,3},{3,2},{4,5},{5,4},{6,7},{7,6},{8,9},{9,8},{10,11... | collective-permute-start | bytes 1572872 | tf_op jit(solution)/shard_map/ppermute | solution.py:373
  38.9 8.7 %collective-permute-start.2 = (bf16[2,32,4096]{2,1,0:T(8,128)(2,1)S(1)}, bf16[2,32,4096]{2,1,0:T(8,128)(2,1)S(1)}, u32[]{:S(2)}, u32[]{:S(2)}) collective-permute-start(bf16[2,32,4096]{2,1,0:T(8,128)(2,1)S(1)} %fusion.2.refs_0_), channel_id=1, source_target_pairs={{0,1},{1,0},{2,3},{3,2},{4,5},{5,4},{6,7},{7,6},{8,9},{9,8},{10,11... | collective-permute-start | bytes 1572872 | tf_op jit(solution)/shard_map/ppermute | solution.py:373
  40.3 7.2 %copy-start.1 = (bf16[2,512,2048]{2,1,0:T(8,128)(2,1)S(1)}, bf16[2,512,2048]{2,1,0:T(8,128)(2,1)}, u32[]{:S(2)}) copy-start(bf16[2,512,2048]{2,1,0:T(8,128)(2,1)} %refs_4_.1) | copy-start | bytes 12582916
  46.9 9.7 %collective-permute-start.1 = (bf16[288,512]{1,0:T(8,128)(2,1)S(1)}, bf16[288,512]{1,0:T(8,128)(2,1)S(1)}, u32[]{:S(2)}, u32[]{:S(2)}) collective-permute-start(bf16[288,512]{1,0:T(8,128)(2,1)S(1)} %get-tuple-element.27), channel_id=1, source_target_pairs={{0,2},{1,3},{2,0},{3,1},{4,6},{5,7},{6,4},{7,5},{8,10},{9,11},{10,... | collective-permute-start | bytes 884744 | tf_op jit(solution)/shard_map/ppermute | solution.py:373
  52.9 6.0 %collective-permute-start.7 = (bf16[64,1024]{1,0:T(8,128)(2,1)S(1)}, bf16[64,1024]{1,0:T(8,128)(2,1)S(1)}, u32[]{:S(2)}, u32[]{:S(2)}) collective-permute-start(bf16[64,1024]{1,0:T(8,128)(2,1)S(1)} %get-tuple-element.40.refs_0_), channel_id=1, source_target_pairs={{0,2},{1,3},{2,0},{3,1},{4,6},{5,7},{6,4},{7,5},{8,10},{9,11},{10,... | collective-permute-start | bytes 393224 | tf_op jit(solution)/shard_map/ppermute | solution.py:373
  57.4 1.5 %collective-permute-start.3 = (bf16[64,1024]{1,0:T(8,128)(2,1)S(1)}, bf16[64,1024]{1,0:T(8,128)(2,1)S(1)}, u32[]{:S(2)}, u32[]{:S(2)}) collective-permute-start(bf16[64,1024]{1,0:T(8,128)(2,1)S(1)} %get-tuple-element.37), channel_id=1, source_target_pairs={{0,1},{1,0},{2,3},{3,2},{4,5},{5,4},{6,7},{7,6},{8,9},{9,8},{10,11... | collective-permute-start | bytes 393224 | tf_op jit(solution)/shard_map/ppermute | solution.py:373
  57.4 2.3 %collective-permute-start.6 = (bf16[64,1024]{1,0:T(8,128)(2,1)S(1)}, bf16[64,1024]{1,0:T(8,128)(2,1)S(1)}, u32[]{:S(2)}, u32[]{:S(2)}) collective-permute-start(bf16[64,1024]{1,0:T(8,128)(2,1)S(1)} %get-tuple-element.40.refs_0_), channel_id=1, source_target_pairs={{0,1},{1,0},{2,3},{3,2},{4,5},{5,4},{6,7},{7,6},{8,9},{9,8},{10,11... | collective-permute-start | bytes 393224 | tf_op jit(solution)/shard_map/ppermute | solution.py:373
  57.9 4.3 %collective-permute-start.5 = (bf16[64,1024]{1,0:T(8,128)(2,1)S(1)}, bf16[64,1024]{1,0:T(8,128)(2,1)S(1)}, u32[]{:S(2)}, u32[]{:S(2)}) collective-permute-start(bf16[64,1024]{1,0:T(8,128)(2,1)S(1)} %get-tuple-element.38), channel_id=1, source_target_pairs={{0,1},{1,0},{2,3},{3,2},{4,5},{5,4},{6,7},{7,6},{8,9},{9,8},{10,11... | collective-permute-start | bytes 393224 | tf_op jit(solution)/shard_map/ppermute | solution.py:373
  58.8 1.3 %collective-permute-start.8 = (bf16[64,1024]{1,0:T(8,128)(2,1)S(1)}, bf16[64,1024]{1,0:T(8,128)(2,1)S(1)}, u32[]{:S(2)}, u32[]{:S(2)}) collective-permute-start(bf16[64,1024]{1,0:T(8,128)(2,1)S(1)} %collective-permute-done.7.refs_2_), channel_id=1, source_target_pairs={{0,1},{1,0},{2,3},{3,2},{4,5},{5,4},{6,7},{7,6},{8,9},{9,8},{10,11... | collective-permute-start | bytes 393224 | tf_op jit(solution)/shard_map/ppermute | solution.py:373
  58.9 8.0 %copy-start.2 = (s32[16,2]{0,1:T(2,128)S(1)}, s32[16,2]{0,1:T(2,128)}, u32[]{:S(2)}) copy-start(s32[16,2]{0,1:T(2,128)} %param.9) | copy-start | bytes 388
  58.9 6.0 %collective-permute-start.4 = (bf16[64,1024]{1,0:T(8,128)(2,1)S(1)}, bf16[64,1024]{1,0:T(8,128)(2,1)S(1)}, u32[]{:S(2)}, u32[]{:S(2)}) collective-permute-start(bf16[64,1024]{1,0:T(8,128)(2,1)S(1)} %add_convert_fusion), channel_id=1, source_target_pairs={{0,2},{1,3},{2,0},{3,1},{4,6},{5,7},{6,4},{7,5},{8,10},{9,11},{10,... | collective-permute-start | bytes 393224 | tf_op jit(solution)/shard_map/ppermute | solution.py:373
  65.6 1.3 %collective-permute-start.9 = (bf16[3,2,16,256]{3,2,1,0:T(8,128)(2,1)S(1)}, bf16[3,2,16,256]{3,2,1,0:T(8,128)(2,1)S(1)}, u32[]{:S(2)}, u32[]{:S(2)}) collective-permute-start(bf16[3,2,16,256]{3,2,1,0:T(8,128)(2,1)S(1)} %get-tuple-element.44), channel_id=1, source_target_pairs={{0,1},{1,0},{2,3},{3,2},{4,5},{5,4},{6,7},{7,6},{8,9},{9,8},{10,11... | collective-permute-start | bytes 147464 | tf_op jit(solution)/shard_map/ppermute | solution.py:373

commit v7 on v6

--- a/solution.py
+++ b/solution.py
@@ -157,9 +157,12 @@
     table_copies = []
     if slot == 0:
         vec, far_table, rho_own, rho_msg, table, sem = *refs[:5], refs[-1]
-        for t in range(sem.shape[0]):
-            span = pl.ds(t * (table.shape[0] // sem.shape[0]), table.shape[0] // sem.shape[0])
-            table_copies.append(pltpu.make_async_copy(far_table.at[span], table.at[span], sem.at[t]))
+        for i in range(3 * sem.shape[0]):
+            size = table.shape[0] // (3 * sem.shape[0])
+            span = pl.ds(i * size, size)
+            table_copies.append(
+                pltpu.make_async_copy(far_table.at[span], table.at[span], sem.at[i // 3, i % 3])
+            )
             table_copies[-1].start()
     else:
         vec, table, far_screened, rho, natural_out, screened = refs[:6]
@@ -207,14 +210,16 @@
 
     def consume(t):
         now = t % 2
-        for table_copy in table_copies[t : t + 1]:
+        first, second, third = 3 * t * block, (3 * t + 1) * block, (3 * t + 3) * block
+        for table_copy in table_copies[3 * t : 3 * t + 1]:
             table_copy.wait()
-        first, second, third = 3 * t * block, (3 * t + 1) * block, (3 * t + 3) * block
-        terms = (
+        terms = [
             dot(evens[now, 0], table[first:second, :quarter]),
             dot(evens[now, 1], table[first:second, quarter:]),
-            dot(odds[now], table[second:third, :]),
-        )
+        ]
+        for table_copy in table_copies[3 * t + 1 : 3 * t + 3]:
+            table_copy.wait()
+        terms.append(dot(odds[now], table[second:third, :]))
         for cols, term in zip((slice(0, quarter), slice(quarter, half), slice(half, waves)), terms):
             if t == 0:
                 acc[:, cols] = term
@@ -443,7 +448,7 @@
                 pltpu.VMEM((2, products, 2 * block), BF16),
                 pltpu.VMEM((products, own_waves), F32),
             ]
-            + [pltpu.SemaphoreType.DMA if slot else pltpu.SemaphoreType.DMA((points // 4 // block,))],
+            + [pltpu.SemaphoreType.DMA if slot else pltpu.SemaphoreType.DMA((points // 4 // block, 3))],
             limit=24 if slot else 36,
             far=1,
         )

time: 84.8 us -> 84.4 us (level)
  no operation moved by 1% of the time
where the time goes in v7:
time: 84.4 us; the launch traced here: 84 us
  Pallas kernels  24.6 us (29%)
  waiting for transfers between devices  22 us (26%)
  blocking collectives  16.2 us (19%)
  starting transfers between devices  12.7 us (15%)
  local copies, waits for them, and re-layouts  6.68 us (8%)
  matrix products  0.85 us (1%)
    pallas_call x7, Pallas kernels, call(): pl.pallas_call(kernel, in_specs=[vmem] * (len(args) - far) + [hbm] * far,...  20.7 us
    all_to_all x1, blocking collectives, exchange(): lax.all_to_all(value, both, 0, 0, tiled=True, axis_index_groups=members)  16.2 us
    all_to_all x1, waiting for transfers between devices, exchange(): lax.all_to_all(value, both, 0, 0, tiled=True, axis_index_groups=members)  14.7 us
    all_to_all x1, starting transfers between devices, exchange(): lax.all_to_all(value, both, 0, 0, tiled=True, axis_index_groups=members)  8.32 us
    ppermute x10, waiting for transfers between devices, shift(): return lax.ppermute(value, 'pw', [(i, i ^ s) for i in range(columns)])  7.25 us
    unnamed x8, local copies, waits for them, and re-layouts  4.54 us
    ppermute x10, starting transfers between devices, shift(): return lax.ppermute(value, 'pw', [(i, i ^ s) for i in range(columns)])  4.41 us
    pallas_call x1, Pallas kernels, local(): pl.pallas_call(functools.partial(gather_kernel, halves=halves), in_specs=...  3.24 us
  transfers between devices with their start and end apart: 11, of which 7 were waited for; matrix products, arithmetic and copies ran while one was open for 3% of the time, Pallas kernels for 24%

profile of v7, /device:TPU:0, one launch (start us, length us, event | category | flops | bytes accessed | tf_op | source)
XLA Modules:
  0.0 84.0 jit_solution(17332701911177358702)
XLA Ops:
  0.0 3.2 %shard_map.64 = bf16[16,2,4,4352]{3,2,1,0:T(4,128)(2,1)} custom-call(s32[2,16]{1,0:T(2,128)} %bitcast.37, bf16[16,4,4096]{2,1,0:T(4,128)(2,1)} %orbitals.1, bf16[16,8,256]{2,1,0:T(8,128)(2,1)} %far_vectors.1), custom_call_target="tpu_custom_call" | custom-call | tf_op jit(solution)/shard_map/pallas_call | solution.py:398
  3.2 8.3 %all-to-all-start = ((bf16[16,2,4,4352]{3,2,1,0:T(4,128)(2,1)}), bf16[16,2,4,4352]{3,2,1,0:T(4,128)(2,1)S(1)}, u32[]{:S(2)}, u32[]{:S(2)}) async-start(bf16[16,2,4,4352]{3,2,1,0:T(4,128)(2,1)} %shard_map.64), calls=%async_computation | async-start | bytes 2228224 | tf_op jit(solution)/shard_map/all_to_all | solution.py:375
  11.6 1.5 %dynamic-slice_bitcast_fusion.seeds = f32[2,192,1024]{2,1,0:T(8,128)S(1)} fusion(f32[2,2,192,1024]{3,2,1,0:T(8,128)} %constant.25.clone, s32[]{:T(128)S(6)} %select_n.12), kind=kLoop, calls=%fused_computation.6 | loop fusion | bytes 3145732 | tf_op jit(solution)/shard_map/jit(dynamic_index_in_dim)/squeeze | solution.py:413
  13.1 0.0 copy-start.3
  13.1 4.9 %shard_map.65.refs_3_ = bf16[12288,512]{1,0:T(8,128)(2,1)S(1)} custom-call(f32[2,192,1024]{2,1,0:T(8,128)S(1)} %dynamic-slice_bitcast_fusion.seeds), custom_call_target="tpu_custom_call" | custom-call | flops 25165824 | bytes 14155776 | tf_op jit(solution)/shard_map/pallas_call | solution.py:382
  18.0 0.0 copy-start
  18.0 4.5 %copy-done = bf16[12288,512]{1,0:T(8,128)(2,1)} copy-done((bf16[12288,512]{1,0:T(8,128)(2,1)}, bf16[12288,512]{1,0:T(8,128)(2,1)S(1)}, u32[]{:S(2)}) %copy-start) | copy-done | bytes 12582936
  22.5 0.0 copy-done.3
  22.5 0.1 fusion.4
  22.6 14.7 %all-to-all-done = bf16[16,2,4,4352]{3,2,1,0:T(4,128)(2,1)S(1)} async-done(((bf16[16,2,4,4352]{3,2,1,0:T(4,128)(2,1)}), bf16[16,2,4,4352]{3,2,1,0:T(4,128)(2,1)S(1)}, u32[]{:S(2)}, u32[]{:S(2)}) %all-to-all-start) | async-done | bytes 1114144 | tf_op jit(solution)/shard_map/all_to_all | solution.py:375
  37.3 0.5 fusion.9
  37.9 0.4 fusion.3.refs_0_
  38.3 0.1 collective-permute-start
  38.4 0.4 fusion.2.refs_0_
  38.8 0.6 collective-permute-start.2
  39.5 0.8 collective-permute-done.refs_1_
  40.3 0.0 copy-start.1
  40.3 6.2 %shard_map.66 = (bf16[256,512]{1,0:T(8,128)(2,1)S(1)}, bf16[288,512]{1,0:T(8,128)(2,1)S(1)}, bf16[12288,512]{1,0:T(8,128)(2,1)S(1)}) custom-call(bf16[2,32,4096]{2,1,0:T(8,128)(2,1)S(1)} %fusion.3.refs_0_, bf16[2,32,4096]{2,1,0:T(8,128)(2,1)S(1)} %collective-permute-done.refs_1_, bf16[64,256]{1,0:T(8,128)(2,1)S(1)} %squeeze.19.refs_2_.refs_0_, ...), custom_call_target="tpu_custom_call" | custom-call | flops 4294967296 | bytes 26804224 | tf_op jit(solution)/shard_map/pallas_call | solution.py:382
  46.5 0.6 collective-permute-start.1
  47.1 0.0 collective-permute-done.2.refs_1_
  47.1 0.0 copy-done.1
  47.1 5.3 %shard_map.67 = (bf16[256,1024]{1,0:T(8,128)(2,1)S(1)}, bf16[64,1024]{1,0:T(8,128)(2,1)S(1)}, bf16[2,512,2048]{2,1,0:T(8,128)(2,1)S(1)}) custom-call(bf16[2,32,4096]{2,1,0:T(8,128)(2,1)S(1)} %fusion.2.refs_0_, bf16[2,32,4096]{2,1,0:T(8,128)(2,1)S(1)} %collective-permute-done.2.refs_1_, bf16[64,256]{1,0:T(8,128)(2,1)S(1)} %squeeze.21.refs_2_, ...), custom_call_target="tpu_custom_call" | custom-call | flops 4294967296 | bytes 22708224 | tf_op jit(solution)/shard_map/pallas_call | solution.py:382
  52.4 1.6 %collective-permute-start.7 = (bf16[64,1024]{1,0:T(8,128)(2,1)S(1)}, bf16[64,1024]{1,0:T(8,128)(2,1)S(1)}, u32[]{:S(2)}, u32[]{:S(2)}) collective-permute-start(bf16[64,1024]{1,0:T(8,128)(2,1)S(1)} %get-tuple-element.40.refs_0_), channel_id=1, source_target_pairs={{0,2},{1,3},{2,0},{3,1},{4,6},{5,7},{6,4},{7,5},{8,10},{9,11},{10,... | collective-permute-start | bytes 393224 | tf_op jit(solution)/shard_map/ppermute | solution.py:378
  54.0 0.8 shard_map.68
  54.8 1.4 %collective-permute-done.1.refs_0_.refs_5_ = bf16[288,512]{1,0:T(8,128)(2,1)S(1)} collective-permute-done((bf16[288,512]{1,0:T(8,128)(2,1)S(1)}, bf16[288,512]{1,0:T(8,128)(2,1)S(1)}, u32[]{:S(2)}, u32[]{:S(2)}) %collective-permute-start.1) | collective-permute-done | bytes 294944 | tf_op jit(solution)/shard_map/ppermute | solution.py:378
  56.1 0.8 shard_map.69
  56.9 0.1 collective-permute-start.3
  57.0 0.5 collective-permute-start.6
  57.5 0.1 collective-permute-start.5
  57.6 0.8 collective-permute-done.7.refs_2_
  58.4 0.0 collective-permute-start.8
  58.4 0.0 collective-permute-done.3
  58.4 0.0 copy-start.2
  58.4 0.9 %collective-permute-start.4 = (bf16[64,1024]{1,0:T(8,128)(2,1)S(1)}, bf16[64,1024]{1,0:T(8,128)(2,1)S(1)}, u32[]{:S(2)}, u32[]{:S(2)}) collective-permute-start(bf16[64,1024]{1,0:T(8,128)(2,1)S(1)} %add_convert_fusion), channel_id=1, source_target_pairs={{0,2},{1,3},{2,0},{3,1},{4,6},{5,7},{6,4},{7,5},{8,10},{9,11},{10,... | collective-permute-start | bytes 393224 | tf_op jit(solution)/shard_map/ppermute | solution.py:378
  59.3 0.0 collective-permute-done.6.refs_1_
  59.3 0.4 collective-permute-done.8.refs_3_
  59.7 2.0 %shard_map.70 = (f32[2,2,16,256]{3,2,1,0:T(8,128)S(1)}, bf16[2,2,16,256]{3,2,1,0:T(8,128)(2,1)S(1)}) custom-call(bf16[64,1024]{1,0:T(8,128)(2,1)S(1)} %get-tuple-element.40.refs_0_, bf16[64,1024]{1,0:T(8,128)(2,1)S(1)} %collective-permute-done.6.refs_1_, bf16[64,1024]{1,0:T(8,128)(2,1)S(1)} %collective-permute-done.7.refs_2_, ...), custom_call_target="tpu_custom_call" | custom-call | bytes 1 | tf_op jit(solution)/shard_map/pallas_call | solution.py:382
  61.8 0.0 collective-permute-done.5.refs_0_
  61.8 2.6 %collective-permute-done.4.q_far = bf16[64,1024]{1,0:T(8,128)(2,1)S(1)} collective-permute-done((bf16[64,1024]{1,0:T(8,128)(2,1)S(1)}, bf16[64,1024]{1,0:T(8,128)(2,1)S(1)}, u32[]{:S(2)}, u32[]{:S(2)}) %collective-permute-start.4) | collective-permute-done | bytes 131104 | tf_op jit(solution)/shard_map/ppermute | solution.py:378
  64.4 0.7 shard_map.71
  65.1 0.1 collective-permute-start.9
  65.2 1.2 %collective-permute-done.9.refs_0_ = bf16[3,2,16,256]{3,2,1,0:T(8,128)(2,1)S(1)} collective-permute-done((bf16[3,2,16,256]{3,2,1,0:T(8,128)(2,1)S(1)}, bf16[3,2,16,256]{3,2,1,0:T(8,128)(2,1)S(1)}, u32[]{:S(2)}, u32[]{:S(2)}) %collective-permute-start.9) | collective-permute-done | bytes 49184 | tf_op jit(solution)/shard_map/ppermute | solution.py:378
  66.4 0.0 copy-done.2
  66.4 0.7 shard_map.72
  67.1 16.2 %all_to_all.10 = bf16[16,2,16,256]{3,2,1,0:T(8,128)(2,1)S(1)} all-to-all(bf16[16,2,16,256]{3,2,1,0:T(8,128)(2,1)S(1)} %shard_map.72), channel_id=1, replica_groups={{0,2,4,6,8,10,12,14,16,18,20,22,24,26,28,30},{1,3,5,7,9,11,13,15,17,19,..., dimensions={0} | all-to-all | bytes 524288 | tf_op jit(solution)/shard_map/all_to_all | solution.py:375
  83.3 0.7 convert_reduce_fusion
  (5 shorter events, 0.1 us)
Async XLA Ops:
  3.2 34.1 %all-to-all-start = ((bf16[16,2,4,4352]{3,2,1,0:T(4,128)(2,1)}), bf16[16,2,4,4352]{3,2,1,0:T(4,128)(2,1)S(1)}, u32[]{:S(2)}, u32[]{:S(2)}) async-start(bf16[16,2,4,4352]{3,2,1,0:T(4,128)(2,1)} %shard_map.64), calls=%async_computation | async-start | bytes 2228224 | tf_op jit(solution)/shard_map/all_to_all | solution.py:375
  13.1 9.4 %copy-start.3 = (s32[32]{0:T(128)S(1)}, s32[32]{0:T(128)}, u32[]{:S(2)}) copy-start(s32[32]{0:T(128)} %param.10) | copy-start | bytes 388
  18.0 4.5 %copy-start = (bf16[12288,512]{1,0:T(8,128)(2,1)}, bf16[12288,512]{1,0:T(8,128)(2,1)S(1)}, u32[]{:S(2)}) copy-start(bf16[12288,512]{1,0:T(8,128)(2,1)S(1)} %shard_map.65.refs_3_) | copy-start | bytes 37748740
  38.3 2.0 %collective-permute-start = (bf16[2,32,4096]{2,1,0:T(8,128)(2,1)S(1)}, bf16[2,32,4096]{2,1,0:T(8,128)(2,1)S(1)}, u32[]{:S(2)}, u32[]{:S(2)}) collective-permute-start(bf16[2,32,4096]{2,1,0:T(8,128)(2,1)S(1)} %fusion.3.refs_0_), channel_id=1, source_target_pairs={{0,1},{1,0},{2,3},{3,2},{4,5},{5,4},{6,7},{7,6},{8,9},{9,8},{10,11... | collective-permute-start | bytes 1572872 | tf_op jit(solution)/shard_map/ppermute | solution.py:378
  38.8 8.3 %collective-permute-start.2 = (bf16[2,32,4096]{2,1,0:T(8,128)(2,1)S(1)}, bf16[2,32,4096]{2,1,0:T(8,128)(2,1)S(1)}, u32[]{:S(2)}, u32[]{:S(2)}) collective-permute-start(bf16[2,32,4096]{2,1,0:T(8,128)(2,1)S(1)} %fusion.2.refs_0_), channel_id=1, source_target_pairs={{0,1},{1,0},{2,3},{3,2},{4,5},{5,4},{6,7},{7,6},{8,9},{9,8},{10,11... | collective-permute-start | bytes 1572872 | tf_op jit(solution)/shard_map/ppermute | solution.py:378
  40.3 6.8 %copy-start.1 = (bf16[2,512,2048]{2,1,0:T(8,128)(2,1)S(1)}, bf16[2,512,2048]{2,1,0:T(8,128)(2,1)}, u32[]{:S(2)}) copy-start(bf16[2,512,2048]{2,1,0:T(8,128)(2,1)} %refs_4_.1) | copy-start | bytes 12582916
  46.5 9.7 %collective-permute-start.1 = (bf16[288,512]{1,0:T(8,128)(2,1)S(1)}, bf16[288,512]{1,0:T(8,128)(2,1)S(1)}, u32[]{:S(2)}, u32[]{:S(2)}) collective-permute-start(bf16[288,512]{1,0:T(8,128)(2,1)S(1)} %get-tuple-element.27), channel_id=1, source_target_pairs={{0,2},{1,3},{2,0},{3,1},{4,6},{5,7},{6,4},{7,5},{8,10},{9,11},{10,... | collective-permute-start | bytes 884744 | tf_op jit(solution)/shard_map/ppermute | solution.py:378
  52.4 6.0 %collective-permute-start.7 = (bf16[64,1024]{1,0:T(8,128)(2,1)S(1)}, bf16[64,1024]{1,0:T(8,128)(2,1)S(1)}, u32[]{:S(2)}, u32[]{:S(2)}) collective-permute-start(bf16[64,1024]{1,0:T(8,128)(2,1)S(1)} %get-tuple-element.40.refs_0_), channel_id=1, source_target_pairs={{0,2},{1,3},{2,0},{3,1},{4,6},{5,7},{6,4},{7,5},{8,10},{9,11},{10,... | collective-permute-start | bytes 393224 | tf_op jit(solution)/shard_map/ppermute | solution.py:378
  56.9 1.5 %collective-permute-start.3 = (bf16[64,1024]{1,0:T(8,128)(2,1)S(1)}, bf16[64,1024]{1,0:T(8,128)(2,1)S(1)}, u32[]{:S(2)}, u32[]{:S(2)}) collective-permute-start(bf16[64,1024]{1,0:T(8,128)(2,1)S(1)} %get-tuple-element.37), channel_id=1, source_target_pairs={{0,1},{1,0},{2,3},{3,2},{4,5},{5,4},{6,7},{7,6},{8,9},{9,8},{10,11... | collective-permute-start | bytes 393224 | tf_op jit(solution)/shard_map/ppermute | solution.py:378
  57.0 2.3 %collective-permute-start.6 = (bf16[64,1024]{1,0:T(8,128)(2,1)S(1)}, bf16[64,1024]{1,0:T(8,128)(2,1)S(1)}, u32[]{:S(2)}, u32[]{:S(2)}) collective-permute-start(bf16[64,1024]{1,0:T(8,128)(2,1)S(1)} %get-tuple-element.40.refs_0_), channel_id=1, source_target_pairs={{0,1},{1,0},{2,3},{3,2},{4,5},{5,4},{6,7},{7,6},{8,9},{9,8},{10,11... | collective-permute-start | bytes 393224 | tf_op jit(solution)/shard_map/ppermute | solution.py:378
  57.5 4.3 %collective-permute-start.5 = (bf16[64,1024]{1,0:T(8,128)(2,1)S(1)}, bf16[64,1024]{1,0:T(8,128)(2,1)S(1)}, u32[]{:S(2)}, u32[]{:S(2)}) collective-permute-start(bf16[64,1024]{1,0:T(8,128)(2,1)S(1)} %get-tuple-element.38), channel_id=1, source_target_pairs={{0,1},{1,0},{2,3},{3,2},{4,5},{5,4},{6,7},{7,6},{8,9},{9,8},{10,11... | collective-permute-start | bytes 393224 | tf_op jit(solution)/shard_map/ppermute | solution.py:378
  58.4 1.3 %collective-permute-start.8 = (bf16[64,1024]{1,0:T(8,128)(2,1)S(1)}, bf16[64,1024]{1,0:T(8,128)(2,1)S(1)}, u32[]{:S(2)}, u32[]{:S(2)}) collective-permute-start(bf16[64,1024]{1,0:T(8,128)(2,1)S(1)} %collective-permute-done.7.refs_2_), channel_id=1, source_target_pairs={{0,1},{1,0},{2,3},{3,2},{4,5},{5,4},{6,7},{7,6},{8,9},{9,8},{10,11... | collective-permute-start | bytes 393224 | tf_op jit(solution)/shard_map/ppermute | solution.py:378
  58.4 8.0 %copy-start.2 = (s32[16,2]{0,1:T(2,128)S(1)}, s32[16,2]{0,1:T(2,128)}, u32[]{:S(2)}) copy-start(s32[16,2]{0,1:T(2,128)} %param.9) | copy-start | bytes 388
  58.4 6.0 %collective-permute-start.4 = (bf16[64,1024]{1,0:T(8,128)(2,1)S(1)}, bf16[64,1024]{1,0:T(8,128)(2,1)S(1)}, u32[]{:S(2)}, u32[]{:S(2)}) collective-permute-start(bf16[64,1024]{1,0:T(8,128)(2,1)S(1)} %add_convert_fusion), channel_id=1, source_target_pairs={{0,2},{1,3},{2,0},{3,1},{4,6},{5,7},{6,4},{7,5},{8,10},{9,11},{10,... | collective-permute-start | bytes 393224 | tf_op jit(solution)/shard_map/ppermute | solution.py:378
  65.1 1.3 %collective-permute-start.9 = (bf16[3,2,16,256]{3,2,1,0:T(8,128)(2,1)S(1)}, bf16[3,2,16,256]{3,2,1,0:T(8,128)(2,1)S(1)}, u32[]{:S(2)}, u32[]{:S(2)}) collective-permute-start(bf16[3,2,16,256]{3,2,1,0:T(8,128)(2,1)S(1)} %get-tuple-element.44), channel_id=1, source_target_pairs={{0,1},{1,0},{2,3},{3,2},{4,5},{5,4},{6,7},{7,6},{8,9},{9,8},{10,11... | collective-permute-start | bytes 147464 | tf_op jit(solution)/shard_map/ppermute | solution.py:378
